TPU v7x, 32 devices: a whole 2x2x4 slice. The times are simulated.
32 devices in a mesh: groups: 2 (over x), space: 16 (over z, y, core).
Axes of the slice: x: 2, y: 2, z: 4, core: 2. Of those that a mesh axis runs over, the one named last changes fastest.
Arguments:
- eigvecs: bfloat16 [4, 2, 3, 16, 128, 256], P('groups', None, None, 'space'), parts along dimension 0, may hold values from -12 to 12
- links: bfloat16 [4, 3, 2, 3, 3, 16, 128], P('groups', None, None, None, None, 'space'), parts along dimension 0, may hold values from -4 to 4
- directions: int32 [4], P('groups'), parts along dimension 0, may hold values from 0 to 2
- pairs: int32 [128, 2], P(('groups', 'space')), parts along dimension 0, may hold values from 0 to 1
- perambulators: bfloat16 [128, 2, 256, 256], P(('groups', 'space')), parts along dimension 0, may hold values from -0.25 to 0.25
Outputs:
- elementals: float32 [4, 2, 2, 256, 256], P('groups', None, None, 'space'), parts along dimension 0
- pair_matrices: bfloat16 [128, 2, 256, 256], P(('groups', 'space')), parts along dimension 0
There are 2 independent parts, one for each index of `groups`. A program takes and returns all parts, laid end to end along the dimension named above; each array names one. Nothing has to cross between parts.
Inputs may be any that keep to these rules, and one draw needn't show every extreme that they name: `directions`: 0 is x, 1 is y, 2 is z. pairs[p, 0] is the source time slice and pairs[p, 1] the sink time slice of pair p.
All inputs are finite; a program needn't handle non-finite values.
Results may differ from a plain program's by a relative error of at most 0.011.
Values may be sent and summed in bfloat16 or wider, within the bound.
No kernel may reach another device: no remote copies, remote signals or barrier semaphores. Data moves between devices by JAX's collectives and lax.ppermute only.
A program may use at most 64 MiB of HBM per device.

v0:
```python
import functools

import jax
import jax.numpy as jnp
from jax import lax
from jax.experimental import pallas as pl
from jax.experimental.pallas import tpu as pltpu
from jax.sharding import PartitionSpec as P

LX = 16
LY = 8
SITES = LX * LY
COLORS = 3
FIELD = COLORS * SITES
LINK_ROWS = 54
PACKED_LINKS = 32
SMEAR = 0.12
VMEM = 56 * 1024 * 1024

bf16 = jnp.bfloat16
f32 = jnp.float32


def position():
    index = lax.axis_index("space")
    return lax.rem(index, 2), lax.rem(lax.div(index, 2), 2)


def whole_in_vmem():
    return pl.BlockSpec(memory_space=pltpu.VMEM)


def link_row(direction, part, row, column):
    return ((direction * 2 + part) * COLORS + row) * COLORS + column


def split_kernel(vectors, links, keep, send):
    core, _ = position()
    half = vectors.shape[5] // 2
    for t in range(vectors.shape[0]):
        for part in range(2):
            for color in range(COLORS):
                rows = pl.ds(color * SITES, SITES)
                lanes = pl.ds(part * half, half)
                block = vectors[t, part, color, 0]
                low, high = block[:, :half], block[:, half:]
                keep[t, rows, lanes] = jnp.where(core == 0, low, high)
                send[t, rows, lanes] = jnp.where(core == 0, high, low)
        gathered = [
            links[t, d, part, row, column].astype(f32)
            for d in range(3)
            for part in range(2)
            for row in range(COLORS)
            for column in range(COLORS)
        ]
        gathered.append(jnp.zeros((2 * PACKED_LINKS - LINK_ROWS, SITES), f32))
        packed = jnp.concatenate(gathered, axis=0).astype(bf16)
        for out in (keep, send):
            out[t, pl.ds(FIELD, PACKED_LINKS), pl.ds(0, SITES)] = packed[:PACKED_LINKS]
            out[t, pl.ds(FIELD, PACKED_LINKS), pl.ds(SITES, SITES)] = packed[PACKED_LINKS:]


def join_kernel(keep, received, own, other):
    core, chip = position()
    own[core] = keep[chip]
    own[1 - core] = received[chip]
    other[core] = keep[1 - chip]
    other[1 - core] = received[1 - chip]


def shift_y(row, lane):
    return jnp.where(
        lax.rem(lane, LY) == 0,
        pltpu.roll(row, SITES - (LY - 1), 1),
        pltpu.roll(row, 1, 1),
    )


def site_masks():
    row = lax.broadcasted_iota(jnp.int32, (SITES, SITES), 0)
    column = lax.broadcasted_iota(jnp.int32, (SITES, SITES), 1)
    y = lax.rem(row, LY)
    ahead_x = column == lax.rem(row + LY, SITES)
    behind_x = column == lax.rem(row + SITES - LY, SITES)
    ahead_y = column == row - y + lax.rem(y + 1, LY)
    behind_y = column == row - y + lax.rem(y + LY - 1, LY)
    return ahead_x, ahead_y, behind_x, behind_y, column == row


def link_planes(packed):
    return jnp.concatenate([packed[:, :SITES], packed[:, SITES:]], axis=0).astype(f32)


def smear_kernel(own, across, first, second, last, w_out, fields, rims, grown, operator, sems):
    _, chip = position()
    own_at, across_at = 2 + 2 * chip, 4 - 2 * chip
    first_at, second_at = 6 * chip, 6 - 6 * chip
    copies = []
    for k, (ref, at) in enumerate(
        ((own, own_at), (across, across_at), (first, first_at), (second, second_at))
    ):
        copies.append(
            pltpu.make_async_copy(
                ref.at[:, pl.ds(0, FIELD)], fields.at[pl.ds(at, 2)], sems.at[2 * k]
            )
        )
        copies.append(
            pltpu.make_async_copy(
                ref.at[:, pl.ds(FIELD, PACKED_LINKS)], rims.at[pl.ds(at, 2)], sems.at[2 * k + 1]
            )
        )
    copies.append(pltpu.make_async_copy(last.at[pl.ds(0, FIELD)], fields.at[8], sems.at[8]))
    copies.append(
        pltpu.make_async_copy(last.at[pl.ds(FIELD, PACKED_LINKS)], rims.at[8], sems.at[9])
    )
    for copy in copies:
        copy.start()
    for copy in copies:
        copy.wait()

    ahead_x, ahead_y, behind_x, behind_y, same = site_masks()

    def build(z, carry):
        table = link_planes(rims[z])
        below = link_planes(rims[z - 1])
        lane = lax.broadcasted_iota(jnp.int32, table.shape, 1)
        from_x = pltpu.roll(table, LY, 1)
        from_y = shift_y(table, lane)

        def row_of(values, *what):
            k = link_row(*what)
            return values[k : k + 1]

        for part in range(2):
            sign = 1.0 if part == 0 else -1.0
            for i in range(COLORS):
                rows = pl.ds((part * COLORS + i) * SITES, SITES)
                for j in range(COLORS):
                    zero = jnp.zeros((SITES, SITES), f32)
                    plane = jnp.where(ahead_x, row_of(from_x, 0, part, i, j), zero)
                    plane = jnp.where(ahead_y, row_of(from_y, 1, part, i, j), plane)
                    plane = jnp.where(behind_x, sign * row_of(table, 0, part, j, i), plane)
                    plane = jnp.where(behind_y, sign * row_of(table, 1, part, j, i), plane)
                    lower = jnp.where(same, sign * row_of(below, 2, part, j, i), zero)
                    upper = jnp.where(same, row_of(table, 2, part, i, j), zero)
                    for k, block in enumerate((lower, plane, upper)):
                        operator[z - 1, rows, pl.ds((k * COLORS + j) * SITES, SITES)] = (
                            block.astype(bf16)
                        )
        return carry

    lax.fori_loop(1, 8, build, 0)
    half = SITES

    def step(source, z, z_operator):
        window = source[pl.ds(z - 1, 3)].reshape(3 * FIELD, 2 * half)
        product = jnp.dot(operator[z_operator], window, preferred_element_type=f32)
        hops = jnp.concatenate(
            [
                product[:FIELD, :half] - product[FIELD:, half:],
                product[:FIELD, half:] + product[FIELD:, :half],
            ],
            axis=1,
        )
        center = source[z].astype(f32)
        return ((1.0 - 6.0 * SMEAR) * center + SMEAR * hops).astype(bf16)

    def smear_first(z, carry):
        grown[z - 1] = step(fields, z, z - 1)
        return carry

    def smear_second(z, carry):
        w_out[z - 1] = step(grown, z, z)
        return carry

    lax.fori_loop(1, 8, smear_first, 0)
    lax.fori_loop(1, 6, smear_second, 0)


def elemental_kernel(scale, directions, mine, theirs, own, across, out, out_low, w, rims, right, sems):
    core, chip = position()
    half = SITES
    planes = mine.shape[0]
    copies = []
    for k, (ref, side) in enumerate(((mine, core), (theirs, 1 - core))):
        for part in range(2):
            copies.append(
                pltpu.make_async_copy(
                    ref.at[:, :, pl.ds(part * half, half)],
                    w.at[:, part, :, pl.ds(pl.multiple_of(side * half, half), half)],
                    sems.at[2 * k + part],
                )
            )
    copies.append(
        pltpu.make_async_copy(
            own.at[:, pl.ds(FIELD, PACKED_LINKS)], rims.at[pl.ds(2 * chip, 2)], sems.at[4]
        )
    )
    copies.append(
        pltpu.make_async_copy(
            across.at[:, pl.ds(FIELD, PACKED_LINKS)], rims.at[pl.ds(2 - 2 * chip, 2)], sems.at[5]
        )
    )
    for copy in copies:
        copy.start()
    for copy in copies:
        copy.wait()
    direction = directions[core]
    ahead_x, ahead_y, _, _, same = site_masks()
    one = jnp.ones((SITES, SITES), f32)
    zero = jnp.zeros((SITES, SITES), f32)
    is_x, is_y, is_z = direction == 0, direction == 1, direction == 2
    mask_x = jnp.where(ahead_x, one, zero)
    mask_y = jnp.where(ahead_y, one, zero)
    mask_z = jnp.where(same, one, zero)
    mask = jnp.where(is_x, mask_x, jnp.where(is_y, mask_y, mask_z))

    def displace(z, carry):
        table = link_planes(rims[z])
        lane = lax.broadcasted_iota(jnp.int32, table.shape, 1)
        count = 2 * COLORS * COLORS
        along_x = pltpu.roll(table, LY, 1)[:count]
        along_y = shift_y(table, lane)[count : 2 * count]
        along_z = table[2 * count : 3 * count]
        chosen = jnp.where(is_x, along_x, jnp.where(is_y, along_y, along_z))
        operator = jnp.concatenate(
            [
                jnp.concatenate(
                    [
                        (mask * chosen[k : k + 1]).astype(bf16)
                        for k in range((part * COLORS + i) * COLORS, (part * COLORS + i + 1) * COLORS)
                    ],
                    axis=1,
                )
                for part in range(2)
                for i in range(COLORS)
            ],
            axis=0,
        )
        source = z + jnp.where(is_z, 1, 0)
        real = jnp.dot(operator, w[source, 0], preferred_element_type=f32)
        imag = jnp.dot(operator, w[source, 1], preferred_element_type=f32)
        hop_real = real[:FIELD] - imag[FIELD:]
        hop_imag = real[FIELD:] + imag[:FIELD]
        total = (hop_real + hop_imag).astype(bf16)
        rest = (hop_imag - hop_real).astype(bf16)
        vectors = 2 * half
        right[z, 0, :, pl.ds(0, vectors)] = total
        right[z, 0, :, pl.ds(vectors, vectors)] = rest
        right[z, 1, :, pl.ds(0, vectors)] = rest
        right[z, 1, :, pl.ds(vectors, vectors)] = -total
        return carry

    lax.fori_loop(0, planes - 1, displace, 0)
    vectors = 2 * half
    depth = (planes - 1) * 2 * FIELD
    product = lax.dot_general(
        w[pl.ds(0, planes - 1)].reshape(depth, vectors),
        right[...].reshape(depth, 2 * vectors),
        (((0,), (0,)), ((), ())),
        preferred_element_type=f32,
    )
    packed = (product[:, :vectors] + product[:, vectors:].T) * scale
    out[...] = packed
    out_low[...] = packed.astype(bf16)


def pair_kernel(pair_scale, pairs, s00, s10, s01, s11, perambulators, elementals, out, parts, left, right):
    core, chip = position()
    index = lax.axis_index("space")
    size = s00.shape[0]
    rows = elementals.shape[3]
    own_rows = pl.ds(pl.multiple_of(index * rows, 8), rows)
    for ref, t, k in (
        (s00, chip, core),
        (s10, 1 - chip, core),
        (s01, chip, 1 - core),
        (s11, 1 - chip, 1 - core),
    ):
        packed = ref[...].astype(f32)
        turned = packed.T
        parts[t, k, 0] = 0.5 * (packed - turned)
        parts[t, k, 1] = 0.5 * (packed + turned)
    for t in range(2):
        for k in range(2):
            for part in range(2):
                elementals[t, k, part] = parts[t, k, part, own_rows]
        real, imag = parts[t, 0, 0].astype(bf16), parts[t, 0, 1].astype(bf16)
        left[t, :size, :size] = real
        left[t, :size, size:] = -imag
        left[t, size:, :size] = imag
        left[t, size:, size:] = real
        real, imag = parts[t, 1, 0].astype(bf16), parts[t, 1, 1].astype(bf16)
        right[t, :size, :size] = real
        right[t, :size, size:] = imag
        right[t, size:, :size] = -imag
        right[t, size:, size:] = real

    def contract(p, carry):
        source, sink = pairs[p, 0], pairs[p, 1]
        propagator = perambulators[p].reshape(2 * size, size)
        first = jnp.dot(left[sink], propagator, preferred_element_type=f32).astype(bf16)
        wide = jnp.concatenate([first[:size], first[size:]], axis=1)
        second = (
            jnp.dot(wide, right[source], preferred_element_type=f32) * pair_scale
        ).astype(bf16)
        real, imag = second[:, :size], second[:, size:]
        both = jnp.concatenate(
            [second, jnp.concatenate([imag, -real], axis=1)], axis=0
        )
        turned = jnp.concatenate([propagator[:size], propagator[size:]], axis=1)
        third = lax.dot_general(
            both, turned, (((1,), (1,)), ((), ())), preferred_element_type=f32
        ).astype(bf16)
        out[p] = third.reshape(2, size, size)
        return carry

    lax.fori_loop(0, perambulators.shape[0], contract, 0)


def params():
    return pltpu.CompilerParams(vmem_limit_bytes=VMEM)


def body(eigvecs, links, directions, pairs, perambulators):
    slices = eigvecs.shape[0]
    vector_count = eigvecs.shape[5]
    n = lax.axis_size("space")
    blocks = n // 4
    vmem = whole_in_vmem()
    anywhere = pl.BlockSpec(memory_space=pl.ANY)
    smem = pl.BlockSpec(memory_space=pltpu.SMEM)
    rows = FIELD + PACKED_LINKS

    def swap(value, bit):
        return lax.ppermute(value, "space", [(i, i ^ bit) for i in range(n)])

    package = jax.ShapeDtypeStruct((slices, rows, vector_count), bf16)
    keep, send = pl.pallas_call(
        split_kernel,
        out_shape=(package, package),
        in_specs=[vmem, vmem],
        out_specs=(vmem, vmem),
        compiler_params=params(),
    )(eigvecs, links)
    received = swap(send, 1)
    own, other = pl.pallas_call(
        join_kernel,
        out_shape=(package, package),
        in_specs=[vmem, vmem],
        out_specs=(vmem, vmem),
        compiler_params=params(),
    )(keep, received)

    crossing, straight, down = [], [], []
    for q in range(blocks):
        above, below = (q + 1) % blocks, (q + blocks - 1) % blocks
        for core in range(2):
            a, b = 4 * q + core, 4 * q + 2 + core
            crossing += [(b, 4 * above + core), (a, 4 * below + 2 + core)]
            straight += [(b, 4 * above + 2 + core), (a, 4 * below + core)]
            down += [(a, 4 * below + core), (b, 4 * below + 2 + core)]
    across = swap(other, 2)
    second = lax.ppermute(own, "space", straight)
    first = lax.ppermute(other, "space", crossing)
    _, chip = position()
    third_plane = jnp.where(chip == 0, across[0], own[0])
    last = lax.ppermute(third_plane, "space", down)

    w_shape = jax.ShapeDtypeStruct((5, FIELD, vector_count), bf16)
    mine = pl.pallas_call(
        smear_kernel,
        out_shape=w_shape,
        in_specs=[anywhere] * 5,
        out_specs=vmem,
        scratch_shapes=[
            pltpu.VMEM((9, FIELD, vector_count), bf16),
            pltpu.VMEM((9, PACKED_LINKS, 2 * SITES), bf16),
            pltpu.VMEM((7, FIELD, vector_count), bf16),
            pltpu.VMEM((7, 2 * FIELD, 3 * FIELD), bf16),
            pltpu.SemaphoreType.DMA((10,)),
        ],
        compiler_params=params(),
    )(own, across, first, second, last)
    theirs = swap(mine, 1)
    site_scale = (6.0 * n * SITES) ** (-0.5)
    square = (vector_count, vector_count)
    partial, partial_low = pl.pallas_call(
        functools.partial(elemental_kernel, site_scale),
        out_shape=(jax.ShapeDtypeStruct(square, f32), jax.ShapeDtypeStruct(square, bf16)),
        in_specs=[smem] + [anywhere] * 4,
        out_specs=(vmem, vmem),
        scratch_shapes=[
            pltpu.VMEM((5, 2, FIELD, vector_count), bf16),
            pltpu.VMEM((4, PACKED_LINKS, 2 * SITES), bf16),
            pltpu.VMEM((4, 2, FIELD, 2 * vector_count), bf16),
            pltpu.SemaphoreType.DMA((6,)),
        ],
        compiler_params=params(),
    )(directions, mine, theirs, own, across)

    bit = 4
    while bit < n:
        partial = partial + swap(partial_low, bit).astype(f32)
        partial_low = partial.astype(bf16)
        bit *= 2
    other_slice = swap(partial_low, 2)
    other_copy = swap(partial_low, 1)
    other_both = swap(other_slice, 1)

    pair_scale = (2.0 * vector_count) ** (-0.5)
    owned_rows = vector_count // n
    big = 2 * vector_count
    return pl.pallas_call(
        functools.partial(pair_kernel, pair_scale),
        out_shape=(
            jax.ShapeDtypeStruct((slices, 2, 2, owned_rows, vector_count), f32),
            jax.ShapeDtypeStruct(perambulators.shape, bf16),
        ),
        in_specs=[smem] + [vmem] * 5,
        out_specs=(vmem, vmem),
        scratch_shapes=[
            pltpu.VMEM((slices, 2, 2, vector_count, vector_count), f32),
            pltpu.VMEM((slices, big, big), bf16),
            pltpu.VMEM((slices, big, big), bf16),
        ],
        compiler_params=params(),
    )(pairs, partial_low, other_slice, other_copy, other_both, perambulators)


def solution(mesh):
    placed = (
        P("groups", None, None, "space", None, None),
        P("groups", None, None, None, None, "space", None),
        P("groups"),
        P(("groups", "space"), None),
        P(("groups", "space"), None, None, None),
    )
    return jax.shard_map(
        body,
        mesh=mesh,
        in_specs=placed,
        out_specs=(
            P("groups", None, None, "space", None),
            P(("groups", "space"), None, None, None),
        ),
        check_vma=False,
    )
```

profile of v0, /device:TPU:0, one launch (start us, length us, event | category | flops | bytes accessed | tf_op | source)
XLA Modules:
  0.0 95.6 jit_solution(6493287636821073765)
XLA Ops:
  0.6 1.4 %copy.7.links = bf16[2,3,2,3,3,1,128]{6,5,4,3,2,1,0:T(2,128)(2,1)} copy(bf16[2,3,2,3,3,1,128]{6,2,5,4,3,1,0:T(2,128)(2,1)} %param.6) | data formatting | bytes 55296 | tf_op args[1]
  2.0 2.2 %shard_map.68 = (bf16[2,416,256]{2,1,0:T(8,128)(2,1)}, bf16[2,416,256]{2,1,0:T(8,128)(2,1)}) custom-call(bf16[2,2,3,1,128,256]{5,4,3,2,1,0:T(8,128)(2,1)} %vectors.1, bf16[2,3,2,3,3,1,128]{6,5,4,3,2,1,0:T(2,128)(2,1)} %copy.7.links), custom_call_target="tpu_custom_call" | custom-call | tf_op jit(solution)/shard_map/pallas_call | solution.py:339
  4.2 0.5 collective-permute-start
  4.7 1.6 %collective-permute-done.received = bf16[2,416,256]{2,1,0:T(8,128)(2,1)S(1)} collective-permute-done((bf16[2,416,256]{2,1,0:T(8,128)(2,1)}, bf16[2,416,256]{2,1,0:T(8,128)(2,1)S(1)}, u32[]{:S(2)}, u32[]{:S(2)}) %collective-permute-start) | collective-permute-done | bytes 426016 | tf_op jit(solution)/shard_map/ppermute | solution.py:336
  6.3 0.0 copy-start.6
  6.3 0.8 copy-done.6
  7.0 2.1 %shard_map.69 = (bf16[2,416,256]{2,1,0:T(8,128)(2,1)}, bf16[2,416,256]{2,1,0:T(8,128)(2,1)}) custom-call(bf16[2,416,256]{2,1,0:T(8,128)(2,1)} %get-tuple-element.8.keep, bf16[2,416,256]{2,1,0:T(8,128)(2,1)} %copy-done.6), custom_call_target="tpu_custom_call" | custom-call | tf_op jit(solution)/shard_map/pallas_call | solution.py:347
  9.1 2.9 %collective-permute-start.1 = (bf16[2,416,256]{2,1,0:T(8,128)(2,1)}, bf16[2,416,256]{2,1,0:T(8,128)(2,1)S(1)}, u32[]{:S(2)}, u32[]{:S(2)}) collective-permute-start(bf16[2,416,256]{2,1,0:T(8,128)(2,1)} %get-tuple-element.11), channel_id=1, source_target_pairs={{0,2},{1,3},{2,0},{3,1},{4,6},{5,7},{6,4},{7,5},{8,10},{9,11},{10,... | collective-permute-start | bytes 1277960 | tf_op jit(solution)/shard_map/ppermute | solution.py:336
  12.0 3.5 %collective-permute-start.2 = (bf16[2,416,256]{2,1,0:T(8,128)(2,1)}, bf16[2,416,256]{2,1,0:T(8,128)(2,1)S(1)}, u32[]{:S(2)}, u32[]{:S(2)}) collective-permute-start(bf16[2,416,256]{2,1,0:T(8,128)(2,1)} %get-tuple-element.11), channel_id=1, source_target_pairs={{2,4},{0,14},{3,5},{1,15},{6,8},{4,2},{7,9},{5,3},{10,12},{8,6},{1... | collective-permute-start | bytes 1277960 | tf_op jit(solution)/shard_map/ppermute | solution.py:365
  15.6 0.4 collective-permute-start.3
  16.0 15.5 %collective-permute-done.1.across = bf16[2,416,256]{2,1,0:T(8,128)(2,1)S(1)} collective-permute-done((bf16[2,416,256]{2,1,0:T(8,128)(2,1)}, bf16[2,416,256]{2,1,0:T(8,128)(2,1)S(1)}, u32[]{:S(2)}, u32[]{:S(2)}) %collective-permute-start.1) | collective-permute-done | bytes 426016 | tf_op jit(solution)/shard_map/ppermute | solution.py:336
  31.5 1.1 %fusion = bf16[416,256]{1,0:T(8,128)(2,1)S(1)} fusion(bf16[2,416,256]{2,1,0:T(8,128)(2,1)S(1)} %collective-permute-done.1.across, bf16[2,416,256]{2,1,0:T(8,128)(2,1)} %get-tuple-element.10.own, pred[]{:T(512)S(6)} %eq.3), kind=kLoop, calls=%fused_computation.3 | loop fusion | flops 106496 | bytes 638977 | tf_op jit(solution)/shard_map/jit(_where)/select_n | solution.py:367
  32.6 3.9 %collective-permute-start.4 = (bf16[416,256]{1,0:T(8,128)(2,1)S(1)}, bf16[416,256]{1,0:T(8,128)(2,1)S(1)}, u32[]{:S(2)}, u32[]{:S(2)}) collective-permute-start(bf16[416,256]{1,0:T(8,128)(2,1)S(1)} %fusion), channel_id=1, source_target_pairs={{0,12},{2,14},{1,13},{3,15},{4,0},{6,2},{5,1},{7,3},{8,4},{10,6},{... | collective-permute-start | bytes 638984 | tf_op jit(solution)/shard_map/ppermute | solution.py:368
  36.5 0.0 collective-permute-done.3.second
  36.5 0.0 collective-permute-done.2.first
  36.5 0.0 copy-start.4
  36.5 4.0 %collective-permute-done.4.last = bf16[416,256]{1,0:T(8,128)(2,1)S(1)} collective-permute-done((bf16[416,256]{1,0:T(8,128)(2,1)S(1)}, bf16[416,256]{1,0:T(8,128)(2,1)S(1)}, u32[]{:S(2)}, u32[]{:S(2)}) %collective-permute-start.4) | collective-permute-done | bytes 213024 | tf_op jit(solution)/shard_map/ppermute | solution.py:368
  40.5 0.0 copy-done
  40.5 0.0 copy-done.5
  40.5 0.0 copy-done.4
  40.5 0.7 copy-done.7
  41.2 14.4 %shard_map.70.mine = bf16[5,384,256]{2,1,0:T(8,128)(2,1)} custom-call(bf16[2,416,256]{2,1,0:T(8,128)(2,1)} %get-tuple-element.10.own, bf16[2,416,256]{2,1,0:T(8,128)(2,1)} %copy-done, bf16[2,416,256]{2,1,0:T(8,128)(2,1)} %copy-done.4, bf16[2,416,256]{2,1,0:T(8,128)(2,1)} %copy-done.5, bf16[416,256]{1,0:T(8,128)(2,1)} %copy-done.7), custom_call_target="tpu_custom_call" | custom-call | tf_op jit(solution)/shard_map/pallas_call | solution.py:371
  55.6 0.1 collective-permute-start.5
  55.7 2.8 %collective-permute-done.5.theirs = bf16[5,384,256]{2,1,0:T(8,128)(2,1)S(1)} collective-permute-done((bf16[5,384,256]{2,1,0:T(8,128)(2,1)}, bf16[5,384,256]{2,1,0:T(8,128)(2,1)S(1)}, u32[]{:S(2)}, u32[]{:S(2)}) %collective-permute-start.5) | collective-permute-done | bytes 983072 | tf_op jit(solution)/shard_map/ppermute | solution.py:336
  58.4 1.0 %copy-done.2 = bf16[5,384,256]{2,1,0:T(8,128)(2,1)} copy-done((bf16[5,384,256]{2,1,0:T(8,128)(2,1)}, bf16[5,384,256]{2,1,0:T(8,128)(2,1)S(1)}, u32[]{:S(2)}) %copy-start.2) | copy-done | bytes 983064
  59.4 6.6 %shard_map.71 = (f32[256,256]{1,0:T(8,128)}, bf16[256,256]{1,0:T(8,128)(2,1)}) custom-call(s32[2]{0:T(128)} %directions.1, bf16[5,384,256]{2,1,0:T(8,128)(2,1)} %shard_map.70.mine, bf16[5,384,256]{2,1,0:T(8,128)(2,1)} %copy-done.2, bf16[2,416,256]{2,1,0:T(8,128)(2,1)} %get-tuple-element.10.own, bf16[2,416,256]{2,1,0:T(8,128)(2,1)} %copy-done), custom_call_target="tpu_custom_call" | custom-call | tf_op jit(solution)/shard_map/pallas_call | solution.py:388
  66.0 0.5 collective-permute-start.6
  66.5 5.3 %collective-permute-done.6 = bf16[256,256]{1,0:T(8,128)(2,1)S(1)} collective-permute-done((bf16[256,256]{1,0:T(8,128)(2,1)}, bf16[256,256]{1,0:T(8,128)(2,1)S(1)}, u32[]{:S(2)}, u32[]{:S(2)}) %collective-permute-start.6) | collective-permute-done | bytes 131104 | tf_op jit(solution)/shard_map/ppermute | solution.py:336
  71.8 1.1 %fusion.1 = bf16[256,256]{1,0:T(8,128)(2,1)S(1)} fusion(f32[256,256]{1,0:T(8,128)} %get-tuple-element.12, bf16[256,256]{1,0:T(8,128)(2,1)S(1)} %collective-permute-done.6), kind=kLoop, calls=%fused_computation.4 | loop fusion | flops 196608 | bytes 524288 | tf_op jit(solution)/shard_map/convert_element_type | solution.py:405
  72.9 0.0 copy-start.11
  72.9 3.2 %collective-permute-start.7 = (bf16[256,256]{1,0:T(8,128)(2,1)S(1)}, bf16[256,256]{1,0:T(8,128)(2,1)S(1)}, u32[]{:S(2)}, u32[]{:S(2)}) collective-permute-start(bf16[256,256]{1,0:T(8,128)(2,1)S(1)} %fusion.1), channel_id=1, source_target_pairs={{0,8},{1,9},{2,10},{3,11},{4,12},{5,13},{6,14},{7,15},{8,0},{9,1},... | collective-permute-start | bytes 393224 | tf_op jit(solution)/shard_map/ppermute | solution.py:336
  76.1 6.1 %collective-permute-done.7 = bf16[256,256]{1,0:T(8,128)(2,1)S(1)} collective-permute-done((bf16[256,256]{1,0:T(8,128)(2,1)S(1)}, bf16[256,256]{1,0:T(8,128)(2,1)S(1)}, u32[]{:S(2)}, u32[]{:S(2)}) %collective-permute-start.7) | collective-permute-done | bytes 131104 | tf_op jit(solution)/shard_map/ppermute | solution.py:336
  82.2 0.0 copy-done.1
  82.2 0.0 copy-start.3
  82.2 1.6 %collective-permute-start.8 = (bf16[256,256]{1,0:T(8,128)(2,1)S(1)}, bf16[256,256]{1,0:T(8,128)(2,1)S(1)}, u32[]{:S(2)}, u32[]{:S(2)}) collective-permute-start(bf16[256,256]{1,0:T(8,128)(2,1)S(1)} %add_convert_fusion.s00), channel_id=1, source_target_pairs={{0,2},{1,3},{2,0},{3,1},{4,6},{5,7},{6,4},{7,5},{8,10},{9,11},{10,... | collective-permute-start | bytes 393224 | tf_op jit(solution)/shard_map/ppermute | solution.py:336
  83.8 0.0 collective-permute-start.9
  83.8 3.4 %collective-permute-done.8.s10 = bf16[256,256]{1,0:T(8,128)(2,1)S(1)} collective-permute-done((bf16[256,256]{1,0:T(8,128)(2,1)S(1)}, bf16[256,256]{1,0:T(8,128)(2,1)S(1)}, u32[]{:S(2)}, u32[]{:S(2)}) %collective-permute-start.8) | collective-permute-done | bytes 131104 | tf_op jit(solution)/shard_map/ppermute | solution.py:336
  87.3 0.0 collective-permute-start.10
  87.3 0.0 copy-done.11
  87.3 0.7 copy.8.pairs
  87.9 0.0 collective-permute-done.9.s01
  87.9 0.7 collective-permute-done.10.s11
  88.6 0.0 copy-done.3
  88.6 0.0 copy-done.8
  88.6 0.0 copy-done.9
  88.6 0.0 copy-start.10
  88.6 0.6 copy-done.10
  89.3 6.4 %shard_map.72 = (f32[2,2,2,16,256]{4,3,2,1,0:T(8,128)}, bf16[4,2,256,256]{3,2,1,0:T(8,128)(2,1)}) custom-call(s32[4,2]{1,0:T(4,128)} %copy.8.pairs, bf16[256,256]{1,0:T(8,128)(2,1)} %copy-done.3, bf16[256,256]{1,0:T(8,128)(2,1)} %copy-done.8, bf16[256,256]{1,0:T(8,128)(2,1)} %copy-done.9, bf16[256,256]{1,0:T(8,128)(2,1)} %copy-done.10, ...), custom_call_target="tpu_custom_call" | custom-call | tf_op jit(solution)/shard_map/pallas_call | solution.py:414
  (8 shorter events, 0.1 us)
Async XLA Ops:
  4.2 2.1 %collective-permute-start = (bf16[2,416,256]{2,1,0:T(8,128)(2,1)}, bf16[2,416,256]{2,1,0:T(8,128)(2,1)S(1)}, u32[]{:S(2)}, u32[]{:S(2)}) collective-permute-start(bf16[2,416,256]{2,1,0:T(8,128)(2,1)} %get-tuple-element.9), channel_id=1, source_target_pairs={{0,1},{1,0},{2,3},{3,2},{4,5},{5,4},{6,7},{7,6},{8,9},{9,8},{10,11... | collective-permute-start | bytes 1277960 | tf_op jit(solution)/shard_map/ppermute | solution.py:336
  6.3 0.8 copy-start.6
  9.1 22.3 %collective-permute-start.1 = (bf16[2,416,256]{2,1,0:T(8,128)(2,1)}, bf16[2,416,256]{2,1,0:T(8,128)(2,1)S(1)}, u32[]{:S(2)}, u32[]{:S(2)}) collective-permute-start(bf16[2,416,256]{2,1,0:T(8,128)(2,1)} %get-tuple-element.11), channel_id=1, source_target_pairs={{0,2},{1,3},{2,0},{3,1},{4,6},{5,7},{6,4},{7,5},{8,10},{9,11},{10,... | collective-permute-start | bytes 1277960 | tf_op jit(solution)/shard_map/ppermute | solution.py:336
  12.0 24.5 %collective-permute-start.2 = (bf16[2,416,256]{2,1,0:T(8,128)(2,1)}, bf16[2,416,256]{2,1,0:T(8,128)(2,1)S(1)}, u32[]{:S(2)}, u32[]{:S(2)}) collective-permute-start(bf16[2,416,256]{2,1,0:T(8,128)(2,1)} %get-tuple-element.11), channel_id=1, source_target_pairs={{2,4},{0,14},{3,5},{1,15},{6,8},{4,2},{7,9},{5,3},{10,12},{8,6},{1... | collective-permute-start | bytes 1277960 | tf_op jit(solution)/shard_map/ppermute | solution.py:365
  15.6 20.9 %collective-permute-start.3 = (bf16[2,416,256]{2,1,0:T(8,128)(2,1)}, bf16[2,416,256]{2,1,0:T(8,128)(2,1)S(1)}, u32[]{:S(2)}, u32[]{:S(2)}) collective-permute-start(bf16[2,416,256]{2,1,0:T(8,128)(2,1)} %get-tuple-element.10.own), channel_id=1, source_target_pairs={{2,6},{0,12},{3,7},{1,13},{6,10},{4,0},{7,11},{5,1},{10,14},{8,4},... | collective-permute-start | bytes 1277960 | tf_op jit(solution)/shard_map/ppermute | solution.py:364
  31.5 9.0 %copy-start = (bf16[2,416,256]{2,1,0:T(8,128)(2,1)}, bf16[2,416,256]{2,1,0:T(8,128)(2,1)S(1)}, u32[]{:S(2)}) copy-start(bf16[2,416,256]{2,1,0:T(8,128)(2,1)S(1)} %collective-permute-done.1.across) | copy-start | bytes 1277956
  32.6 7.9 %collective-permute-start.4 = (bf16[416,256]{1,0:T(8,128)(2,1)S(1)}, bf16[416,256]{1,0:T(8,128)(2,1)S(1)}, u32[]{:S(2)}, u32[]{:S(2)}) collective-permute-start(bf16[416,256]{1,0:T(8,128)(2,1)S(1)} %fusion), channel_id=1, source_target_pairs={{0,12},{2,14},{1,13},{3,15},{4,0},{6,2},{5,1},{7,3},{8,4},{10,6},{... | collective-permute-start | bytes 638984 | tf_op jit(solution)/shard_map/ppermute | solution.py:368
  36.5 4.0 %copy-start.5 = (bf16[2,416,256]{2,1,0:T(8,128)(2,1)}, bf16[2,416,256]{2,1,0:T(8,128)(2,1)S(1)}, u32[]{:S(2)}) copy-start(bf16[2,416,256]{2,1,0:T(8,128)(2,1)S(1)} %collective-permute-done.3.second) | copy-start | bytes 1277956
  36.5 4.0 %copy-start.4 = (bf16[2,416,256]{2,1,0:T(8,128)(2,1)}, bf16[2,416,256]{2,1,0:T(8,128)(2,1)S(1)}, u32[]{:S(2)}) copy-start(bf16[2,416,256]{2,1,0:T(8,128)(2,1)S(1)} %collective-permute-done.2.first) | copy-start | bytes 1277956
  40.5 0.7 copy-start.7
  55.6 2.8 %collective-permute-start.5 = (bf16[5,384,256]{2,1,0:T(8,128)(2,1)}, bf16[5,384,256]{2,1,0:T(8,128)(2,1)S(1)}, u32[]{:S(2)}, u32[]{:S(2)}) collective-permute-start(bf16[5,384,256]{2,1,0:T(8,128)(2,1)} %shard_map.70.mine), channel_id=1, source_target_pairs={{0,1},{1,0},{2,3},{3,2},{4,5},{5,4},{6,7},{7,6},{8,9},{9,8},{10,11... | collective-permute-start | bytes 2949128 | tf_op jit(solution)/shard_map/ppermute | solution.py:336
  58.4 1.0 %copy-start.2 = (bf16[5,384,256]{2,1,0:T(8,128)(2,1)}, bf16[5,384,256]{2,1,0:T(8,128)(2,1)S(1)}, u32[]{:S(2)}) copy-start(bf16[5,384,256]{2,1,0:T(8,128)(2,1)S(1)} %collective-permute-done.5.theirs) | copy-start | bytes 2949124
  66.0 5.8 %collective-permute-start.6 = (bf16[256,256]{1,0:T(8,128)(2,1)}, bf16[256,256]{1,0:T(8,128)(2,1)S(1)}, u32[]{:S(2)}, u32[]{:S(2)}) collective-permute-start(bf16[256,256]{1,0:T(8,128)(2,1)} %get-tuple-element.13), channel_id=1, source_target_pairs={{0,4},{1,5},{2,6},{3,7},{4,0},{5,1},{6,2},{7,3},{8,12},{9,13},{10,... | collective-permute-start | bytes 393224 | tf_op jit(solution)/shard_map/ppermute | solution.py:336
  71.8 10.3 %copy-start.1 = (f32[256,256]{1,0:T(8,128)S(1)}, f32[256,256]{1,0:T(8,128)}, u32[]{:S(2)}) copy-start(f32[256,256]{1,0:T(8,128)} %get-tuple-element.12) | copy-start | bytes 786436
  72.9 14.4 %copy-start.11 = (s32[4,2]{0,1:T(2,128)S(1)}, s32[4,2]{0,1:T(2,128)}, u32[]{:S(2)}) copy-start(s32[4,2]{0,1:T(2,128)} %param.8) | copy-start | bytes 100
  72.9 9.3 %collective-permute-start.7 = (bf16[256,256]{1,0:T(8,128)(2,1)S(1)}, bf16[256,256]{1,0:T(8,128)(2,1)S(1)}, u32[]{:S(2)}, u32[]{:S(2)}) collective-permute-start(bf16[256,256]{1,0:T(8,128)(2,1)S(1)} %fusion.1), channel_id=1, source_target_pairs={{0,8},{1,9},{2,10},{3,11},{4,12},{5,13},{6,14},{7,15},{8,0},{9,1},... | collective-permute-start | bytes 393224 | tf_op jit(solution)/shard_map/ppermute | solution.py:336
  82.2 6.4 %copy-start.3 = (bf16[256,256]{1,0:T(8,128)(2,1)}, bf16[256,256]{1,0:T(8,128)(2,1)S(1)}, u32[]{:S(2)}) copy-start(bf16[256,256]{1,0:T(8,128)(2,1)S(1)} %add_convert_fusion.s00) | copy-start | bytes 393220
  82.2 5.0 %collective-permute-start.8 = (bf16[256,256]{1,0:T(8,128)(2,1)S(1)}, bf16[256,256]{1,0:T(8,128)(2,1)S(1)}, u32[]{:S(2)}, u32[]{:S(2)}) collective-permute-start(bf16[256,256]{1,0:T(8,128)(2,1)S(1)} %add_convert_fusion.s00), channel_id=1, source_target_pairs={{0,2},{1,3},{2,0},{3,1},{4,6},{5,7},{6,4},{7,5},{8,10},{9,11},{10,... | collective-permute-start | bytes 393224 | tf_op jit(solution)/shard_map/ppermute | solution.py:336
  83.8 4.1 %collective-permute-start.9 = (bf16[256,256]{1,0:T(8,128)(2,1)S(1)}, bf16[256,256]{1,0:T(8,128)(2,1)S(1)}, u32[]{:S(2)}, u32[]{:S(2)}) collective-permute-start(bf16[256,256]{1,0:T(8,128)(2,1)S(1)} %add_convert_fusion.s00), channel_id=1, source_target_pairs={{0,1},{1,0},{2,3},{3,2},{4,5},{5,4},{6,7},{7,6},{8,9},{9,8},{10,11... | collective-permute-start | bytes 393224 | tf_op jit(solution)/shard_map/ppermute | solution.py:336
  87.3 1.4 %copy-start.8 = (bf16[256,256]{1,0:T(8,128)(2,1)}, bf16[256,256]{1,0:T(8,128)(2,1)S(1)}, u32[]{:S(2)}) copy-start(bf16[256,256]{1,0:T(8,128)(2,1)S(1)} %collective-permute-done.8.s10) | copy-start | bytes 393220
  87.3 1.3 %collective-permute-start.10 = (bf16[256,256]{1,0:T(8,128)(2,1)S(1)}, bf16[256,256]{1,0:T(8,128)(2,1)S(1)}, u32[]{:S(2)}, u32[]{:S(2)}) collective-permute-start(bf16[256,256]{1,0:T(8,128)(2,1)S(1)} %collective-permute-done.8.s10), channel_id=1, source_target_pairs={{0,1},{1,0},{2,3},{3,2},{4,5},{5,4},{6,7},{7,6},{8,9},{9,8},{10,11... | collective-permute-start | bytes 393224 | tf_op jit(solution)/shard_map/ppermute | solution.py:336
  87.9 0.7 copy-start.9
  88.6 0.7 copy-start.10
where the time goes:
time: 96 us; the launch traced here: 95.6 us
  waiting for transfers between devices  39.3 us (41%)
  Pallas kernels  31.7 us (33%)
  starting transfers between devices  16.6 us (17%)
  local copies, waits for them, and re-layouts  5.13 us (5%)
  other arithmetic  2.21 us (2%)
    ppermute x8, waiting for transfers between devices, swap(): return lax.ppermute(value, 'space', [(i, i ^ bit) for i in range(n)])  35.3 us
    pallas_call x1, Pallas kernels, body(): pl.pallas_call(smear_kernel, out_shape=w_shape, in_specs=[anywhere] * 5,...  14.4 us
    ppermute x8, starting transfers between devices, swap(): return lax.ppermute(value, 'space', [(i, i ^ bit) for i in range(n)])  8.7 us
    pallas_call x1, Pallas kernels, body(): pl.pallas_call(functools.partial(elemental_kernel, site_scale), out_shape...  6.61 us
    pallas_call x1, Pallas kernels, body(): pl.pallas_call(functools.partial(pair_kernel, pair_scale), out_shape=(jax...  6.35 us
    unnamed x26, local copies, waits for them, and re-layouts  5.13 us
    ppermute x1, waiting for transfers between devices, body(): last = lax.ppermute(third_plane, 'space', down)  3.96 us
    ppermute x1, starting transfers between devices, body(): last = lax.ppermute(third_plane, 'space', down)  3.88 us
  transfers between devices with their start and end apart: 11, of which 8 were waited for; matrix products, arithmetic and copies ran while one was open for 2% of the time, Pallas kernels for 0%

commit v1 on v0

--- a/solution.py
+++ b/solution.py
@@ -15,7 +15,6 @@
 LINK_ROWS = 54
 PACKED_LINKS = 32
 SMEAR = 0.12
-VMEM = 56 * 1024 * 1024
 
 bf16 = jnp.bfloat16
 f32 = jnp.float32
@@ -31,41 +30,64 @@
 
 
 def link_row(direction, part, row, column):
-    return ((direction * 2 + part) * COLORS + row) * COLORS + column
-
-
-def split_kernel(vectors, links, keep, send):
-    core, _ = position()
+    return ((direction * COLORS + row) * COLORS + column) * 2 + part
+
+
+def split_kernel(vectors, links, own, other, send, packed, sems):
+    core, chip = position()
     half = vectors.shape[5] // 2
-    for t in range(vectors.shape[0]):
+    copies = []
+    for t in range(2):
         for part in range(2):
             for color in range(COLORS):
                 rows = pl.ds(color * SITES, SITES)
                 lanes = pl.ds(part * half, half)
-                block = vectors[t, part, color, 0]
-                low, high = block[:, :half], block[:, half:]
-                keep[t, rows, lanes] = jnp.where(core == 0, low, high)
-                send[t, rows, lanes] = jnp.where(core == 0, high, low)
+                near = pl.ds(pl.multiple_of(core * half, half), half)
+                far = pl.ds(pl.multiple_of((1 - core) * half, half), half)
+                block = vectors.at[chip + t * (1 - 2 * chip), part, color, 0]
+                kept = (own, other)[t]
+                for source, target in (
+                    (block.at[:, near], kept.at[core, rows, lanes]),
+                    (block.at[:, far], send.at[t, rows, lanes]),
+                ):
+                    copies.append(pltpu.make_async_copy(source, target, sems.at[len(copies)]))
+                    copies[-1].start()
+    for t in range(2):
+        table = links.at[chip + t * (1 - 2 * chip)]
         gathered = [
-            links[t, d, part, row, column].astype(f32)
+            table[d, row, column, 0].astype(f32)
             for d in range(3)
-            for part in range(2)
             for row in range(COLORS)
             for column in range(COLORS)
         ]
         gathered.append(jnp.zeros((2 * PACKED_LINKS - LINK_ROWS, SITES), f32))
-        packed = jnp.concatenate(gathered, axis=0).astype(bf16)
-        for out in (keep, send):
-            out[t, pl.ds(FIELD, PACKED_LINKS), pl.ds(0, SITES)] = packed[:PACKED_LINKS]
-            out[t, pl.ds(FIELD, PACKED_LINKS), pl.ds(SITES, SITES)] = packed[PACKED_LINKS:]
-
-
-def join_kernel(keep, received, own, other):
+        rows = jnp.concatenate(gathered, axis=0).astype(bf16)
+        packed[t, :, pl.ds(0, SITES)] = rows[:PACKED_LINKS]
+        packed[t, :, pl.ds(SITES, SITES)] = rows[PACKED_LINKS:]
+        for target in ((own, other)[t].at[core], send.at[t]):
+            copies.append(
+                pltpu.make_async_copy(
+                    packed.at[t], target.at[pl.ds(FIELD, PACKED_LINKS)], sems.at[len(copies)]
+                )
+            )
+            copies[-1].start()
+    for copy in copies:
+        copy.wait()
+
+
+def join_kernel(received, own_in, other_in, own, other, edge, sems):
     core, chip = position()
-    own[core] = keep[chip]
-    own[1 - core] = received[chip]
-    other[core] = keep[1 - chip]
-    other[1 - core] = received[1 - chip]
+    copies = [
+        pltpu.make_async_copy(received.at[t], kept.at[1 - core], sems.at[t])
+        for t, kept in enumerate((own, other))
+    ]
+    for copy in copies:
+        copy.start()
+    for copy in copies:
+        copy.wait()
+    copy = pltpu.make_async_copy(own.at[1 - chip], edge, sems.at[2])
+    copy.start()
+    copy.wait()
 
 
 def shift_y(row, lane):
@@ -91,10 +113,10 @@
     return jnp.concatenate([packed[:, :SITES], packed[:, SITES:]], axis=0).astype(f32)
 
 
-def smear_kernel(own, across, first, second, last, w_out, fields, rims, grown, operator, sems):
+def smear_kernel(own, across, first, second, last, w_out, rims_out, fields, rims, grown, operator, sems):
     _, chip = position()
-    own_at, across_at = 2 + 2 * chip, 4 - 2 * chip
-    first_at, second_at = 6 * chip, 6 - 6 * chip
+    own_at, across_at = 3 + chip, 5 - 3 * chip
+    first_at, second_at, last_at = 1 + 5 * chip, 7 - 7 * chip, 8 * chip
     copies = []
     for k, (ref, at) in enumerate(
         ((own, own_at), (across, across_at), (first, first_at), (second, second_at))
@@ -109,15 +131,16 @@
                 ref.at[:, pl.ds(FIELD, PACKED_LINKS)], rims.at[pl.ds(at, 2)], sems.at[2 * k + 1]
             )
         )
-    copies.append(pltpu.make_async_copy(last.at[pl.ds(0, FIELD)], fields.at[8], sems.at[8]))
+    copies.append(pltpu.make_async_copy(last.at[pl.ds(0, FIELD)], fields.at[last_at], sems.at[8]))
     copies.append(
-        pltpu.make_async_copy(last.at[pl.ds(FIELD, PACKED_LINKS)], rims.at[8], sems.at[9])
+        pltpu.make_async_copy(last.at[pl.ds(FIELD, PACKED_LINKS)], rims.at[last_at], sems.at[9])
     )
     for copy in copies:
         copy.start()
     for copy in copies:
         copy.wait()
 
+    rims_out[...] = rims[2:6]
     ahead_x, ahead_y, behind_x, behind_y, same = site_masks()
 
     def build(z, carry):
@@ -177,8 +200,8 @@
     lax.fori_loop(1, 6, smear_second, 0)
 
 
-def elemental_kernel(scale, directions, mine, theirs, own, across, out, out_low, w, rims, right, sems):
-    core, chip = position()
+def elemental_kernel(scale, directions, mine, theirs, rims, out, out_low, w, right, sems):
+    core, _ = position()
     half = SITES
     planes = mine.shape[0]
     copies = []
@@ -191,16 +214,6 @@
                     sems.at[2 * k + part],
                 )
             )
-    copies.append(
-        pltpu.make_async_copy(
-            own.at[:, pl.ds(FIELD, PACKED_LINKS)], rims.at[pl.ds(2 * chip, 2)], sems.at[4]
-        )
-    )
-    copies.append(
-        pltpu.make_async_copy(
-            across.at[:, pl.ds(FIELD, PACKED_LINKS)], rims.at[pl.ds(2 - 2 * chip, 2)], sems.at[5]
-        )
-    )
     for copy in copies:
         copy.start()
     for copy in copies:
@@ -228,7 +241,7 @@
                 jnp.concatenate(
                     [
                         (mask * chosen[k : k + 1]).astype(bf16)
-                        for k in range((part * COLORS + i) * COLORS, (part * COLORS + i + 1) * COLORS)
+                        for k in range(2 * COLORS * i + part, 2 * COLORS * (i + 1), 2)
                     ],
                     axis=1,
                 )
@@ -297,7 +310,7 @@
         right[t, size:, size:] = real
 
     def contract(p, carry):
-        source, sink = pairs[p, 0], pairs[p, 1]
+        source, sink = pairs[0, p], pairs[1, p]
         propagator = perambulators[p].reshape(2 * size, size)
         first = jnp.dot(left[sink], propagator, preferred_element_type=f32).astype(bf16)
         wide = jnp.concatenate([first[:size], first[size:]], axis=1)
@@ -318,8 +331,8 @@
     lax.fori_loop(0, perambulators.shape[0], contract, 0)
 
 
-def params():
-    return pltpu.CompilerParams(vmem_limit_bytes=VMEM)
+def params(megabytes):
+    return pltpu.CompilerParams(vmem_limit_bytes=megabytes * 1024 * 1024)
 
 
 def body(eigvecs, links, directions, pairs, perambulators):
@@ -335,44 +348,49 @@
     def swap(value, bit):
         return lax.ppermute(value, "space", [(i, i ^ bit) for i in range(n)])
 
-    package = jax.ShapeDtypeStruct((slices, rows, vector_count), bf16)
-    keep, send = pl.pallas_call(
+    package = jax.ShapeDtypeStruct((2, rows, vector_count), bf16)
+    own, other, send = pl.pallas_call(
         split_kernel,
-        out_shape=(package, package),
-        in_specs=[vmem, vmem],
-        out_specs=(vmem, vmem),
-        compiler_params=params(),
-    )(eigvecs, links)
+        out_shape=(package, package, package),
+        in_specs=[anywhere, vmem],
+        out_specs=(anywhere, anywhere, anywhere),
+        scratch_shapes=[
+            pltpu.VMEM((2, PACKED_LINKS, 2 * SITES), bf16),
+            pltpu.SemaphoreType.DMA((28,)),
+        ],
+        compiler_params=params(8),
+    )(eigvecs, jnp.transpose(links, (0, 1, 3, 4, 5, 2, 6)))
     received = swap(send, 1)
-    own, other = pl.pallas_call(
+    own, other, edge = pl.pallas_call(
         join_kernel,
-        out_shape=(package, package),
-        in_specs=[vmem, vmem],
-        out_specs=(vmem, vmem),
-        compiler_params=params(),
-    )(keep, received)
-
-    crossing, straight, down = [], [], []
+        out_shape=(package, package, jax.ShapeDtypeStruct((rows, vector_count), bf16)),
+        in_specs=[anywhere] * 3,
+        out_specs=(anywhere, anywhere, anywhere),
+        scratch_shapes=[pltpu.SemaphoreType.DMA((3,))],
+        input_output_aliases={1: 0, 2: 1},
+        compiler_params=params(8),
+    )(received, own, other)
+
+    crossing, straight, outer = [], [], []
     for q in range(blocks):
         above, below = (q + 1) % blocks, (q + blocks - 1) % blocks
         for core in range(2):
             a, b = 4 * q + core, 4 * q + 2 + core
             crossing += [(b, 4 * above + core), (a, 4 * below + 2 + core)]
             straight += [(b, 4 * above + 2 + core), (a, 4 * below + core)]
-            down += [(a, 4 * below + core), (b, 4 * below + 2 + core)]
+            outer += [(a, 4 * above + core), (b, 4 * below + 2 + core)]
     across = swap(other, 2)
     second = lax.ppermute(own, "space", straight)
     first = lax.ppermute(other, "space", crossing)
-    _, chip = position()
-    third_plane = jnp.where(chip == 0, across[0], own[0])
-    last = lax.ppermute(third_plane, "space", down)
+    last = lax.ppermute(edge, "space", outer)
 
     w_shape = jax.ShapeDtypeStruct((5, FIELD, vector_count), bf16)
-    mine = pl.pallas_call(
+    rims_shape = jax.ShapeDtypeStruct((4, PACKED_LINKS, 2 * SITES), bf16)
+    mine, rims = pl.pallas_call(
         smear_kernel,
-        out_shape=w_shape,
+        out_shape=(w_shape, rims_shape),
         in_specs=[anywhere] * 5,
-        out_specs=vmem,
+        out_specs=(vmem, vmem),
         scratch_shapes=[
             pltpu.VMEM((9, FIELD, vector_count), bf16),
             pltpu.VMEM((9, PACKED_LINKS, 2 * SITES), bf16),
@@ -380,7 +398,7 @@
             pltpu.VMEM((7, 2 * FIELD, 3 * FIELD), bf16),
             pltpu.SemaphoreType.DMA((10,)),
         ],
-        compiler_params=params(),
+        compiler_params=params(24),
     )(own, across, first, second, last)
     theirs = swap(mine, 1)
     site_scale = (6.0 * n * SITES) ** (-0.5)
@@ -388,16 +406,15 @@
     partial, partial_low = pl.pallas_call(
         functools.partial(elemental_kernel, site_scale),
         out_shape=(jax.ShapeDtypeStruct(square, f32), jax.ShapeDtypeStruct(square, bf16)),
-        in_specs=[smem] + [anywhere] * 4,
+        in_specs=[smem, anywhere, anywhere, vmem],
         out_specs=(vmem, vmem),
         scratch_shapes=[
             pltpu.VMEM((5, 2, FIELD, vector_count), bf16),
-            pltpu.VMEM((4, PACKED_LINKS, 2 * SITES), bf16),
             pltpu.VMEM((4, 2, FIELD, 2 * vector_count), bf16),
-            pltpu.SemaphoreType.DMA((6,)),
+            pltpu.SemaphoreType.DMA((4,)),
         ],
-        compiler_params=params(),
-    )(directions, mine, theirs, own, across)
+        compiler_params=params(16),
+    )(directions, mine, theirs, rims)
 
     bit = 4
     while bit < n:
@@ -424,8 +441,8 @@
             pltpu.VMEM((slices, big, big), bf16),
             pltpu.VMEM((slices, big, big), bf16),
         ],
-        compiler_params=params(),
-    )(pairs, partial_low, other_slice, other_copy, other_both, perambulators)
+        compiler_params=params(16),
+    )(pairs.T, partial_low, other_slice, other_copy, other_both, perambulators)
 
 
 def solution(mesh):

time: 96 us -> 81.2 us (0.85)
  Pallas kernels: 31.7 us -> 24.2 us
  starting transfers between devices: 16.6 us -> 12.7 us
  local copies, waits for them, and re-layouts: 5.13 us -> 1.89 us
  other arithmetic: 2.21 us -> 0.07 us
  waiting for transfers between devices: 39.3 us -> 41.4 us
    ppermute x1, waiting for transfers between devices: 3.96 us -> 22.6 us  [body(): last = lax.ppermute(edge, 'space', outer)]
    ppermute x8, waiting for transfers between devices: 35.3 us -> 18.9 us  [swap(): return lax.ppermute(value, 'space', [(i, i ^ bit) for i in range(n)])]
    ppermute x1, starting transfers between devices: 0.45 us -> 5.03 us  [body(): second = lax.ppermute(own, 'space', straight)]
    pallas_call x3, Pallas kernels: 18.7 us -> 14.2 us  [the longest x1 12.8 us: body(): pl.pallas_call(smear_kernel, out_shape=(w_shape, rims_shape), in_specs=[a...]
    ppermute x1, starting transfers between devices: 3.88 us -> 0.28 us  [body(): last = lax.ppermute(edge, 'space', outer)]
    unnamed x26 -> x10, local copies, waits for them, and re-layouts: 5.13 us -> 1.89 us
    ppermute x8, starting transfers between devices: 8.7 us -> 6.17 us  [swap(): return lax.ppermute(value, 'space', [(i, i ^ bit) for i in range(n)])]
    ppermute x1, starting transfers between devices: 3.54 us -> 1.18 us  [body(): first = lax.ppermute(other, 'space', crossing)]
  transfers between devices with their start and end apart: 11 -> 11, of which waited for: 8 -> 7; matrix products, arithmetic and copies ran while one was open for 2% -> 0% of each run, Pallas kernels for 0% -> 0%
where the time goes in v1:
time: 81.2 us; the launch traced here: 81 us
  waiting for transfers between devices  41.4 us (51%)
  Pallas kernels  24.2 us (30%)
  starting transfers between devices  12.7 us (16%)
  local copies, waits for them, and re-layouts  1.89 us (2%)
    ppermute x1, waiting for transfers between devices, body(): last = lax.ppermute(edge, 'space', outer)  22.6 us
    ppermute x8, waiting for transfers between devices, swap(): return lax.ppermute(value, 'space', [(i, i ^ bit) for i in range(n)])  18.9 us
    pallas_call x1, Pallas kernels, body(): pl.pallas_call(smear_kernel, out_shape=(w_shape, rims_shape), in_specs=[a...  12.8 us
    ppermute x8, starting transfers between devices, swap(): return lax.ppermute(value, 'space', [(i, i ^ bit) for i in range(n)])  6.17 us
    pallas_call x1, Pallas kernels, body(): pl.pallas_call(functools.partial(pair_kernel, pair_scale), out_shape=(jax...  5.41 us
    ppermute x1, starting transfers between devices, body(): second = lax.ppermute(own, 'space', straight)  5.03 us
    pallas_call x1, Pallas kernels, body(): pl.pallas_call(functools.partial(elemental_kernel, site_scale), out_shape...  4.59 us
    unnamed x10, local copies, waits for them, and re-layouts  1.89 us
  transfers between devices with their start and end apart: 11, of which 7 were waited for; matrix products, arithmetic and copies ran while one was open for 0% of the time, Pallas kernels for 0%

profile of v1, /device:TPU:0, one launch (start us, length us, event | category | flops | bytes accessed | tf_op | source)
XLA Modules:
  0.0 81.0 jit_solution(10144984608394153068)
XLA Ops:
  0.6 0.0 copy-start.1
  0.6 1.1 %copy-done.1 = bf16[2,2,3,1,128,256]{5,4,3,2,1,0:T(8,128)(2,1)S(1)} copy-done((bf16[2,2,3,1,128,256]{5,4,3,2,1,0:T(8,128)(2,1)S(1)}, bf16[2,2,3,1,128,256]{5,4,3,2,1,0:T(8,128)(2,1)}, u32[]{:S(2)}) %copy-start.1) | copy-done | bytes 786456
  1.8 0.0 copy-start.2
  1.8 0.7 copy-done.2
  2.5 0.6 shard_map.68
  3.1 0.5 collective-permute-start
  3.6 1.4 %collective-permute-done.received = bf16[2,416,256]{2,1,0:T(8,128)(2,1)S(1)} collective-permute-done((bf16[2,416,256]{2,1,0:T(8,128)(2,1)S(1)}, bf16[2,416,256]{2,1,0:T(8,128)(2,1)S(1)}, u32[]{:S(2)}, u32[]{:S(2)}) %collective-permute-start) | collective-permute-done | bytes 426016 | tf_op jit(solution)/shard_map/ppermute | solution.py:349
  5.0 0.8 %shard_map.69 = (bf16[2,416,256]{2,1,0:T(8,128)(2,1)S(1)}, bf16[2,416,256]{2,1,0:T(8,128)(2,1)S(1)}, bf16[416,256]{1,0:T(8,128)(2,1)S(1)}) custom-call(bf16[2,416,256]{2,1,0:T(8,128)(2,1)S(1)} %collective-permute-done.received, bf16[2,416,256]{2,1,0:T(8,128)(2,1)S(1)} %get-tuple-element.13.own_in, ...), custom_call_target="tpu_custom_call", output_to_operand_aliasing={{0}: (1, {}), {1}: (2, {})} | custom-call | tf_op jit(solution)/shard_map/pallas_call | solution.py:364
  5.8 5.0 %collective-permute-start.3 = (bf16[2,416,256]{2,1,0:T(8,128)(2,1)S(1)}, bf16[2,416,256]{2,1,0:T(8,128)(2,1)S(1)}, u32[]{:S(2)}, u32[]{:S(2)}) collective-permute-start(bf16[2,416,256]{2,1,0:T(8,128)(2,1)S(1)} %get-tuple-element.15.own), channel_id=1, source_target_pairs={{2,6},{0,12},{3,7},{1,13},{6,10},{4,0},{7,11},{5,1},{10,14},{8,4},... | collective-permute-start | bytes 1277960 | tf_op jit(solution)/shard_map/ppermute | solution.py:383
  10.9 1.2 %collective-permute-start.2 = (bf16[2,416,256]{2,1,0:T(8,128)(2,1)S(1)}, bf16[2,416,256]{2,1,0:T(8,128)(2,1)S(1)}, u32[]{:S(2)}, u32[]{:S(2)}) collective-permute-start(bf16[2,416,256]{2,1,0:T(8,128)(2,1)S(1)} %get-tuple-element.16), channel_id=1, source_target_pairs={{2,4},{0,14},{3,5},{1,15},{6,8},{4,2},{7,9},{5,3},{10,12},{8,6},{1... | collective-permute-start | bytes 1277960 | tf_op jit(solution)/shard_map/ppermute | solution.py:384
  12.0 0.0 collective-permute-start.1
  12.0 0.3 collective-permute-start.4
  12.3 22.6 %collective-permute-done.4.last = bf16[416,256]{1,0:T(8,128)(2,1)S(1)} collective-permute-done((bf16[416,256]{1,0:T(8,128)(2,1)S(1)}, bf16[416,256]{1,0:T(8,128)(2,1)S(1)}, u32[]{:S(2)}, u32[]{:S(2)}) %collective-permute-start.4) | collective-permute-done | bytes 213024 | tf_op jit(solution)/shard_map/ppermute | solution.py:385
  34.9 0.0 collective-permute-done.3.second
  34.9 0.0 collective-permute-done.2.first
  34.9 0.0 collective-permute-done.1.across
  34.9 12.8 %shard_map.70 = (bf16[5,384,256]{2,1,0:T(8,128)(2,1)S(1)}, bf16[4,32,256]{2,1,0:T(8,128)(2,1)S(1)}) custom-call(bf16[2,416,256]{2,1,0:T(8,128)(2,1)S(1)} %get-tuple-element.15.own, bf16[2,416,256]{2,1,0:T(8,128)(2,1)S(1)} %collective-permute-done.1.across, bf16[2,416,256]{2,1,0:T(8,128)(2,1)S(1)} %collective-permute-done.2.first, ...), custom_call_target="tpu_custom_call" | custom-call | tf_op jit(solution)/shard_map/pallas_call | solution.py:389
  47.7 0.0 copy-start.4
  47.7 0.1 collective-permute-start.5
  47.8 2.6 %collective-permute-done.5.theirs = bf16[5,384,256]{2,1,0:T(8,128)(2,1)S(1)} collective-permute-done((bf16[5,384,256]{2,1,0:T(8,128)(2,1)S(1)}, bf16[5,384,256]{2,1,0:T(8,128)(2,1)S(1)}, u32[]{:S(2)}, u32[]{:S(2)}) %collective-permute-start.5) | collective-permute-done | bytes 983072 | tf_op jit(solution)/shard_map/ppermute | solution.py:349
  50.4 0.0 copy-done.4
  50.4 4.6 %shard_map.71 = (f32[256,256]{1,0:T(8,128)S(1)}, bf16[256,256]{1,0:T(8,128)(2,1)S(1)}) custom-call(s32[2]{0:T(128)S(1)} %copy-done.4, bf16[5,384,256]{2,1,0:T(8,128)(2,1)S(1)} %get-tuple-element.18.mine, bf16[5,384,256]{2,1,0:T(8,128)(2,1)S(1)} %collective-permute-done.5.theirs, bf16[4,32,256]{2,1,0:T(8,128)(2,1)S(1)} %get-tuple-element.19.rims), custom_call_target="tpu_custom_call" | custom-call | tf_op jit(solution)/shard_map/pallas_call | solution.py:406
  55.0 0.0 copy-start
  55.0 1.7 %collective-permute-start.6 = (bf16[256,256]{1,0:T(8,128)(2,1)S(1)}, bf16[256,256]{1,0:T(8,128)(2,1)S(1)}, u32[]{:S(2)}, u32[]{:S(2)}) collective-permute-start(bf16[256,256]{1,0:T(8,128)(2,1)S(1)} %get-tuple-element.21), channel_id=1, source_target_pairs={{0,4},{1,5},{2,6},{3,7},{4,0},{5,1},{6,2},{7,3},{8,12},{9,13},{10,... | collective-permute-start | bytes 393224 | tf_op jit(solution)/shard_map/ppermute | solution.py:349
  56.7 3.9 %collective-permute-done.6 = bf16[256,256]{1,0:T(8,128)(2,1)S(1)} collective-permute-done((bf16[256,256]{1,0:T(8,128)(2,1)S(1)}, bf16[256,256]{1,0:T(8,128)(2,1)S(1)}, u32[]{:S(2)}, u32[]{:S(2)}) %collective-permute-start.6) | collective-permute-done | bytes 131104 | tf_op jit(solution)/shard_map/ppermute | solution.py:349
  60.6 2.5 %collective-permute-start.7 = (bf16[256,256]{1,0:T(8,128)(2,1)S(1)}, bf16[256,256]{1,0:T(8,128)(2,1)S(1)}, u32[]{:S(2)}, u32[]{:S(2)}) collective-permute-start(bf16[256,256]{1,0:T(8,128)(2,1)S(1)} %fusion), channel_id=1, source_target_pairs={{0,8},{1,9},{2,10},{3,11},{4,12},{5,13},{6,14},{7,15},{8,0},{9,1},... | collective-permute-start | bytes 393224 | tf_op jit(solution)/shard_map/ppermute | solution.py:349
  63.1 6.0 %collective-permute-done.7 = bf16[256,256]{1,0:T(8,128)(2,1)S(1)} collective-permute-done((bf16[256,256]{1,0:T(8,128)(2,1)S(1)}, bf16[256,256]{1,0:T(8,128)(2,1)S(1)}, u32[]{:S(2)}, u32[]{:S(2)}) %collective-permute-start.7) | collective-permute-done | bytes 131104 | tf_op jit(solution)/shard_map/ppermute | solution.py:349
  69.2 0.0 copy-start.3
  69.2 1.3 %collective-permute-start.8 = (bf16[256,256]{1,0:T(8,128)(2,1)S(1)}, bf16[256,256]{1,0:T(8,128)(2,1)S(1)}, u32[]{:S(2)}, u32[]{:S(2)}) collective-permute-start(bf16[256,256]{1,0:T(8,128)(2,1)S(1)} %add_convert_fusion.s00), channel_id=1, source_target_pairs={{0,2},{1,3},{2,0},{3,1},{4,6},{5,7},{6,4},{7,5},{8,10},{9,11},{10,... | collective-permute-start | bytes 393224 | tf_op jit(solution)/shard_map/ppermute | solution.py:349
  70.5 0.0 collective-permute-start.9
  70.5 3.7 %collective-permute-done.8.s10 = bf16[256,256]{1,0:T(8,128)(2,1)S(1)} collective-permute-done((bf16[256,256]{1,0:T(8,128)(2,1)S(1)}, bf16[256,256]{1,0:T(8,128)(2,1)S(1)}, u32[]{:S(2)}, u32[]{:S(2)}) %collective-permute-start.8) | collective-permute-done | bytes 131104 | tf_op jit(solution)/shard_map/ppermute | solution.py:349
  74.2 0.0 collective-permute-start.10
  74.2 0.0 collective-permute-done.9.s01
  74.2 1.3 %collective-permute-done.10.s11 = bf16[256,256]{1,0:T(8,128)(2,1)S(1)} collective-permute-done((bf16[256,256]{1,0:T(8,128)(2,1)S(1)}, bf16[256,256]{1,0:T(8,128)(2,1)S(1)}, u32[]{:S(2)}, u32[]{:S(2)}) %collective-permute-start.10) | collective-permute-done | bytes 131104 | tf_op jit(solution)/shard_map/ppermute | solution.py:349
  75.6 0.0 copy-done
  75.6 0.0 copy-done.3
  75.6 5.4 %shard_map.72 = (f32[2,2,2,16,256]{4,3,2,1,0:T(8,128)}, bf16[4,2,256,256]{3,2,1,0:T(8,128)(2,1)}) custom-call(s32[2,4]{1,0:T(2,128)S(1)} %bitcast.3, bf16[256,256]{1,0:T(8,128)(2,1)S(1)} %add_convert_fusion.s00, bf16[256,256]{1,0:T(8,128)(2,1)S(1)} %collective-permute-done.8.s10, bf16[256,256]{1,0:T(8,128)(2,1)S(1)} %collective-permute-done.9.s01, ...), custom_call_target="tpu_custom_call" | custom-call | tf_op jit(solution)/shard_map/pallas_call | solution.py:431
  (2 shorter events, 0.1 us)
Async XLA Ops:
  0.6 1.1 %copy-start.1 = (bf16[2,2,3,1,128,256]{5,4,3,2,1,0:T(8,128)(2,1)S(1)}, bf16[2,2,3,1,128,256]{5,4,3,2,1,0:T(8,128)(2,1)}, u32[]{:S(2)}) copy-start(bf16[2,2,3,1,128,256]{5,4,3,2,1,0:T(8,128)(2,1)} %vectors.1) | copy-start | bytes 2359300
  1.8 0.7 copy-start.2
  3.1 1.9 %collective-permute-start = (bf16[2,416,256]{2,1,0:T(8,128)(2,1)S(1)}, bf16[2,416,256]{2,1,0:T(8,128)(2,1)S(1)}, u32[]{:S(2)}, u32[]{:S(2)}) collective-permute-start(bf16[2,416,256]{2,1,0:T(8,128)(2,1)S(1)} %get-tuple-element.12), channel_id=1, source_target_pairs={{0,1},{1,0},{2,3},{3,2},{4,5},{5,4},{6,7},{7,6},{8,9},{9,8},{10,11... | collective-permute-start | bytes 1277960 | tf_op jit(solution)/shard_map/ppermute | solution.py:349
  5.8 29.0 %collective-permute-start.3 = (bf16[2,416,256]{2,1,0:T(8,128)(2,1)S(1)}, bf16[2,416,256]{2,1,0:T(8,128)(2,1)S(1)}, u32[]{:S(2)}, u32[]{:S(2)}) collective-permute-start(bf16[2,416,256]{2,1,0:T(8,128)(2,1)S(1)} %get-tuple-element.15.own), channel_id=1, source_target_pairs={{2,6},{0,12},{3,7},{1,13},{6,10},{4,0},{7,11},{5,1},{10,14},{8,4},... | collective-permute-start | bytes 1277960 | tf_op jit(solution)/shard_map/ppermute | solution.py:383
  10.9 24.0 %collective-permute-start.2 = (bf16[2,416,256]{2,1,0:T(8,128)(2,1)S(1)}, bf16[2,416,256]{2,1,0:T(8,128)(2,1)S(1)}, u32[]{:S(2)}, u32[]{:S(2)}) collective-permute-start(bf16[2,416,256]{2,1,0:T(8,128)(2,1)S(1)} %get-tuple-element.16), channel_id=1, source_target_pairs={{2,4},{0,14},{3,5},{1,15},{6,8},{4,2},{7,9},{5,3},{10,12},{8,6},{1... | collective-permute-start | bytes 1277960 | tf_op jit(solution)/shard_map/ppermute | solution.py:384
  12.0 22.8 %collective-permute-start.1 = (bf16[2,416,256]{2,1,0:T(8,128)(2,1)S(1)}, bf16[2,416,256]{2,1,0:T(8,128)(2,1)S(1)}, u32[]{:S(2)}, u32[]{:S(2)}) collective-permute-start(bf16[2,416,256]{2,1,0:T(8,128)(2,1)S(1)} %get-tuple-element.16), channel_id=1, source_target_pairs={{0,2},{1,3},{2,0},{3,1},{4,6},{5,7},{6,4},{7,5},{8,10},{9,11},{10,... | collective-permute-start | bytes 1277960 | tf_op jit(solution)/shard_map/ppermute | solution.py:349
  12.0 22.8 %collective-permute-start.4 = (bf16[416,256]{1,0:T(8,128)(2,1)S(1)}, bf16[416,256]{1,0:T(8,128)(2,1)S(1)}, u32[]{:S(2)}, u32[]{:S(2)}) collective-permute-start(bf16[416,256]{1,0:T(8,128)(2,1)S(1)} %get-tuple-element.17), channel_id=1, source_target_pairs={{0,4},{2,14},{1,5},{3,15},{4,8},{6,2},{5,9},{7,3},{8,12},{10,6},{9... | collective-permute-start | bytes 638984 | tf_op jit(solution)/shard_map/ppermute | solution.py:385
  47.7 2.6 %copy-start.4 = (s32[2]{0:T(128)S(1)}, s32[2]{0:T(128)}, u32[]{:S(2)}) copy-start(s32[2]{0:T(128)} %directions.1) | copy-start | bytes 28
  47.7 2.6 %collective-permute-start.5 = (bf16[5,384,256]{2,1,0:T(8,128)(2,1)S(1)}, bf16[5,384,256]{2,1,0:T(8,128)(2,1)S(1)}, u32[]{:S(2)}, u32[]{:S(2)}) collective-permute-start(bf16[5,384,256]{2,1,0:T(8,128)(2,1)S(1)} %get-tuple-element.18.mine), channel_id=1, source_target_pairs={{0,1},{1,0},{2,3},{3,2},{4,5},{5,4},{6,7},{7,6},{8,9},{9,8},{10,11... | collective-permute-start | bytes 2949128 | tf_op jit(solution)/shard_map/ppermute | solution.py:349
  55.0 20.6 %copy-start = (bf16[4,2,256,256]{3,2,1,0:T(8,128)(2,1)S(1)}, bf16[4,2,256,256]{3,2,1,0:T(8,128)(2,1)}, u32[]{:S(2)}) copy-start(bf16[4,2,256,256]{3,2,1,0:T(8,128)(2,1)} %perambulators.1) | copy-start | bytes 3145732
  55.0 5.6 %collective-permute-start.6 = (bf16[256,256]{1,0:T(8,128)(2,1)S(1)}, bf16[256,256]{1,0:T(8,128)(2,1)S(1)}, u32[]{:S(2)}, u32[]{:S(2)}) collective-permute-start(bf16[256,256]{1,0:T(8,128)(2,1)S(1)} %get-tuple-element.21), channel_id=1, source_target_pairs={{0,4},{1,5},{2,6},{3,7},{4,0},{5,1},{6,2},{7,3},{8,12},{9,13},{10,... | collective-permute-start | bytes 393224 | tf_op jit(solution)/shard_map/ppermute | solution.py:349
  60.6 8.5 %collective-permute-start.7 = (bf16[256,256]{1,0:T(8,128)(2,1)S(1)}, bf16[256,256]{1,0:T(8,128)(2,1)S(1)}, u32[]{:S(2)}, u32[]{:S(2)}) collective-permute-start(bf16[256,256]{1,0:T(8,128)(2,1)S(1)} %fusion), channel_id=1, source_target_pairs={{0,8},{1,9},{2,10},{3,11},{4,12},{5,13},{6,14},{7,15},{8,0},{9,1},... | collective-permute-start | bytes 393224 | tf_op jit(solution)/shard_map/ppermute | solution.py:349
  69.2 6.4 %copy-start.3 = (s32[4,2]{0,1:T(2,128)S(1)}, s32[4,2]{0,1:T(2,128)}, u32[]{:S(2)}) copy-start(s32[4,2]{0,1:T(2,128)} %param.8) | copy-start | bytes 100
  69.2 5.0 %collective-permute-start.8 = (bf16[256,256]{1,0:T(8,128)(2,1)S(1)}, bf16[256,256]{1,0:T(8,128)(2,1)S(1)}, u32[]{:S(2)}, u32[]{:S(2)}) collective-permute-start(bf16[256,256]{1,0:T(8,128)(2,1)S(1)} %add_convert_fusion.s00), channel_id=1, source_target_pairs={{0,2},{1,3},{2,0},{3,1},{4,6},{5,7},{6,4},{7,5},{8,10},{9,11},{10,... | collective-permute-start | bytes 393224 | tf_op jit(solution)/shard_map/ppermute | solution.py:349
  70.5 3.7 %collective-permute-start.9 = (bf16[256,256]{1,0:T(8,128)(2,1)S(1)}, bf16[256,256]{1,0:T(8,128)(2,1)S(1)}, u32[]{:S(2)}, u32[]{:S(2)}) collective-permute-start(bf16[256,256]{1,0:T(8,128)(2,1)S(1)} %add_convert_fusion.s00), channel_id=1, source_target_pairs={{0,1},{1,0},{2,3},{3,2},{4,5},{5,4},{6,7},{7,6},{8,9},{9,8},{10,11... | collective-permute-start | bytes 393224 | tf_op jit(solution)/shard_map/ppermute | solution.py:349
  74.2 1.3 %collective-permute-start.10 = (bf16[256,256]{1,0:T(8,128)(2,1)S(1)}, bf16[256,256]{1,0:T(8,128)(2,1)S(1)}, u32[]{:S(2)}, u32[]{:S(2)}) collective-permute-start(bf16[256,256]{1,0:T(8,128)(2,1)S(1)} %collective-permute-done.8.s10), channel_id=1, source_target_pairs={{0,1},{1,0},{2,3},{3,2},{4,5},{5,4},{6,7},{7,6},{8,9},{9,8},{10,11... | collective-permute-start | bytes 393224 | tf_op jit(solution)/shard_map/ppermute | solution.py:349

commit v2 on v1

--- a/solution.py
+++ b/solution.py
@@ -143,7 +143,7 @@
     rims_out[...] = rims[2:6]
     ahead_x, ahead_y, behind_x, behind_y, same = site_masks()
 
-    def build(z, carry):
+    def build(z):
         table = link_planes(rims[z])
         below = link_planes(rims[z - 1])
         lane = lax.broadcasted_iota(jnp.int32, table.shape, 1)
@@ -170,9 +170,9 @@
                         operator[z - 1, rows, pl.ds((k * COLORS + j) * SITES, SITES)] = (
                             block.astype(bf16)
                         )
-        return carry
-
-    lax.fori_loop(1, 8, build, 0)
+
+    for z in range(1, 8):
+        build(z)
     half = SITES
 
     def step(source, z, z_operator):
@@ -188,16 +188,10 @@
         center = source[z].astype(f32)
         return ((1.0 - 6.0 * SMEAR) * center + SMEAR * hops).astype(bf16)
 
-    def smear_first(z, carry):
+    for z in range(1, 8):
         grown[z - 1] = step(fields, z, z - 1)
-        return carry
-
-    def smear_second(z, carry):
+    for z in range(1, 6):
         w_out[z - 1] = step(grown, z, z)
-        return carry
-
-    lax.fori_loop(1, 8, smear_first, 0)
-    lax.fori_loop(1, 6, smear_second, 0)
 
 
 def elemental_kernel(scale, directions, mine, theirs, rims, out, out_low, w, right, sems):
@@ -228,7 +222,7 @@
     mask_z = jnp.where(same, one, zero)
     mask = jnp.where(is_x, mask_x, jnp.where(is_y, mask_y, mask_z))
 
-    def displace(z, carry):
+    for z in range(planes - 1):
         table = link_planes(rims[z])
         lane = lax.broadcasted_iota(jnp.int32, table.shape, 1)
         count = 2 * COLORS * COLORS
@@ -262,9 +256,6 @@
         right[z, 0, :, pl.ds(vectors, vectors)] = rest
         right[z, 1, :, pl.ds(0, vectors)] = rest
         right[z, 1, :, pl.ds(vectors, vectors)] = -total
-        return carry
-
-    lax.fori_loop(0, planes - 1, displace, 0)
     vectors = 2 * half
     depth = (planes - 1) * 2 * FIELD
     product = lax.dot_general(
@@ -309,7 +300,7 @@
         right[t, size:, :size] = -imag
         right[t, size:, size:] = real
 
-    def contract(p, carry):
+    for p in range(perambulators.shape[0]):
         source, sink = pairs[0, p], pairs[1, p]
         propagator = perambulators[p].reshape(2 * size, size)
         first = jnp.dot(left[sink], propagator, preferred_element_type=f32).astype(bf16)
@@ -326,9 +317,6 @@
             both, turned, (((1,), (1,)), ((), ())), preferred_element_type=f32
         ).astype(bf16)
         out[p] = third.reshape(2, size, size)
-        return carry
-
-    lax.fori_loop(0, perambulators.shape[0], contract, 0)
 
 
 def params(megabytes):

time: 81.2 us -> 74.1 us (0.913)
  Pallas kernels: 24.2 us -> 17.1 us
    pallas_call x1, Pallas kernels: 12.8 us -> 7.88 us  [body(): pl.pallas_call(smear_kernel, out_shape=(w_shape, rims_shape), in_specs=[a...]
    pallas_call x1, Pallas kernels: 5.41 us -> 4.16 us  [body(): pl.pallas_call(functools.partial(pair_kernel, pair_scale), out_shape=(jax...]
    pallas_call x1, Pallas kernels: 4.59 us -> 3.71 us  [body(): pl.pallas_call(functools.partial(elemental_kernel, site_scale), out_shape...]
where the time goes in v2:
time: 74.1 us; the launch traced here: 73.9 us
  waiting for transfers between devices  41.4 us (56%)
  Pallas kernels  17.1 us (23%)
  starting transfers between devices  12.7 us (17%)
  local copies, waits for them, and re-layouts  1.89 us (3%)
    ppermute x1, waiting for transfers between devices, body(): last = lax.ppermute(edge, 'space', outer)  22.6 us
    ppermute x8, waiting for transfers between devices, swap(): return lax.ppermute(value, 'space', [(i, i ^ bit) for i in range(n)])  18.8 us
    pallas_call x1, Pallas kernels, body(): pl.pallas_call(smear_kernel, out_shape=(w_shape, rims_shape), in_specs=[a...  7.88 us
    ppermute x8, starting transfers between devices, swap(): return lax.ppermute(value, 'space', [(i, i ^ bit) for i in range(n)])  6.2 us
    ppermute x1, starting transfers between devices, body(): second = lax.ppermute(own, 'space', straight)  5.03 us
    pallas_call x1, Pallas kernels, body(): pl.pallas_call(functools.partial(pair_kernel, pair_scale), out_shape=(jax...  4.16 us
    pallas_call x1, Pallas kernels, body(): pl.pallas_call(functools.partial(elemental_kernel, site_scale), out_shape...  3.71 us
    unnamed x10, local copies, waits for them, and re-layouts  1.89 us
  transfers between devices with their start and end apart: 11, of which 7 were waited for; matrix products, arithmetic and copies ran while one was open for 0% of the time, Pallas kernels for 0%

profile of v2, /device:TPU:0, one launch (start us, length us, event | category | flops | bytes accessed | tf_op | source)
XLA Modules:
  0.0 73.9 jit_solution(15386737264542881102)
XLA Ops:
  0.6 0.0 copy-start.1
  0.6 1.1 %copy-done.1 = bf16[2,2,3,1,128,256]{5,4,3,2,1,0:T(8,128)(2,1)S(1)} copy-done((bf16[2,2,3,1,128,256]{5,4,3,2,1,0:T(8,128)(2,1)S(1)}, bf16[2,2,3,1,128,256]{5,4,3,2,1,0:T(8,128)(2,1)}, u32[]{:S(2)}) %copy-start.1) | copy-done | bytes 786456
  1.8 0.0 copy-start.2
  1.8 0.7 %copy-done.2 = bf16[2,3,2,3,3,1,128]{6,2,5,4,3,1,0:T(2,128)(2,1)S(1)} copy-done((bf16[2,3,2,3,3,1,128]{6,2,5,4,3,1,0:T(2,128)(2,1)S(1)}, bf16[2,3,2,3,3,1,128]{6,2,5,4,3,1,0:T(2,128)(2,1)}, u32[]{:S(2)}) %copy-start.2) | copy-done | bytes 27672
  2.5 0.6 shard_map.68
  3.1 0.5 collective-permute-start
  3.6 1.4 %collective-permute-done.received = bf16[2,416,256]{2,1,0:T(8,128)(2,1)S(1)} collective-permute-done((bf16[2,416,256]{2,1,0:T(8,128)(2,1)S(1)}, bf16[2,416,256]{2,1,0:T(8,128)(2,1)S(1)}, u32[]{:S(2)}, u32[]{:S(2)}) %collective-permute-start) | collective-permute-done | bytes 426016 | tf_op jit(solution)/shard_map/ppermute | solution.py:337
  5.0 0.8 %shard_map.69 = (bf16[2,416,256]{2,1,0:T(8,128)(2,1)S(1)}, bf16[2,416,256]{2,1,0:T(8,128)(2,1)S(1)}, bf16[416,256]{1,0:T(8,128)(2,1)S(1)}) custom-call(bf16[2,416,256]{2,1,0:T(8,128)(2,1)S(1)} %collective-permute-done.received, bf16[2,416,256]{2,1,0:T(8,128)(2,1)S(1)} %get-tuple-element.13.own_in, ...), custom_call_target="tpu_custom_call", output_to_operand_aliasing={{0}: (1, {}), {1}: (2, {})} | custom-call | tf_op jit(solution)/shard_map/pallas_call | solution.py:352
  5.8 5.0 %collective-permute-start.3 = (bf16[2,416,256]{2,1,0:T(8,128)(2,1)S(1)}, bf16[2,416,256]{2,1,0:T(8,128)(2,1)S(1)}, u32[]{:S(2)}, u32[]{:S(2)}) collective-permute-start(bf16[2,416,256]{2,1,0:T(8,128)(2,1)S(1)} %get-tuple-element.15.own), channel_id=1, source_target_pairs={{2,6},{0,12},{3,7},{1,13},{6,10},{4,0},{7,11},{5,1},{10,14},{8,4},... | collective-permute-start | bytes 1277960 | tf_op jit(solution)/shard_map/ppermute | solution.py:371
  10.9 1.2 %collective-permute-start.2 = (bf16[2,416,256]{2,1,0:T(8,128)(2,1)S(1)}, bf16[2,416,256]{2,1,0:T(8,128)(2,1)S(1)}, u32[]{:S(2)}, u32[]{:S(2)}) collective-permute-start(bf16[2,416,256]{2,1,0:T(8,128)(2,1)S(1)} %get-tuple-element.16), channel_id=1, source_target_pairs={{2,4},{0,14},{3,5},{1,15},{6,8},{4,2},{7,9},{5,3},{10,12},{8,6},{1... | collective-permute-start | bytes 1277960 | tf_op jit(solution)/shard_map/ppermute | solution.py:372
  12.0 0.0 collective-permute-start.1
  12.0 0.3 collective-permute-start.4
  12.3 22.6 %collective-permute-done.4.last = bf16[416,256]{1,0:T(8,128)(2,1)S(1)} collective-permute-done((bf16[416,256]{1,0:T(8,128)(2,1)S(1)}, bf16[416,256]{1,0:T(8,128)(2,1)S(1)}, u32[]{:S(2)}, u32[]{:S(2)}) %collective-permute-start.4) | collective-permute-done | bytes 213024 | tf_op jit(solution)/shard_map/ppermute | solution.py:373
  34.9 0.0 collective-permute-done.3.second
  34.9 0.0 collective-permute-done.2.first
  34.9 0.0 collective-permute-done.1.across
  34.9 7.9 %shard_map.70 = (bf16[5,384,256]{2,1,0:T(8,128)(2,1)S(1)}, bf16[4,32,256]{2,1,0:T(8,128)(2,1)S(1)}) custom-call(bf16[2,416,256]{2,1,0:T(8,128)(2,1)S(1)} %get-tuple-element.15.own, bf16[2,416,256]{2,1,0:T(8,128)(2,1)S(1)} %collective-permute-done.1.across, bf16[2,416,256]{2,1,0:T(8,128)(2,1)S(1)} %collective-permute-done.2.first, ...), custom_call_target="tpu_custom_call" | custom-call | tf_op jit(solution)/shard_map/pallas_call | solution.py:377
  42.8 0.0 copy-start.4
  42.8 0.1 collective-permute-start.5
  42.9 2.6 %collective-permute-done.5.theirs = bf16[5,384,256]{2,1,0:T(8,128)(2,1)S(1)} collective-permute-done((bf16[5,384,256]{2,1,0:T(8,128)(2,1)S(1)}, bf16[5,384,256]{2,1,0:T(8,128)(2,1)S(1)}, u32[]{:S(2)}, u32[]{:S(2)}) %collective-permute-start.5) | collective-permute-done | bytes 983072 | tf_op jit(solution)/shard_map/ppermute | solution.py:337
  45.4 0.0 copy-done.4
  45.4 3.7 %shard_map.71 = (f32[256,256]{1,0:T(8,128)S(1)}, bf16[256,256]{1,0:T(8,128)(2,1)S(1)}) custom-call(s32[2]{0:T(128)S(1)} %copy-done.4, bf16[5,384,256]{2,1,0:T(8,128)(2,1)S(1)} %get-tuple-element.18.mine, bf16[5,384,256]{2,1,0:T(8,128)(2,1)S(1)} %collective-permute-done.5.theirs, bf16[4,32,256]{2,1,0:T(8,128)(2,1)S(1)} %get-tuple-element.19.rims), custom_call_target="tpu_custom_call" | custom-call | tf_op jit(solution)/shard_map/pallas_call | solution.py:394
  49.1 0.0 copy-start
  49.2 1.7 %collective-permute-start.6 = (bf16[256,256]{1,0:T(8,128)(2,1)S(1)}, bf16[256,256]{1,0:T(8,128)(2,1)S(1)}, u32[]{:S(2)}, u32[]{:S(2)}) collective-permute-start(bf16[256,256]{1,0:T(8,128)(2,1)S(1)} %get-tuple-element.21), channel_id=1, source_target_pairs={{0,4},{1,5},{2,6},{3,7},{4,0},{5,1},{6,2},{7,3},{8,12},{9,13},{10,... | collective-permute-start | bytes 393224 | tf_op jit(solution)/shard_map/ppermute | solution.py:337
  50.9 3.9 %collective-permute-done.6 = bf16[256,256]{1,0:T(8,128)(2,1)S(1)} collective-permute-done((bf16[256,256]{1,0:T(8,128)(2,1)S(1)}, bf16[256,256]{1,0:T(8,128)(2,1)S(1)}, u32[]{:S(2)}, u32[]{:S(2)}) %collective-permute-start.6) | collective-permute-done | bytes 131104 | tf_op jit(solution)/shard_map/ppermute | solution.py:337
  54.8 2.5 %collective-permute-start.7 = (bf16[256,256]{1,0:T(8,128)(2,1)S(1)}, bf16[256,256]{1,0:T(8,128)(2,1)S(1)}, u32[]{:S(2)}, u32[]{:S(2)}) collective-permute-start(bf16[256,256]{1,0:T(8,128)(2,1)S(1)} %fusion), channel_id=1, source_target_pairs={{0,8},{1,9},{2,10},{3,11},{4,12},{5,13},{6,14},{7,15},{8,0},{9,1},... | collective-permute-start | bytes 393224 | tf_op jit(solution)/shard_map/ppermute | solution.py:337
  57.3 6.0 %collective-permute-done.7 = bf16[256,256]{1,0:T(8,128)(2,1)S(1)} collective-permute-done((bf16[256,256]{1,0:T(8,128)(2,1)S(1)}, bf16[256,256]{1,0:T(8,128)(2,1)S(1)}, u32[]{:S(2)}, u32[]{:S(2)}) %collective-permute-start.7) | collective-permute-done | bytes 131104 | tf_op jit(solution)/shard_map/ppermute | solution.py:337
  63.3 0.0 copy-start.3
  63.3 1.4 %collective-permute-start.8 = (bf16[256,256]{1,0:T(8,128)(2,1)S(1)}, bf16[256,256]{1,0:T(8,128)(2,1)S(1)}, u32[]{:S(2)}, u32[]{:S(2)}) collective-permute-start(bf16[256,256]{1,0:T(8,128)(2,1)S(1)} %add_convert_fusion.s00), channel_id=1, source_target_pairs={{0,2},{1,3},{2,0},{3,1},{4,6},{5,7},{6,4},{7,5},{8,10},{9,11},{10,... | collective-permute-start | bytes 393224 | tf_op jit(solution)/shard_map/ppermute | solution.py:337
  64.7 0.0 collective-permute-start.9
  64.7 3.6 %collective-permute-done.8.s10 = bf16[256,256]{1,0:T(8,128)(2,1)S(1)} collective-permute-done((bf16[256,256]{1,0:T(8,128)(2,1)S(1)}, bf16[256,256]{1,0:T(8,128)(2,1)S(1)}, u32[]{:S(2)}, u32[]{:S(2)}) %collective-permute-start.8) | collective-permute-done | bytes 131104 | tf_op jit(solution)/shard_map/ppermute | solution.py:337
  68.4 0.0 collective-permute-start.10
  68.4 0.0 collective-permute-done.9.s01
  68.4 1.3 %collective-permute-done.10.s11 = bf16[256,256]{1,0:T(8,128)(2,1)S(1)} collective-permute-done((bf16[256,256]{1,0:T(8,128)(2,1)S(1)}, bf16[256,256]{1,0:T(8,128)(2,1)S(1)}, u32[]{:S(2)}, u32[]{:S(2)}) %collective-permute-start.10) | collective-permute-done | bytes 131104 | tf_op jit(solution)/shard_map/ppermute | solution.py:337
  69.7 0.0 copy-done
  69.7 0.0 copy-done.3
  69.7 4.2 %shard_map.72 = (f32[2,2,2,16,256]{4,3,2,1,0:T(8,128)}, bf16[4,2,256,256]{3,2,1,0:T(8,128)(2,1)}) custom-call(s32[2,4]{1,0:T(2,128)S(1)} %bitcast.3, bf16[256,256]{1,0:T(8,128)(2,1)S(1)} %add_convert_fusion.s00, bf16[256,256]{1,0:T(8,128)(2,1)S(1)} %collective-permute-done.8.s10, bf16[256,256]{1,0:T(8,128)(2,1)S(1)} %collective-permute-done.9.s01, ...), custom_call_target="tpu_custom_call" | custom-call | tf_op jit(solution)/shard_map/pallas_call | solution.py:419
  (2 shorter events, 0.1 us)
Async XLA Ops:
  0.6 1.1 %copy-start.1 = (bf16[2,2,3,1,128,256]{5,4,3,2,1,0:T(8,128)(2,1)S(1)}, bf16[2,2,3,1,128,256]{5,4,3,2,1,0:T(8,128)(2,1)}, u32[]{:S(2)}) copy-start(bf16[2,2,3,1,128,256]{5,4,3,2,1,0:T(8,128)(2,1)} %vectors.1) | copy-start | bytes 2359300
  1.8 0.7 %copy-start.2 = (bf16[2,3,2,3,3,1,128]{6,2,5,4,3,1,0:T(2,128)(2,1)S(1)}, bf16[2,3,2,3,3,1,128]{6,2,5,4,3,1,0:T(2,128)(2,1)}, u32[]{:S(2)}) copy-start(bf16[2,3,2,3,3,1,128]{6,2,5,4,3,1,0:T(2,128)(2,1)} %param.6) | copy-start | bytes 82948
  3.1 1.9 %collective-permute-start = (bf16[2,416,256]{2,1,0:T(8,128)(2,1)S(1)}, bf16[2,416,256]{2,1,0:T(8,128)(2,1)S(1)}, u32[]{:S(2)}, u32[]{:S(2)}) collective-permute-start(bf16[2,416,256]{2,1,0:T(8,128)(2,1)S(1)} %get-tuple-element.12), channel_id=1, source_target_pairs={{0,1},{1,0},{2,3},{3,2},{4,5},{5,4},{6,7},{7,6},{8,9},{9,8},{10,11... | collective-permute-start | bytes 1277960 | tf_op jit(solution)/shard_map/ppermute | solution.py:337
  5.8 29.0 %collective-permute-start.3 = (bf16[2,416,256]{2,1,0:T(8,128)(2,1)S(1)}, bf16[2,416,256]{2,1,0:T(8,128)(2,1)S(1)}, u32[]{:S(2)}, u32[]{:S(2)}) collective-permute-start(bf16[2,416,256]{2,1,0:T(8,128)(2,1)S(1)} %get-tuple-element.15.own), channel_id=1, source_target_pairs={{2,6},{0,12},{3,7},{1,13},{6,10},{4,0},{7,11},{5,1},{10,14},{8,4},... | collective-permute-start | bytes 1277960 | tf_op jit(solution)/shard_map/ppermute | solution.py:371
  10.9 24.0 %collective-permute-start.2 = (bf16[2,416,256]{2,1,0:T(8,128)(2,1)S(1)}, bf16[2,416,256]{2,1,0:T(8,128)(2,1)S(1)}, u32[]{:S(2)}, u32[]{:S(2)}) collective-permute-start(bf16[2,416,256]{2,1,0:T(8,128)(2,1)S(1)} %get-tuple-element.16), channel_id=1, source_target_pairs={{2,4},{0,14},{3,5},{1,15},{6,8},{4,2},{7,9},{5,3},{10,12},{8,6},{1... | collective-permute-start | bytes 1277960 | tf_op jit(solution)/shard_map/ppermute | solution.py:372
  12.0 22.8 %collective-permute-start.1 = (bf16[2,416,256]{2,1,0:T(8,128)(2,1)S(1)}, bf16[2,416,256]{2,1,0:T(8,128)(2,1)S(1)}, u32[]{:S(2)}, u32[]{:S(2)}) collective-permute-start(bf16[2,416,256]{2,1,0:T(8,128)(2,1)S(1)} %get-tuple-element.16), channel_id=1, source_target_pairs={{0,2},{1,3},{2,0},{3,1},{4,6},{5,7},{6,4},{7,5},{8,10},{9,11},{10,... | collective-permute-start | bytes 1277960 | tf_op jit(solution)/shard_map/ppermute | solution.py:337
  12.0 22.8 %collective-permute-start.4 = (bf16[416,256]{1,0:T(8,128)(2,1)S(1)}, bf16[416,256]{1,0:T(8,128)(2,1)S(1)}, u32[]{:S(2)}, u32[]{:S(2)}) collective-permute-start(bf16[416,256]{1,0:T(8,128)(2,1)S(1)} %get-tuple-element.17), channel_id=1, source_target_pairs={{0,4},{2,14},{1,5},{3,15},{4,8},{6,2},{5,9},{7,3},{8,12},{10,6},{9... | collective-permute-start | bytes 638984 | tf_op jit(solution)/shard_map/ppermute | solution.py:373
  42.8 2.6 %copy-start.4 = (s32[2]{0:T(128)S(1)}, s32[2]{0:T(128)}, u32[]{:S(2)}) copy-start(s32[2]{0:T(128)} %directions.1) | copy-start | bytes 28
  42.8 2.6 %collective-permute-start.5 = (bf16[5,384,256]{2,1,0:T(8,128)(2,1)S(1)}, bf16[5,384,256]{2,1,0:T(8,128)(2,1)S(1)}, u32[]{:S(2)}, u32[]{:S(2)}) collective-permute-start(bf16[5,384,256]{2,1,0:T(8,128)(2,1)S(1)} %get-tuple-element.18.mine), channel_id=1, source_target_pairs={{0,1},{1,0},{2,3},{3,2},{4,5},{5,4},{6,7},{7,6},{8,9},{9,8},{10,11... | collective-permute-start | bytes 2949128 | tf_op jit(solution)/shard_map/ppermute | solution.py:337
  49.1 20.6 %copy-start = (bf16[4,2,256,256]{3,2,1,0:T(8,128)(2,1)S(1)}, bf16[4,2,256,256]{3,2,1,0:T(8,128)(2,1)}, u32[]{:S(2)}) copy-start(bf16[4,2,256,256]{3,2,1,0:T(8,128)(2,1)} %perambulators.1) | copy-start | bytes 3145732
  49.2 5.6 %collective-permute-start.6 = (bf16[256,256]{1,0:T(8,128)(2,1)S(1)}, bf16[256,256]{1,0:T(8,128)(2,1)S(1)}, u32[]{:S(2)}, u32[]{:S(2)}) collective-permute-start(bf16[256,256]{1,0:T(8,128)(2,1)S(1)} %get-tuple-element.21), channel_id=1, source_target_pairs={{0,4},{1,5},{2,6},{3,7},{4,0},{5,1},{6,2},{7,3},{8,12},{9,13},{10,... | collective-permute-start | bytes 393224 | tf_op jit(solution)/shard_map/ppermute | solution.py:337
  54.8 8.5 %collective-permute-start.7 = (bf16[256,256]{1,0:T(8,128)(2,1)S(1)}, bf16[256,256]{1,0:T(8,128)(2,1)S(1)}, u32[]{:S(2)}, u32[]{:S(2)}) collective-permute-start(bf16[256,256]{1,0:T(8,128)(2,1)S(1)} %fusion), channel_id=1, source_target_pairs={{0,8},{1,9},{2,10},{3,11},{4,12},{5,13},{6,14},{7,15},{8,0},{9,1},... | collective-permute-start | bytes 393224 | tf_op jit(solution)/shard_map/ppermute | solution.py:337
  63.3 6.4 %copy-start.3 = (s32[4,2]{0,1:T(2,128)S(1)}, s32[4,2]{0,1:T(2,128)}, u32[]{:S(2)}) copy-start(s32[4,2]{0,1:T(2,128)} %param.8) | copy-start | bytes 100
  63.3 5.0 %collective-permute-start.8 = (bf16[256,256]{1,0:T(8,128)(2,1)S(1)}, bf16[256,256]{1,0:T(8,128)(2,1)S(1)}, u32[]{:S(2)}, u32[]{:S(2)}) collective-permute-start(bf16[256,256]{1,0:T(8,128)(2,1)S(1)} %add_convert_fusion.s00), channel_id=1, source_target_pairs={{0,2},{1,3},{2,0},{3,1},{4,6},{5,7},{6,4},{7,5},{8,10},{9,11},{10,... | collective-permute-start | bytes 393224 | tf_op jit(solution)/shard_map/ppermute | solution.py:337
  64.7 3.7 %collective-permute-start.9 = (bf16[256,256]{1,0:T(8,128)(2,1)S(1)}, bf16[256,256]{1,0:T(8,128)(2,1)S(1)}, u32[]{:S(2)}, u32[]{:S(2)}) collective-permute-start(bf16[256,256]{1,0:T(8,128)(2,1)S(1)} %add_convert_fusion.s00), channel_id=1, source_target_pairs={{0,1},{1,0},{2,3},{3,2},{4,5},{5,4},{6,7},{7,6},{8,9},{9,8},{10,11... | collective-permute-start | bytes 393224 | tf_op jit(solution)/shard_map/ppermute | solution.py:337
  68.4 1.3 %collective-permute-start.10 = (bf16[256,256]{1,0:T(8,128)(2,1)S(1)}, bf16[256,256]{1,0:T(8,128)(2,1)S(1)}, u32[]{:S(2)}, u32[]{:S(2)}) collective-permute-start(bf16[256,256]{1,0:T(8,128)(2,1)S(1)} %collective-permute-done.8.s10), channel_id=1, source_target_pairs={{0,1},{1,0},{2,3},{3,2},{4,5},{5,4},{6,7},{7,6},{8,9},{9,8},{10,11... | collective-permute-start | bytes 393224 | tf_op jit(solution)/shard_map/ppermute | solution.py:337

commit v3 on v2

--- a/solution.py
+++ b/solution.py
@@ -31,6 +31,10 @@
 
 def link_row(direction, part, row, column):
     return ((direction * COLORS + row) * COLORS + column) * 2 + part
+
+
+def slot_of(core, chip, t):
+    return core + (1 - 2 * core) * ((1 - chip) if t == 0 else chip)
 
 
 def split_kernel(vectors, links, own, other, send, packed, sems):
@@ -47,7 +51,7 @@
                 block = vectors.at[chip + t * (1 - 2 * chip), part, color, 0]
                 kept = (own, other)[t]
                 for source, target in (
-                    (block.at[:, near], kept.at[core, rows, lanes]),
+                    (block.at[:, near], kept.at[slot_of(core, chip, t), rows, lanes]),
                     (block.at[:, far], send.at[t, rows, lanes]),
                 ):
                     copies.append(pltpu.make_async_copy(source, target, sems.at[len(copies)]))
@@ -64,7 +68,7 @@
         rows = jnp.concatenate(gathered, axis=0).astype(bf16)
         packed[t, :, pl.ds(0, SITES)] = rows[:PACKED_LINKS]
         packed[t, :, pl.ds(SITES, SITES)] = rows[PACKED_LINKS:]
-        for target in ((own, other)[t].at[core], send.at[t]):
+        for target in ((own, other)[t].at[slot_of(core, chip, t)], send.at[t]):
             copies.append(
                 pltpu.make_async_copy(
                     packed.at[t], target.at[pl.ds(FIELD, PACKED_LINKS)], sems.at[len(copies)]
@@ -78,14 +82,14 @@
 def join_kernel(received, own_in, other_in, own, other, edge, sems):
     core, chip = position()
     copies = [
-        pltpu.make_async_copy(received.at[t], kept.at[1 - core], sems.at[t])
+        pltpu.make_async_copy(received.at[t], kept.at[1 - slot_of(core, chip, t)], sems.at[t])
         for t, kept in enumerate((own, other))
     ]
     for copy in copies:
         copy.start()
     for copy in copies:
         copy.wait()
-    copy = pltpu.make_async_copy(own.at[1 - chip], edge, sems.at[2])
+    copy = pltpu.make_async_copy(own.at[0], edge, sems.at[2])
     copy.start()
     copy.wait()
 
@@ -113,105 +117,153 @@
     return jnp.concatenate([packed[:, :SITES], packed[:, SITES:]], axis=0).astype(f32)
 
 
-def smear_kernel(own, across, first, second, last, w_out, rims_out, fields, rims, grown, operator, sems):
+def fetch(copies, sems):
+    started = [
+        pltpu.make_async_copy(source, target, sems.at[k])
+        for k, (source, target) in enumerate(copies)
+    ]
+    for copy in started:
+        copy.start()
+    for copy in started:
+        copy.wait()
+
+
+def field_of(package):
+    return package.at[:, pl.ds(0, FIELD)]
+
+
+def links_of(package):
+    return package.at[:, pl.ds(FIELD, PACKED_LINKS)]
+
+
+def build(operator, rims, at):
     _, chip = position()
-    own_at, across_at = 3 + chip, 5 - 3 * chip
-    first_at, second_at, last_at = 1 + 5 * chip, 7 - 7 * chip, 8 * chip
+    ascending = chip == 1
+    ahead_x, ahead_y, behind_x, behind_y, same = site_masks()
+    table = link_planes(rims[at])
+    below = link_planes(jnp.where(ascending, rims[at - 1], rims[at + 1]))
+    lane = lax.broadcasted_iota(jnp.int32, table.shape, 1)
+    from_x = pltpu.roll(table, LY, 1)
+    from_y = shift_y(table, lane)
+
+    def row_of(values, *what):
+        k = link_row(*what)
+        return values[k : k + 1]
+
+    for part in range(2):
+        sign = 1.0 if part == 0 else -1.0
+        for i in range(COLORS):
+            rows = pl.ds((part * COLORS + i) * SITES, SITES)
+            for j in range(COLORS):
+                zero = jnp.zeros((SITES, SITES), f32)
+                plane = jnp.where(ahead_x, row_of(from_x, 0, part, i, j), zero)
+                plane = jnp.where(ahead_y, row_of(from_y, 1, part, i, j), plane)
+                plane = jnp.where(behind_x, sign * row_of(table, 0, part, j, i), plane)
+                plane = jnp.where(behind_y, sign * row_of(table, 1, part, j, i), plane)
+                lower = sign * row_of(below, 2, part, j, i)
+                upper = row_of(table, 2, part, i, j)
+                before = jnp.where(same, jnp.where(ascending, lower, upper), zero)
+                after = jnp.where(same, jnp.where(ascending, upper, lower), zero)
+                for k, block in enumerate((before, plane, after)):
+                    operator[rows, pl.ds((k * COLORS + j) * SITES, SITES)] = block.astype(bf16)
+
+
+def smeared(operator, source, at):
+    half = SITES
+    window = source[pl.ds(at - 1, 3)].reshape(3 * FIELD, 2 * half)
+    product = jnp.dot(operator[...], window, preferred_element_type=f32)
+    hops = jnp.concatenate(
+        [
+            product[:FIELD, :half] - product[FIELD:, half:],
+            product[:FIELD, half:] + product[FIELD:, :half],
+        ],
+        axis=1,
+    )
+    center = source[at].astype(f32)
+    return ((1.0 - 6.0 * SMEAR) * center + SMEAR * hops).astype(bf16)
+
+
+def smear_inner(second, across, own, w_out, u_out, fields, rims, grown, operators, sems):
     copies = []
-    for k, (ref, at) in enumerate(
-        ((own, own_at), (across, across_at), (first, first_at), (second, second_at))
-    ):
-        copies.append(
-            pltpu.make_async_copy(
-                ref.at[:, pl.ds(0, FIELD)], fields.at[pl.ds(at, 2)], sems.at[2 * k]
-            )
-        )
-        copies.append(
-            pltpu.make_async_copy(
-                ref.at[:, pl.ds(FIELD, PACKED_LINKS)], rims.at[pl.ds(at, 2)], sems.at[2 * k + 1]
-            )
-        )
-    copies.append(pltpu.make_async_copy(last.at[pl.ds(0, FIELD)], fields.at[last_at], sems.at[8]))
-    copies.append(
-        pltpu.make_async_copy(last.at[pl.ds(FIELD, PACKED_LINKS)], rims.at[last_at], sems.at[9])
-    )
-    for copy in copies:
-        copy.start()
-    for copy in copies:
-        copy.wait()
-
-    rims_out[...] = rims[2:6]
-    ahead_x, ahead_y, behind_x, behind_y, same = site_masks()
-
-    def build(z):
-        table = link_planes(rims[z])
-        below = link_planes(rims[z - 1])
-        lane = lax.broadcasted_iota(jnp.int32, table.shape, 1)
-        from_x = pltpu.roll(table, LY, 1)
-        from_y = shift_y(table, lane)
-
-        def row_of(values, *what):
-            k = link_row(*what)
-            return values[k : k + 1]
-
-        for part in range(2):
-            sign = 1.0 if part == 0 else -1.0
-            for i in range(COLORS):
-                rows = pl.ds((part * COLORS + i) * SITES, SITES)
-                for j in range(COLORS):
-                    zero = jnp.zeros((SITES, SITES), f32)
-                    plane = jnp.where(ahead_x, row_of(from_x, 0, part, i, j), zero)
-                    plane = jnp.where(ahead_y, row_of(from_y, 1, part, i, j), plane)
-                    plane = jnp.where(behind_x, sign * row_of(table, 0, part, j, i), plane)
-                    plane = jnp.where(behind_y, sign * row_of(table, 1, part, j, i), plane)
-                    lower = jnp.where(same, sign * row_of(below, 2, part, j, i), zero)
-                    upper = jnp.where(same, row_of(table, 2, part, i, j), zero)
-                    for k, block in enumerate((lower, plane, upper)):
-                        operator[z - 1, rows, pl.ds((k * COLORS + j) * SITES, SITES)] = (
-                            block.astype(bf16)
-                        )
-
-    for z in range(1, 8):
-        build(z)
+    for k, package in enumerate((second, across, own)):
+        copies.append((field_of(package), fields.at[pl.ds(2 * k, 2)]))
+        copies.append((links_of(package), rims.at[pl.ds(2 * k, 2)]))
+    fetch(copies, sems)
+    for r in range(1, 5):
+        build(operators.at[r - 1], rims, r)
+        grown[r - 1] = smeared(operators.at[r - 1], fields, r)
+    for r in range(2, 4):
+        w_out[r - 2] = smeared(operators.at[r - 1], grown, r - 1)
+    u_out[...] = grown[2:4]
+
+
+def smear_middle(across, own, first, u_in, w_out, u_out, fields, rims, grown, operators, sems):
+    fetch(
+        [
+            (field_of(own), fields.at[pl.ds(0, 2)]),
+            (field_of(first), fields.at[pl.ds(2, 2)]),
+            (across.at[1, pl.ds(FIELD, PACKED_LINKS)], rims.at[0]),
+            (links_of(own), rims.at[pl.ds(1, 2)]),
+            (links_of(first), rims.at[pl.ds(3, 2)]),
+            (u_in, grown.at[pl.ds(0, 2)]),
+        ],
+        sems,
+    )
+    for r in (5, 6, 4):
+        build(operators.at[r - 4], rims, r - 3)
+        if r > 4:
+            grown[r - 3] = smeared(operators.at[r - 4], fields, r - 4)
+    for r in (4, 5):
+        w_out[r - 4] = smeared(operators.at[r - 4], grown, r - 3)
+    u_out[...] = grown[2:4]
+
+
+def smear_outer(own, first, last, u_in, w_out, fields, rims, grown, operators, sems):
+    fetch(
+        [
+            (field_of(first), fields.at[pl.ds(0, 2)]),
+            (last.at[pl.ds(0, FIELD)], fields.at[2]),
+            (own.at[1, pl.ds(FIELD, PACKED_LINKS)], rims.at[0]),
+            (links_of(first), rims.at[pl.ds(1, 2)]),
+            (last.at[pl.ds(FIELD, PACKED_LINKS)], rims.at[3]),
+            (u_in, grown.at[pl.ds(0, 2)]),
+        ],
+        sems,
+    )
+    build(operators.at[1], rims, 2)
+    grown[2] = smeared(operators.at[1], fields, 1)
+    build(operators.at[0], rims, 1)
+    w_out[0] = smeared(operators.at[0], grown, 1)
+
+
+def elemental_kernel(scale, directions, *refs):
+    mine, theirs, (across, own, first) = refs[:3], refs[3:6], refs[6:9]
+    out, out_low, w, rims, right, sems = refs[9:]
+    core, chip = position()
     half = SITES
-
-    def step(source, z, z_operator):
-        window = source[pl.ds(z - 1, 3)].reshape(3 * FIELD, 2 * half)
-        product = jnp.dot(operator[z_operator], window, preferred_element_type=f32)
-        hops = jnp.concatenate(
-            [
-                product[:FIELD, :half] - product[FIELD:, half:],
-                product[:FIELD, half:] + product[FIELD:, :half],
-            ],
-            axis=1,
-        )
-        center = source[z].astype(f32)
-        return ((1.0 - 6.0 * SMEAR) * center + SMEAR * hops).astype(bf16)
-
-    for z in range(1, 8):
-        grown[z - 1] = step(fields, z, z - 1)
-    for z in range(1, 6):
-        w_out[z - 1] = step(grown, z, z)
-
-
-def elemental_kernel(scale, directions, mine, theirs, rims, out, out_low, w, right, sems):
-    core, _ = position()
-    half = SITES
-    planes = mine.shape[0]
-    copies = []
-    for k, (ref, side) in enumerate(((mine, core), (theirs, 1 - core))):
-        for part in range(2):
-            copies.append(
-                pltpu.make_async_copy(
-                    ref.at[:, :, pl.ds(part * half, half)],
-                    w.at[:, part, :, pl.ds(pl.multiple_of(side * half, half), half)],
-                    sems.at[2 * k + part],
+    copies = [
+        (links_of(across), rims.at[pl.ds(0, 2)]),
+        (links_of(own), rims.at[pl.ds(2, 2)]),
+        (first.at[0, pl.ds(FIELD, PACKED_LINKS)], rims.at[4]),
+    ]
+    for group, side in ((mine, core), (theirs, 1 - core)):
+        at = 0
+        for ref in group:
+            count = ref.shape[0]
+            for part in range(2):
+                copies.append(
+                    (
+                        ref.at[:, :, pl.ds(part * half, half)],
+                        w.at[
+                            pl.ds(at, count),
+                            part,
+                            :,
+                            pl.ds(pl.multiple_of(side * half, half), half),
+                        ],
+                    )
                 )
-            )
-    for copy in copies:
-        copy.start()
-    for copy in copies:
-        copy.wait()
+            at += count
+    fetch(copies, sems)
     direction = directions[core]
     ahead_x, ahead_y, _, _, same = site_masks()
     one = jnp.ones((SITES, SITES), f32)
@@ -221,9 +273,12 @@
     mask_y = jnp.where(ahead_y, one, zero)
     mask_z = jnp.where(same, one, zero)
     mask = jnp.where(is_x, mask_x, jnp.where(is_y, mask_y, mask_z))
-
-    for z in range(planes - 1):
-        table = link_planes(rims[z])
+    start = jnp.where(is_z, 1 - chip, 0)
+    ahead = jnp.where(is_z, chip, 0)
+    steps = w.shape[0] - 1
+
+    for z in range(steps):
+        table = link_planes(rims[z + start])
         lane = lax.broadcasted_iota(jnp.int32, table.shape, 1)
         count = 2 * COLORS * COLORS
         along_x = pltpu.roll(table, LY, 1)[:count]
@@ -244,7 +299,7 @@
             ],
             axis=0,
         )
-        source = z + jnp.where(is_z, 1, 0)
+        source = z + ahead
         real = jnp.dot(operator, w[source, 0], preferred_element_type=f32)
         imag = jnp.dot(operator, w[source, 1], preferred_element_type=f32)
         hop_real = real[:FIELD] - imag[FIELD:]
@@ -257,9 +312,9 @@
         right[z, 1, :, pl.ds(0, vectors)] = rest
         right[z, 1, :, pl.ds(vectors, vectors)] = -total
     vectors = 2 * half
-    depth = (planes - 1) * 2 * FIELD
+    depth = steps * 2 * FIELD
     product = lax.dot_general(
-        w[pl.ds(0, planes - 1)].reshape(depth, vectors),
+        w[pl.ds(start, steps)].reshape(depth, vectors),
         right[...].reshape(depth, 2 * vectors),
         (((0,), (0,)), ((), ())),
         preferred_element_type=f32,
@@ -372,37 +427,49 @@
     first = lax.ppermute(other, "space", crossing)
     last = lax.ppermute(edge, "space", outer)
 
-    w_shape = jax.ShapeDtypeStruct((5, FIELD, vector_count), bf16)
-    rims_shape = jax.ShapeDtypeStruct((4, PACKED_LINKS, 2 * SITES), bf16)
-    mine, rims = pl.pallas_call(
-        smear_kernel,
-        out_shape=(w_shape, rims_shape),
-        in_specs=[anywhere] * 5,
-        out_specs=(vmem, vmem),
-        scratch_shapes=[
-            pltpu.VMEM((9, FIELD, vector_count), bf16),
-            pltpu.VMEM((9, PACKED_LINKS, 2 * SITES), bf16),
-            pltpu.VMEM((7, FIELD, vector_count), bf16),
-            pltpu.VMEM((7, 2 * FIELD, 3 * FIELD), bf16),
-            pltpu.SemaphoreType.DMA((10,)),
-        ],
-        compiler_params=params(24),
-    )(own, across, first, second, last)
-    theirs = swap(mine, 1)
+    def smear(kernel, operands, ranks, link_planes_held, grown_held, operators_held, outputs):
+        def shape(count):
+            return jax.ShapeDtypeStruct((count, FIELD, vector_count), bf16)
+
+        products = 2 * FIELD * 3 * FIELD * vector_count * (operators_held + outputs[0])
+        return pl.pallas_call(
+            kernel,
+            out_shape=tuple(shape(count) for count in outputs),
+            in_specs=[anywhere] * len(operands),
+            out_specs=(vmem,) * len(outputs),
+            scratch_shapes=[
+                pltpu.VMEM((ranks, FIELD, vector_count), bf16),
+                pltpu.VMEM((link_planes_held, PACKED_LINKS, 2 * SITES), bf16),
+                pltpu.VMEM((grown_held, FIELD, vector_count), bf16),
+                pltpu.VMEM((operators_held, 2 * FIELD, 3 * FIELD), bf16),
+                pltpu.SemaphoreType.DMA((6,)),
+            ],
+            compiler_params=params(20),
+            cost_estimate=pl.CostEstimate(
+                flops=4 * products, bytes_accessed=4 * 1024 * 1024, transcendentals=0
+            ),
+        )(*operands)
+
+    w_inner, u_inner = smear(smear_inner, (second, across, own), 6, 6, 4, 4, (2, 2))
+    w_middle, u_middle = smear(smear_middle, (across, own, first, u_inner), 4, 5, 4, 3, (2, 2))
+    (w_outer,) = smear(smear_outer, (own, first, last, u_middle), 3, 4, 3, 2, (1,))
+    mine = (w_inner, w_middle, w_outer)
+    theirs = tuple(swap(part, 1) for part in mine)
     site_scale = (6.0 * n * SITES) ** (-0.5)
     square = (vector_count, vector_count)
     partial, partial_low = pl.pallas_call(
         functools.partial(elemental_kernel, site_scale),
         out_shape=(jax.ShapeDtypeStruct(square, f32), jax.ShapeDtypeStruct(square, bf16)),
-        in_specs=[smem, anywhere, anywhere, vmem],
+        in_specs=[smem] + [anywhere] * 9,
         out_specs=(vmem, vmem),
         scratch_shapes=[
             pltpu.VMEM((5, 2, FIELD, vector_count), bf16),
+            pltpu.VMEM((5, PACKED_LINKS, 2 * SITES), bf16),
             pltpu.VMEM((4, 2, FIELD, 2 * vector_count), bf16),
-            pltpu.SemaphoreType.DMA((4,)),
+            pltpu.SemaphoreType.DMA((15,)),
         ],
         compiler_params=params(16),
-    )(directions, mine, theirs, rims)
+    )(directions, *mine, *theirs, across, own, first)
 
     bit = 4
     while bit < n:

time: 74.1 us -> 70.9 us (0.957)
  waiting for transfers between devices: 41.4 us -> 34.6 us
  Pallas kernels: 17.1 us -> 19.5 us
  starting transfers between devices: 12.7 us -> 13.8 us
    ppermute x1, waiting for transfers between devices: 22.6 us -> 0.26 us  [body(): last = lax.ppermute(edge, 'space', outer)]
    ppermute x8 -> x10, waiting for transfers between devices: 18.8 us -> 25.3 us  [swap(): return lax.ppermute(value, 'space', [(i, i ^ bit) for i in range(n)])]
    ppermute x1, waiting for transfers between devices: 0.01 us -> 5.36 us  [body(): first = lax.ppermute(other, 'space', crossing)]
    ppermute x8 -> x10, starting transfers between devices: 6.2 us -> 10.2 us  [swap(): return lax.ppermute(value, 'space', [(i, i ^ bit) for i in range(n)])]
    ppermute x1, waiting for transfers between devices: 0.01 us -> 3.71 us  [body(): second = lax.ppermute(own, 'space', straight)]
    pallas_call x1 -> x3, Pallas kernels: 7.88 us -> 9.91 us  [smear(): pl.pallas_call(kernel, out_shape=tuple((shape(count) for count in outputs...]
    ppermute x1, starting transfers between devices: 5.03 us -> 3.6 us  [body(): second = lax.ppermute(own, 'space', straight)]
    ppermute x1, starting transfers between devices: 1.18 us -> 0.01 us  [body(): first = lax.ppermute(other, 'space', crossing)]
  transfers between devices with their start and end apart: 11 -> 13, of which waited for: 7 -> 10; matrix products, arithmetic and copies ran while one was open for 0% -> 0% of each run, Pallas kernels for 0% -> 14%
where the time goes in v3:
time: 70.9 us; the launch traced here: 70.7 us
  waiting for transfers between devices  34.6 us (49%)
  Pallas kernels  19.5 us (28%)
  starting transfers between devices  13.8 us (19%)
  local copies, waits for them, and re-layouts  1.89 us (3%)
  between operations  0.75 us (1%)
    ppermute x10, waiting for transfers between devices, swap(): return lax.ppermute(value, 'space', [(i, i ^ bit) for i in range(n)])  25.3 us
    ppermute x10, starting transfers between devices, swap(): return lax.ppermute(value, 'space', [(i, i ^ bit) for i in range(n)])  10.2 us
    pallas_call x3, Pallas kernels, smear(): pl.pallas_call(kernel, out_shape=tuple((shape(count) for count in outputs...  9.91 us
    ppermute x1, waiting for transfers between devices, body(): first = lax.ppermute(other, 'space', crossing)  5.36 us
    pallas_call x1, Pallas kernels, body(): pl.pallas_call(functools.partial(pair_kernel, pair_scale), out_shape=(jax...  4.15 us
    pallas_call x1, Pallas kernels, body(): pl.pallas_call(functools.partial(elemental_kernel, site_scale), out_shape...  4.08 us
    ppermute x1, waiting for transfers between devices, body(): second = lax.ppermute(own, 'space', straight)  3.71 us
    ppermute x1, starting transfers between devices, body(): second = lax.ppermute(own, 'space', straight)  3.6 us
  transfers between devices with their start and end apart: 13, of which 10 were waited for; matrix products, arithmetic and copies ran while one was open for 0% of the time, Pallas kernels for 14%

profile of v3, /device:TPU:0, one launch (start us, length us, event | category | flops | bytes accessed | tf_op | source)
XLA Modules:
  0.0 70.7 jit_solution(17955186181408529411)
XLA Ops:
  0.6 0.0 copy-start.1
  0.6 1.1 %copy-done.1 = bf16[2,2,3,1,128,256]{5,4,3,2,1,0:T(8,128)(2,1)S(1)} copy-done((bf16[2,2,3,1,128,256]{5,4,3,2,1,0:T(8,128)(2,1)S(1)}, bf16[2,2,3,1,128,256]{5,4,3,2,1,0:T(8,128)(2,1)}, u32[]{:S(2)}) %copy-start.1) | copy-done | bytes 786456
  1.8 0.0 copy-start.2
  1.8 0.7 %copy-done.2 = bf16[2,3,2,3,3,1,128]{6,2,5,4,3,1,0:T(2,128)(2,1)S(1)} copy-done((bf16[2,3,2,3,3,1,128]{6,2,5,4,3,1,0:T(2,128)(2,1)S(1)}, bf16[2,3,2,3,3,1,128]{6,2,5,4,3,1,0:T(2,128)(2,1)}, u32[]{:S(2)}) %copy-start.2) | copy-done | bytes 27672
  2.5 0.6 shard_map.68
  3.1 0.5 collective-permute-start
  3.6 1.4 %collective-permute-done.received = bf16[2,416,256]{2,1,0:T(8,128)(2,1)S(1)} collective-permute-done((bf16[2,416,256]{2,1,0:T(8,128)(2,1)S(1)}, bf16[2,416,256]{2,1,0:T(8,128)(2,1)S(1)}, u32[]{:S(2)}, u32[]{:S(2)}) %collective-permute-start) | collective-permute-done | bytes 426016 | tf_op jit(solution)/shard_map/ppermute | solution.py:392
  5.0 0.8 %shard_map.69 = (bf16[2,416,256]{2,1,0:T(8,128)(2,1)S(1)}, bf16[2,416,256]{2,1,0:T(8,128)(2,1)S(1)}, bf16[416,256]{1,0:T(8,128)(2,1)S(1)}) custom-call(bf16[2,416,256]{2,1,0:T(8,128)(2,1)S(1)} %collective-permute-done.received, bf16[2,416,256]{2,1,0:T(8,128)(2,1)S(1)} %get-tuple-element.15.own_in, ...), custom_call_target="tpu_custom_call", output_to_operand_aliasing={{0}: (1, {}), {1}: (2, {})} | custom-call | tf_op jit(solution)/shard_map/pallas_call | solution.py:407
  5.8 3.0 %collective-permute-start.2 = (bf16[2,416,256]{2,1,0:T(8,128)(2,1)S(1)}, bf16[2,416,256]{2,1,0:T(8,128)(2,1)S(1)}, u32[]{:S(2)}, u32[]{:S(2)}) collective-permute-start(bf16[2,416,256]{2,1,0:T(8,128)(2,1)S(1)} %get-tuple-element.18), channel_id=1, source_target_pairs={{0,2},{1,3},{2,0},{3,1},{4,6},{5,7},{6,4},{7,5},{8,10},{9,11},{10,... | collective-permute-start | bytes 1277960 | tf_op jit(solution)/shard_map/ppermute | solution.py:392
  8.8 3.6 %collective-permute-start.1 = (bf16[2,416,256]{2,1,0:T(8,128)(2,1)S(1)}, bf16[2,416,256]{2,1,0:T(8,128)(2,1)S(1)}, u32[]{:S(2)}, u32[]{:S(2)}) collective-permute-start(bf16[2,416,256]{2,1,0:T(8,128)(2,1)S(1)} %get-tuple-element.17.own.refs_7_), channel_id=1, source_target_pairs={{2,6},{0,12},{3,7},{1,13},{6,10},{4,0},{7,11},{5,1},{10,14},{8,4},... | collective-permute-start | bytes 1277960 | tf_op jit(solution)/shard_map/ppermute | solution.py:426
  12.4 0.0 collective-permute-start.3
  12.4 0.0 collective-permute-start.4
  12.4 6.5 %collective-permute-done.2.across.refs_6_ = bf16[2,416,256]{2,1,0:T(8,128)(2,1)S(1)} collective-permute-done((bf16[2,416,256]{2,1,0:T(8,128)(2,1)S(1)}, bf16[2,416,256]{2,1,0:T(8,128)(2,1)S(1)}, u32[]{:S(2)}, u32[]{:S(2)}) %collective-permute-start.2) | collective-permute-done | bytes 426016 | tf_op jit(solution)/shard_map/ppermute | solution.py:392
  18.9 3.7 %collective-permute-done.1.second = bf16[2,416,256]{2,1,0:T(8,128)(2,1)S(1)} collective-permute-done((bf16[2,416,256]{2,1,0:T(8,128)(2,1)S(1)}, bf16[2,416,256]{2,1,0:T(8,128)(2,1)S(1)}, u32[]{:S(2)}, u32[]{:S(2)}) %collective-permute-start.1) | collective-permute-done | bytes 426016 | tf_op jit(solution)/shard_map/ppermute | solution.py:426
  22.6 4.2 %shard_map.70 = (bf16[2,384,256]{2,1,0:T(8,128)(2,1)S(1)}, bf16[2,384,256]{2,1,0:T(8,128)(2,1)S(1)}) custom-call(bf16[2,416,256]{2,1,0:T(8,128)(2,1)S(1)} %collective-permute-done.1.second, bf16[2,416,256]{2,1,0:T(8,128)(2,1)S(1)} %collective-permute-done.2.across.refs_6_, bf16[2,416,256]{2,1,0:T(8,128)(2,1)S(1)} %get-tuple-element.17.own.refs_7_), custom_call_target="tpu_custom_call" | custom-call | flops 5435817984 | bytes 4194304 | tf_op jit(solution)/shard_map/pallas_call | solution.py:435
  26.8 5.4 %collective-permute-done.3.first.refs_8_ = bf16[2,416,256]{2,1,0:T(8,128)(2,1)S(1)} collective-permute-done((bf16[2,416,256]{2,1,0:T(8,128)(2,1)S(1)}, bf16[2,416,256]{2,1,0:T(8,128)(2,1)S(1)}, u32[]{:S(2)}, u32[]{:S(2)}) %collective-permute-start.3) | collective-permute-done | bytes 426016 | tf_op jit(solution)/shard_map/ppermute | solution.py:427
  32.1 3.1 %shard_map.71 = (bf16[2,384,256]{2,1,0:T(8,128)(2,1)S(1)}, bf16[2,384,256]{2,1,0:T(8,128)(2,1)S(1)}) custom-call(bf16[2,416,256]{2,1,0:T(8,128)(2,1)S(1)} %collective-permute-done.2.across.refs_6_, bf16[2,416,256]{2,1,0:T(8,128)(2,1)S(1)} %get-tuple-element.17.own.refs_7_, bf16[2,416,256]{2,1,0:T(8,128)(2,1)S(1)} %collective-permute-done.3.first.refs_8_, ...), custom_call_target="tpu_custom_call" | custom-call | flops 4529848320 | bytes 4194304 | tf_op jit(solution)/shard_map/pallas_call | solution.py:435
  35.2 0.1 collective-permute-start.6
  35.3 0.5 collective-permute-start.5
  35.8 0.3 collective-permute-done.4.last
  36.1 0.0 copy-start.4
  36.1 2.7 %shard_map.72.refs_2_ = bf16[1,384,256]{2,1,0:T(8,128)(2,1)S(1)} custom-call(bf16[2,416,256]{2,1,0:T(8,128)(2,1)S(1)} %get-tuple-element.17.own.refs_7_, bf16[2,416,256]{2,1,0:T(8,128)(2,1)S(1)} %collective-permute-done.3.first.refs_8_, bf16[416,256]{1,0:T(8,128)(2,1)S(1)} %collective-permute-done.4.last, bf16[2,384,256]{2,1,0:T(8,128)(2,1)S(1)} %get-tuple-element.23.u_in), custom_call_target="tpu_custom_call" | custom-call | flops 2717908992 | bytes 4194304 | tf_op jit(solution)/shard_map/pallas_call | solution.py:435
  38.7 0.1 collective-permute-start.7
  38.8 1.4 %collective-permute-done.7.refs_5_ = bf16[1,384,256]{2,1,0:T(8,128)(2,1)S(1)} collective-permute-done((bf16[1,384,256]{2,1,0:T(8,128)(2,1)S(1)}, bf16[1,384,256]{2,1,0:T(8,128)(2,1)S(1)}, u32[]{:S(2)}, u32[]{:S(2)}) %collective-permute-start.7) | collective-permute-done | bytes 196640 | tf_op jit(solution)/shard_map/ppermute | solution.py:392
  40.3 0.0 collective-permute-done.6.refs_4_
  40.3 0.0 collective-permute-done.5.refs_3_
  40.3 0.0 copy-done.4
  40.3 4.1 %shard_map.73 = (f32[256,256]{1,0:T(8,128)S(1)}, bf16[256,256]{1,0:T(8,128)(2,1)S(1)}) custom-call(s32[2]{0:T(128)S(1)} %copy-done.4, bf16[2,384,256]{2,1,0:T(8,128)(2,1)S(1)} %get-tuple-element.19.refs_0_, bf16[2,384,256]{2,1,0:T(8,128)(2,1)S(1)} %get-tuple-element.21.refs_1_, bf16[1,384,256]{2,1,0:T(8,128)(2,1)S(1)} %shard_map.72.refs_2_, ...), custom_call_target="tpu_custom_call" | custom-call | tf_op jit(solution)/shard_map/pallas_call | solution.py:460
  44.4 0.0 copy-start
  44.4 1.7 %collective-permute-start.8 = (bf16[256,256]{1,0:T(8,128)(2,1)S(1)}, bf16[256,256]{1,0:T(8,128)(2,1)S(1)}, u32[]{:S(2)}, u32[]{:S(2)}) collective-permute-start(bf16[256,256]{1,0:T(8,128)(2,1)S(1)} %get-tuple-element.25), channel_id=1, source_target_pairs={{0,4},{1,5},{2,6},{3,7},{4,0},{5,1},{6,2},{7,3},{8,12},{9,13},{10,... | collective-permute-start | bytes 393224 | tf_op jit(solution)/shard_map/ppermute | solution.py:392
  46.1 3.9 %collective-permute-done.8 = bf16[256,256]{1,0:T(8,128)(2,1)S(1)} collective-permute-done((bf16[256,256]{1,0:T(8,128)(2,1)S(1)}, bf16[256,256]{1,0:T(8,128)(2,1)S(1)}, u32[]{:S(2)}, u32[]{:S(2)}) %collective-permute-start.8) | collective-permute-done | bytes 131104 | tf_op jit(solution)/shard_map/ppermute | solution.py:392
  50.0 4.3 %collective-permute-start.9 = (bf16[256,256]{1,0:T(8,128)(2,1)S(1)}, bf16[256,256]{1,0:T(8,128)(2,1)S(1)}, u32[]{:S(2)}, u32[]{:S(2)}) collective-permute-start(bf16[256,256]{1,0:T(8,128)(2,1)S(1)} %fusion), channel_id=1, source_target_pairs={{0,8},{1,9},{2,10},{3,11},{4,12},{5,13},{6,14},{7,15},{8,0},{9,1},... | collective-permute-start | bytes 393224 | tf_op jit(solution)/shard_map/ppermute | solution.py:392
  54.3 5.8 %collective-permute-done.9 = bf16[256,256]{1,0:T(8,128)(2,1)S(1)} collective-permute-done((bf16[256,256]{1,0:T(8,128)(2,1)S(1)}, bf16[256,256]{1,0:T(8,128)(2,1)S(1)}, u32[]{:S(2)}, u32[]{:S(2)}) %collective-permute-start.9) | collective-permute-done | bytes 131104 | tf_op jit(solution)/shard_map/ppermute | solution.py:392
  60.1 0.0 copy-start.3
  60.1 0.1 collective-permute-start.10
  60.2 0.0 collective-permute-start.11
  60.3 4.9 %collective-permute-done.10.s10 = bf16[256,256]{1,0:T(8,128)(2,1)S(1)} collective-permute-done((bf16[256,256]{1,0:T(8,128)(2,1)S(1)}, bf16[256,256]{1,0:T(8,128)(2,1)S(1)}, u32[]{:S(2)}, u32[]{:S(2)}) %collective-permute-start.10) | collective-permute-done | bytes 131104 | tf_op jit(solution)/shard_map/ppermute | solution.py:392
  65.1 0.0 collective-permute-start.12
  65.1 0.0 collective-permute-done.11.s01
  65.1 1.3 %collective-permute-done.12.s11 = bf16[256,256]{1,0:T(8,128)(2,1)S(1)} collective-permute-done((bf16[256,256]{1,0:T(8,128)(2,1)S(1)}, bf16[256,256]{1,0:T(8,128)(2,1)S(1)}, u32[]{:S(2)}, u32[]{:S(2)}) %collective-permute-start.12) | collective-permute-done | bytes 131104 | tf_op jit(solution)/shard_map/ppermute | solution.py:392
  66.5 0.0 copy-done
  66.5 0.0 copy-done.3
  66.5 4.2 %shard_map.74 = (f32[2,2,2,16,256]{4,3,2,1,0:T(8,128)}, bf16[4,2,256,256]{3,2,1,0:T(8,128)(2,1)}) custom-call(s32[2,4]{1,0:T(2,128)S(1)} %bitcast.3, bf16[256,256]{1,0:T(8,128)(2,1)S(1)} %add_convert_fusion.s00, bf16[256,256]{1,0:T(8,128)(2,1)S(1)} %collective-permute-done.10.s10, bf16[256,256]{1,0:T(8,128)(2,1)S(1)} %collective-permute-done.11.s01, ...), custom_call_target="tpu_custom_call" | custom-call | tf_op jit(solution)/shard_map/pallas_call | solution.py:486
  (2 shorter events, 0.1 us)
Async XLA Ops:
  0.6 1.1 %copy-start.1 = (bf16[2,2,3,1,128,256]{5,4,3,2,1,0:T(8,128)(2,1)S(1)}, bf16[2,2,3,1,128,256]{5,4,3,2,1,0:T(8,128)(2,1)}, u32[]{:S(2)}) copy-start(bf16[2,2,3,1,128,256]{5,4,3,2,1,0:T(8,128)(2,1)} %vectors.1) | copy-start | bytes 2359300
  1.8 0.7 %copy-start.2 = (bf16[2,3,2,3,3,1,128]{6,2,5,4,3,1,0:T(2,128)(2,1)S(1)}, bf16[2,3,2,3,3,1,128]{6,2,5,4,3,1,0:T(2,128)(2,1)}, u32[]{:S(2)}) copy-start(bf16[2,3,2,3,3,1,128]{6,2,5,4,3,1,0:T(2,128)(2,1)} %param.6) | copy-start | bytes 82948
  3.1 1.9 %collective-permute-start = (bf16[2,416,256]{2,1,0:T(8,128)(2,1)S(1)}, bf16[2,416,256]{2,1,0:T(8,128)(2,1)S(1)}, u32[]{:S(2)}, u32[]{:S(2)}) collective-permute-start(bf16[2,416,256]{2,1,0:T(8,128)(2,1)S(1)} %get-tuple-element.14), channel_id=1, source_target_pairs={{0,1},{1,0},{2,3},{3,2},{4,5},{5,4},{6,7},{7,6},{8,9},{9,8},{10,11... | collective-permute-start | bytes 1277960 | tf_op jit(solution)/shard_map/ppermute | solution.py:392
  5.8 13.1 %collective-permute-start.2 = (bf16[2,416,256]{2,1,0:T(8,128)(2,1)S(1)}, bf16[2,416,256]{2,1,0:T(8,128)(2,1)S(1)}, u32[]{:S(2)}, u32[]{:S(2)}) collective-permute-start(bf16[2,416,256]{2,1,0:T(8,128)(2,1)S(1)} %get-tuple-element.18), channel_id=1, source_target_pairs={{0,2},{1,3},{2,0},{3,1},{4,6},{5,7},{6,4},{7,5},{8,10},{9,11},{10,... | collective-permute-start | bytes 1277960 | tf_op jit(solution)/shard_map/ppermute | solution.py:392
  8.8 13.8 %collective-permute-start.1 = (bf16[2,416,256]{2,1,0:T(8,128)(2,1)S(1)}, bf16[2,416,256]{2,1,0:T(8,128)(2,1)S(1)}, u32[]{:S(2)}, u32[]{:S(2)}) collective-permute-start(bf16[2,416,256]{2,1,0:T(8,128)(2,1)S(1)} %get-tuple-element.17.own.refs_7_), channel_id=1, source_target_pairs={{2,6},{0,12},{3,7},{1,13},{6,10},{4,0},{7,11},{5,1},{10,14},{8,4},... | collective-permute-start | bytes 1277960 | tf_op jit(solution)/shard_map/ppermute | solution.py:426
  12.4 19.8 %collective-permute-start.3 = (bf16[2,416,256]{2,1,0:T(8,128)(2,1)S(1)}, bf16[2,416,256]{2,1,0:T(8,128)(2,1)S(1)}, u32[]{:S(2)}, u32[]{:S(2)}) collective-permute-start(bf16[2,416,256]{2,1,0:T(8,128)(2,1)S(1)} %get-tuple-element.18), channel_id=1, source_target_pairs={{2,4},{0,14},{3,5},{1,15},{6,8},{4,2},{7,9},{5,3},{10,12},{8,6},{1... | collective-permute-start | bytes 1277960 | tf_op jit(solution)/shard_map/ppermute | solution.py:427
  12.4 23.7 %collective-permute-start.4 = (bf16[416,256]{1,0:T(8,128)(2,1)S(1)}, bf16[416,256]{1,0:T(8,128)(2,1)S(1)}, u32[]{:S(2)}, u32[]{:S(2)}) collective-permute-start(bf16[416,256]{1,0:T(8,128)(2,1)S(1)} %get-tuple-element.22), channel_id=1, source_target_pairs={{0,4},{2,14},{1,5},{3,15},{4,8},{6,2},{5,9},{7,3},{8,12},{10,6},{9... | collective-permute-start | bytes 638984 | tf_op jit(solution)/shard_map/ppermute | solution.py:428
  35.2 5.0 %collective-permute-start.6 = (bf16[2,384,256]{2,1,0:T(8,128)(2,1)S(1)}, bf16[2,384,256]{2,1,0:T(8,128)(2,1)S(1)}, u32[]{:S(2)}, u32[]{:S(2)}) collective-permute-start(bf16[2,384,256]{2,1,0:T(8,128)(2,1)S(1)} %get-tuple-element.21.refs_1_), channel_id=1, source_target_pairs={{0,1},{1,0},{2,3},{3,2},{4,5},{5,4},{6,7},{7,6},{8,9},{9,8},{10,11... | collective-permute-start | bytes 1179656 | tf_op jit(solution)/shard_map/ppermute | solution.py:392
  35.3 4.9 %collective-permute-start.5 = (bf16[2,384,256]{2,1,0:T(8,128)(2,1)S(1)}, bf16[2,384,256]{2,1,0:T(8,128)(2,1)S(1)}, u32[]{:S(2)}, u32[]{:S(2)}) collective-permute-start(bf16[2,384,256]{2,1,0:T(8,128)(2,1)S(1)} %get-tuple-element.19.refs_0_), channel_id=1, source_target_pairs={{0,1},{1,0},{2,3},{3,2},{4,5},{5,4},{6,7},{7,6},{8,9},{9,8},{10,11... | collective-permute-start | bytes 1179656 | tf_op jit(solution)/shard_map/ppermute | solution.py:392
  36.1 4.2 %copy-start.4 = (s32[2]{0:T(128)S(1)}, s32[2]{0:T(128)}, u32[]{:S(2)}) copy-start(s32[2]{0:T(128)} %directions.1) | copy-start | bytes 28
  38.7 1.5 %collective-permute-start.7 = (bf16[1,384,256]{2,1,0:T(8,128)(2,1)S(1)}, bf16[1,384,256]{2,1,0:T(8,128)(2,1)S(1)}, u32[]{:S(2)}, u32[]{:S(2)}) collective-permute-start(bf16[1,384,256]{2,1,0:T(8,128)(2,1)S(1)} %shard_map.72.refs_2_), channel_id=1, source_target_pairs={{0,1},{1,0},{2,3},{3,2},{4,5},{5,4},{6,7},{7,6},{8,9},{9,8},{10,11... | collective-permute-start | bytes 589832 | tf_op jit(solution)/shard_map/ppermute | solution.py:392
  44.4 22.1 %copy-start = (bf16[4,2,256,256]{3,2,1,0:T(8,128)(2,1)S(1)}, bf16[4,2,256,256]{3,2,1,0:T(8,128)(2,1)}, u32[]{:S(2)}) copy-start(bf16[4,2,256,256]{3,2,1,0:T(8,128)(2,1)} %perambulators.1) | copy-start | bytes 3145732
  44.4 5.6 %collective-permute-start.8 = (bf16[256,256]{1,0:T(8,128)(2,1)S(1)}, bf16[256,256]{1,0:T(8,128)(2,1)S(1)}, u32[]{:S(2)}, u32[]{:S(2)}) collective-permute-start(bf16[256,256]{1,0:T(8,128)(2,1)S(1)} %get-tuple-element.25), channel_id=1, source_target_pairs={{0,4},{1,5},{2,6},{3,7},{4,0},{5,1},{6,2},{7,3},{8,12},{9,13},{10,... | collective-permute-start | bytes 393224 | tf_op jit(solution)/shard_map/ppermute | solution.py:392
  50.0 10.0 %collective-permute-start.9 = (bf16[256,256]{1,0:T(8,128)(2,1)S(1)}, bf16[256,256]{1,0:T(8,128)(2,1)S(1)}, u32[]{:S(2)}, u32[]{:S(2)}) collective-permute-start(bf16[256,256]{1,0:T(8,128)(2,1)S(1)} %fusion), channel_id=1, source_target_pairs={{0,8},{1,9},{2,10},{3,11},{4,12},{5,13},{6,14},{7,15},{8,0},{9,1},... | collective-permute-start | bytes 393224 | tf_op jit(solution)/shard_map/ppermute | solution.py:392
  60.1 6.4 %copy-start.3 = (s32[4,2]{0,1:T(2,128)S(1)}, s32[4,2]{0,1:T(2,128)}, u32[]{:S(2)}) copy-start(s32[4,2]{0,1:T(2,128)} %param.8) | copy-start | bytes 100
  60.1 5.0 %collective-permute-start.10 = (bf16[256,256]{1,0:T(8,128)(2,1)S(1)}, bf16[256,256]{1,0:T(8,128)(2,1)S(1)}, u32[]{:S(2)}, u32[]{:S(2)}) collective-permute-start(bf16[256,256]{1,0:T(8,128)(2,1)S(1)} %add_convert_fusion.s00), channel_id=1, source_target_pairs={{0,2},{1,3},{2,0},{3,1},{4,6},{5,7},{6,4},{7,5},{8,10},{9,11},{10,... | collective-permute-start | bytes 393224 | tf_op jit(solution)/shard_map/ppermute | solution.py:392
  60.2 4.9 %collective-permute-start.11 = (bf16[256,256]{1,0:T(8,128)(2,1)S(1)}, bf16[256,256]{1,0:T(8,128)(2,1)S(1)}, u32[]{:S(2)}, u32[]{:S(2)}) collective-permute-start(bf16[256,256]{1,0:T(8,128)(2,1)S(1)} %add_convert_fusion.s00), channel_id=1, source_target_pairs={{0,1},{1,0},{2,3},{3,2},{4,5},{5,4},{6,7},{7,6},{8,9},{9,8},{10,11... | collective-permute-start | bytes 393224 | tf_op jit(solution)/shard_map/ppermute | solution.py:392
  65.1 1.3 %collective-permute-start.12 = (bf16[256,256]{1,0:T(8,128)(2,1)S(1)}, bf16[256,256]{1,0:T(8,128)(2,1)S(1)}, u32[]{:S(2)}, u32[]{:S(2)}) collective-permute-start(bf16[256,256]{1,0:T(8,128)(2,1)S(1)} %collective-permute-done.10.s10), channel_id=1, source_target_pairs={{0,1},{1,0},{2,3},{3,2},{4,5},{5,4},{6,7},{7,6},{8,9},{9,8},{10,11... | collective-permute-start | bytes 393224 | tf_op jit(solution)/shard_map/ppermute | solution.py:392

commit v4 on v3

--- a/solution.py
+++ b/solution.py
@@ -37,9 +37,11 @@
     return core + (1 - 2 * core) * ((1 - chip) if t == 0 else chip)
 
 
-def split_kernel(vectors, links, own, other, send, packed, sems):
+def split_kernel(vectors, links_in, own, other, send, links, packed, sems):
     core, chip = position()
     half = vectors.shape[5] // 2
+    arriving = pltpu.make_async_copy(links_in, links, sems.at[28])
+    arriving.start()
     copies = []
     for t in range(2):
         for part in range(2):
@@ -56,6 +58,7 @@
                 ):
                     copies.append(pltpu.make_async_copy(source, target, sems.at[len(copies)]))
                     copies[-1].start()
+    arriving.wait()
     for t in range(2):
         table = links.at[chip + t * (1 - 2 * chip)]
         gathered = [
@@ -87,11 +90,14 @@
     ]
     for copy in copies:
         copy.start()
+    here = slot_of(core, chip, 0) == 0
+    kept_edge = pltpu.make_async_copy(own_in.at[0], edge, sems.at[2])
+    received_edge = pltpu.make_async_copy(received.at[0], edge, sems.at[2])
+    pl.when(here)(kept_edge.start)
+    pl.when(jnp.logical_not(here))(received_edge.start)
     for copy in copies:
         copy.wait()
-    copy = pltpu.make_async_copy(own.at[0], edge, sems.at[2])
-    copy.start()
-    copy.wait()
+    kept_edge.wait()
 
 
 def shift_y(row, lane):
@@ -236,30 +242,28 @@
     w_out[0] = smeared(operators.at[0], grown, 1)
 
 
-def elemental_kernel(scale, directions, *refs):
-    mine, theirs, (across, own, first) = refs[:3], refs[3:6], refs[6:9]
-    out, out_low, w, rims, right, sems = refs[9:]
+def elemental_kernel(scale, vector_pieces, link_pieces, directions, *refs):
+    groups = max(piece[0] for piece in vector_pieces) + 1
+    packages = max(piece[0] for piece in link_pieces) + 1
+    mine, theirs, refs = refs[:groups], refs[groups : 2 * groups], refs[2 * groups :]
+    packages, refs = refs[:packages], refs[packages:]
+    *sums, w, rims, right, sems = refs
     core, chip = position()
     half = SITES
-    copies = [
-        (links_of(across), rims.at[pl.ds(0, 2)]),
-        (links_of(own), rims.at[pl.ds(2, 2)]),
-        (first.at[0, pl.ds(FIELD, PACKED_LINKS)], rims.at[4]),
-    ]
+    copies = []
+    at = 0
+    for k, first, count in link_pieces:
+        copies.append((links_of(packages[k].at[pl.ds(first, count)]), rims.at[pl.ds(at, count)]))
+        at += count
     for group, side in ((mine, core), (theirs, 1 - core)):
+        lanes = pl.ds(pl.multiple_of(side * half, half), half)
         at = 0
-        for ref in group:
-            count = ref.shape[0]
+        for k, first, count in vector_pieces:
             for part in range(2):
                 copies.append(
                     (
-                        ref.at[:, :, pl.ds(part * half, half)],
-                        w.at[
-                            pl.ds(at, count),
-                            part,
-                            :,
-                            pl.ds(pl.multiple_of(side * half, half), half),
-                        ],
+                        group[k].at[pl.ds(first, count), :, pl.ds(part * half, half)],
+                        w.at[pl.ds(at, count), part, :, lanes],
                     )
                 )
             at += count
@@ -319,6 +323,11 @@
         (((0,), (0,)), ((), ())),
         preferred_element_type=f32,
     )
+    if scale is None:
+        sums[-1][...] = product if len(sums) == 1 else product + sums[0][...]
+        return
+    before, out, out_low = sums
+    product = product + before[...]
     packed = (product[:, :vectors] + product[:, vectors:].T) * scale
     out[...] = packed
     out_low[...] = packed.astype(bf16)
@@ -385,7 +394,9 @@
     blocks = n // 4
     vmem = whole_in_vmem()
     anywhere = pl.BlockSpec(memory_space=pl.ANY)
+    hbm = pl.BlockSpec(memory_space=pltpu.HBM)
     smem = pl.BlockSpec(memory_space=pltpu.SMEM)
+    table = jnp.transpose(links, (0, 1, 3, 4, 5, 2, 6))
     rows = FIELD + PACKED_LINKS
 
     def swap(value, bit):
@@ -395,14 +406,15 @@
     own, other, send = pl.pallas_call(
         split_kernel,
         out_shape=(package, package, package),
-        in_specs=[anywhere, vmem],
+        in_specs=[hbm, hbm],
         out_specs=(anywhere, anywhere, anywhere),
         scratch_shapes=[
+            pltpu.VMEM(table.shape, bf16),
             pltpu.VMEM((2, PACKED_LINKS, 2 * SITES), bf16),
-            pltpu.SemaphoreType.DMA((28,)),
+            pltpu.SemaphoreType.DMA((29,)),
         ],
         compiler_params=params(8),
-    )(eigvecs, jnp.transpose(links, (0, 1, 3, 4, 5, 2, 6)))
+    )(eigvecs, table)
     received = swap(send, 1)
     own, other, edge = pl.pallas_call(
         join_kernel,
@@ -446,36 +458,64 @@
             ],
             compiler_params=params(20),
             cost_estimate=pl.CostEstimate(
-                flops=4 * products, bytes_accessed=4 * 1024 * 1024, transcendentals=0
+                flops=1024, bytes_accessed=1024, transcendentals=0
             ),
         )(*operands)
 
-    w_inner, u_inner = smear(smear_inner, (second, across, own), 6, 6, 4, 4, (2, 2))
-    w_middle, u_middle = smear(smear_middle, (across, own, first, u_inner), 4, 5, 4, 3, (2, 2))
-    (w_outer,) = smear(smear_outer, (own, first, last, u_middle), 3, 4, 3, 2, (1,))
-    mine = (w_inner, w_middle, w_outer)
-    theirs = tuple(swap(part, 1) for part in mine)
     site_scale = (6.0 * n * SITES) ** (-0.5)
     square = (vector_count, vector_count)
-    partial, partial_low = pl.pallas_call(
-        functools.partial(elemental_kernel, site_scale),
-        out_shape=(jax.ShapeDtypeStruct(square, f32), jax.ShapeDtypeStruct(square, bf16)),
-        in_specs=[smem] + [anywhere] * 9,
-        out_specs=(vmem, vmem),
-        scratch_shapes=[
-            pltpu.VMEM((5, 2, FIELD, vector_count), bf16),
-            pltpu.VMEM((5, PACKED_LINKS, 2 * SITES), bf16),
-            pltpu.VMEM((4, 2, FIELD, 2 * vector_count), bf16),
-            pltpu.SemaphoreType.DMA((15,)),
-        ],
-        compiler_params=params(16),
-    )(directions, *mine, *theirs, across, own, first)
-
-    bit = 4
-    while bit < n:
-        partial = partial + swap(partial_low, bit).astype(f32)
+    running = jax.ShapeDtypeStruct((vector_count, 2 * vector_count), f32)
+
+    def elemental(scale, groups, vector_pieces, packages, link_pieces, sums):
+        ranks = sum(piece[2] for piece in vector_pieces)
+        outputs = (running,)
+        if scale is not None:
+            outputs = (jax.ShapeDtypeStruct(square, f32), jax.ShapeDtypeStruct(square, bf16))
+        operands = [part[0] for part in groups] + [part[1] for part in groups] + list(packages)
+        products = (ranks - 1) * 4 * FIELD * vector_count * (FIELD + 2 * vector_count)
+        return pl.pallas_call(
+            functools.partial(elemental_kernel, scale, vector_pieces, link_pieces),
+            out_shape=outputs,
+            in_specs=[smem] + [anywhere] * len(operands) + [vmem] * len(sums),
+            out_specs=(vmem,) * len(outputs),
+            scratch_shapes=[
+                pltpu.VMEM((ranks, 2, FIELD, vector_count), bf16),
+                pltpu.VMEM((ranks, PACKED_LINKS, 2 * SITES), bf16),
+                pltpu.VMEM((ranks - 1, 2, FIELD, 2 * vector_count), bf16),
+                pltpu.SemaphoreType.DMA((4 * len(vector_pieces) + len(link_pieces),)),
+            ],
+            compiler_params=params(16),
+            cost_estimate=pl.CostEstimate(
+                flops=1024, bytes_accessed=1024, transcendentals=0
+            ),
+        )(directions, *operands, *sums)
+
+    def with_partner(part):
+        return part, swap(part, 1)
+
+    w_inner, u_inner = smear(smear_inner, (second, across, own), 6, 6, 4, 4, (2, 2))
+    inner = with_partner(w_inner)
+    (sum_inner,) = elemental(None, (inner,), ((0, 0, 2),), (across,), ((0, 0, 2),), ())
+    u_inner, sum_inner = lax.optimization_barrier((u_inner, sum_inner))
+    w_middle, u_middle = smear(smear_middle, (across, own, first, u_inner), 4, 5, 4, 3, (2, 2))
+    middle = with_partner(w_middle)
+    (w_outer,) = smear(smear_outer, (own, first, last, u_middle), 3, 4, 3, 2, (1,))
+    outer_part = with_partner(w_outer)
+    partial, partial_low = elemental(
+        site_scale,
+        (inner, middle, outer_part),
+        ((0, 1, 1), (1, 0, 2), (2, 0, 1)),
+        (across, own, first),
+        ((0, 1, 1), (1, 0, 2), (2, 0, 1)),
+        (sum_inner,),
+    )
+
+    bit = n // 2
+    while bit >= 4:
+        partner = bit if bit == 4 else bit + bit // 2
+        partial = partial + swap(partial_low, partner).astype(f32)
         partial_low = partial.astype(bf16)
-        bit *= 2
+        bit //= 2
     other_slice = swap(partial_low, 2)
     other_copy = swap(partial_low, 1)
     other_both = swap(other_slice, 1)

time: 70.9 us -> 68.7 us (0.969)
  waiting for transfers between devices: 34.6 us -> 31.3 us
  Pallas kernels: 19.5 us -> 21.6 us
  starting transfers between devices: 13.8 us -> 12.9 us
    ppermute x1, waiting for transfers between devices: 5.36 us -> 1.08 us  [body(): first = lax.ppermute(other, 'space', crossing)]
    pallas_call x1 -> x2, Pallas kernels: 4.08 us -> 6.14 us  [elemental(): pl.pallas_call(functools.partial(elemental_kernel, scale, vector_pieces,...]
    ppermute x1, waiting for transfers between devices: 0.26 us -> 2.14 us  [body(): last = lax.ppermute(edge, 'space', outer)]
    ppermute x10, starting transfers between devices: 10.2 us -> 8.58 us  [swap(): return lax.ppermute(value, 'space', [(i, i ^ bit) for i in range(n)])]
    ppermute x10, waiting for transfers between devices: 25.3 us -> 24.4 us  [swap(): return lax.ppermute(value, 'space', [(i, i ^ bit) for i in range(n)])]
  transfers between devices with their start and end apart: 13 -> 13, of which waited for: 10 -> 11; matrix products, arithmetic and copies ran while one was open for 0% -> 0% of each run, Pallas kernels for 14% -> 17%
where the time goes in v4:
time: 68.7 us; the launch traced here: 68.5 us
  waiting for transfers between devices  31.3 us (46%)
  Pallas kernels  21.6 us (31%)
  starting transfers between devices  12.9 us (19%)
  local copies, waits for them, and re-layouts  1.89 us (3%)
  between operations  0.76 us (1%)
    ppermute x10, waiting for transfers between devices, swap(): return lax.ppermute(value, 'space', [(i, i ^ bit) for i in range(n)])  24.4 us
    pallas_call x3, Pallas kernels, smear(): pl.pallas_call(kernel, out_shape=tuple((shape(count) for count in outputs...  9.91 us
    ppermute x10, starting transfers between devices, swap(): return lax.ppermute(value, 'space', [(i, i ^ bit) for i in range(n)])  8.58 us
    pallas_call x2, Pallas kernels, elemental(): pl.pallas_call(functools.partial(elemental_kernel, scale, vector_pieces,...  6.14 us
    pallas_call x1, Pallas kernels, body(): pl.pallas_call(functools.partial(pair_kernel, pair_scale), out_shape=(jax...  4.16 us
    ppermute x1, waiting for transfers between devices, body(): second = lax.ppermute(own, 'space', straight)  3.71 us
    ppermute x1, starting transfers between devices, body(): second = lax.ppermute(own, 'space', straight)  3.6 us
    ppermute x1, waiting for transfers between devices, body(): last = lax.ppermute(edge, 'space', outer)  2.14 us
  transfers between devices with their start and end apart: 13, of which 11 were waited for; matrix products, arithmetic and copies ran while one was open for 0% of the time, Pallas kernels for 17%

profile of v4, /device:TPU:0, one launch (start us, length us, event | category | flops | bytes accessed | tf_op | source)
XLA Modules:
  0.0 68.5 jit_solution(1999633794712281314)
XLA Ops:
  0.6 0.0 copy-start.1
  0.6 1.1 %copy-done.1 = bf16[2,2,3,1,128,256]{5,4,3,2,1,0:T(8,128)(2,1)S(1)} copy-done((bf16[2,2,3,1,128,256]{5,4,3,2,1,0:T(8,128)(2,1)S(1)}, bf16[2,2,3,1,128,256]{5,4,3,2,1,0:T(8,128)(2,1)}, u32[]{:S(2)}) %copy-start.1) | copy-done | bytes 786456
  1.8 0.0 copy-start.2
  1.8 0.7 %copy-done.2 = bf16[2,3,2,3,3,1,128]{6,2,5,4,3,1,0:T(2,128)(2,1)S(1)} copy-done((bf16[2,3,2,3,3,1,128]{6,2,5,4,3,1,0:T(2,128)(2,1)S(1)}, bf16[2,3,2,3,3,1,128]{6,2,5,4,3,1,0:T(2,128)(2,1)}, u32[]{:S(2)}) %copy-start.2) | copy-done | bytes 27672
  2.5 0.6 shard_map.68
  3.1 0.5 collective-permute-start
  3.6 1.4 %collective-permute-done.received = bf16[2,416,256]{2,1,0:T(8,128)(2,1)S(1)} collective-permute-done((bf16[2,416,256]{2,1,0:T(8,128)(2,1)S(1)}, bf16[2,416,256]{2,1,0:T(8,128)(2,1)S(1)}, u32[]{:S(2)}, u32[]{:S(2)}) %collective-permute-start) | collective-permute-done | bytes 426016 | tf_op jit(solution)/shard_map/ppermute | solution.py:403
  5.0 0.8 %shard_map.69 = (bf16[2,416,256]{2,1,0:T(8,128)(2,1)S(1)}, bf16[2,416,256]{2,1,0:T(8,128)(2,1)S(1)}, bf16[416,256]{1,0:T(8,128)(2,1)S(1)}) custom-call(bf16[2,416,256]{2,1,0:T(8,128)(2,1)S(1)} %collective-permute-done.received, bf16[2,416,256]{2,1,0:T(8,128)(2,1)S(1)} %get-tuple-element.17.own_in, ...), custom_call_target="tpu_custom_call", output_to_operand_aliasing={{0}: (1, {}), {1}: (2, {})} | custom-call | tf_op jit(solution)/shard_map/pallas_call | solution.py:419
  5.9 3.0 %collective-permute-start.2 = (bf16[2,416,256]{2,1,0:T(8,128)(2,1)S(1)}, bf16[2,416,256]{2,1,0:T(8,128)(2,1)S(1)}, u32[]{:S(2)}, u32[]{:S(2)}) collective-permute-start(bf16[2,416,256]{2,1,0:T(8,128)(2,1)S(1)} %get-tuple-element.20), channel_id=1, source_target_pairs={{0,2},{1,3},{2,0},{3,1},{4,6},{5,7},{6,4},{7,5},{8,10},{9,11},{10,... | collective-permute-start | bytes 1277960 | tf_op jit(solution)/shard_map/ppermute | solution.py:403
  8.8 3.6 %collective-permute-start.1 = (bf16[2,416,256]{2,1,0:T(8,128)(2,1)S(1)}, bf16[2,416,256]{2,1,0:T(8,128)(2,1)S(1)}, u32[]{:S(2)}, u32[]{:S(2)}) collective-permute-start(bf16[2,416,256]{2,1,0:T(8,128)(2,1)S(1)} %get-tuple-element.19.own.refs_7_), channel_id=1, source_target_pairs={{2,6},{0,12},{3,7},{1,13},{6,10},{4,0},{7,11},{5,1},{10,14},{8,4},... | collective-permute-start | bytes 1277960 | tf_op jit(solution)/shard_map/ppermute | solution.py:438
  12.4 0.0 collective-permute-start.3
  12.4 6.5 %collective-permute-done.2.across.refs_2_.refs_6_ = bf16[2,416,256]{2,1,0:T(8,128)(2,1)S(1)} collective-permute-done((bf16[2,416,256]{2,1,0:T(8,128)(2,1)S(1)}, bf16[2,416,256]{2,1,0:T(8,128)(2,1)S(1)}, u32[]{:S(2)}, u32[]{:S(2)}) %collective-permute-start.2) | collective-permute-done | bytes 426016 | tf_op jit(solution)/shard_map/ppermute | solution.py:403
  18.9 3.7 %collective-permute-done.1.second = bf16[2,416,256]{2,1,0:T(8,128)(2,1)S(1)} collective-permute-done((bf16[2,416,256]{2,1,0:T(8,128)(2,1)S(1)}, bf16[2,416,256]{2,1,0:T(8,128)(2,1)S(1)}, u32[]{:S(2)}, u32[]{:S(2)}) %collective-permute-start.1) | collective-permute-done | bytes 426016 | tf_op jit(solution)/shard_map/ppermute | solution.py:438
  22.6 4.2 %shard_map.70 = (bf16[2,384,256]{2,1,0:T(8,128)(2,1)S(1)}, bf16[2,384,256]{2,1,0:T(8,128)(2,1)S(1)}) custom-call(bf16[2,416,256]{2,1,0:T(8,128)(2,1)S(1)} %collective-permute-done.1.second, bf16[2,416,256]{2,1,0:T(8,128)(2,1)S(1)} %collective-permute-done.2.across.refs_2_.refs_6_, bf16[2,416,256]{2,1,0:T(8,128)(2,1)S(1)} %get-tuple-element.19.own.refs_7_), custom_call_target="tpu_custom_call" | custom-call | flops 1024 | bytes 1024 | tf_op jit(solution)/shard_map/pallas_call | solution.py:447
  26.8 0.0 copy-start.3
  26.8 0.1 collective-permute-start.4
  26.9 0.7 %collective-permute-start.5 = (bf16[416,256]{1,0:T(8,128)(2,1)S(1)}, bf16[416,256]{1,0:T(8,128)(2,1)S(1)}, u32[]{:S(2)}, u32[]{:S(2)}) collective-permute-start(bf16[416,256]{1,0:T(8,128)(2,1)S(1)} %get-tuple-element.25), channel_id=1, source_target_pairs={{0,4},{2,14},{1,5},{3,15},{4,8},{6,2},{5,9},{7,3},{8,12},{10,6},{9... | collective-permute-start | bytes 638984 | tf_op jit(solution)/shard_map/ppermute | solution.py:440
  27.6 1.0 %collective-permute-done.4.refs_1_.refs_3_ = bf16[2,384,256]{2,1,0:T(8,128)(2,1)S(1)} collective-permute-done((bf16[2,384,256]{2,1,0:T(8,128)(2,1)S(1)}, bf16[2,384,256]{2,1,0:T(8,128)(2,1)S(1)}, u32[]{:S(2)}, u32[]{:S(2)}) %collective-permute-start.4) | collective-permute-done | bytes 393248 | tf_op jit(solution)/shard_map/ppermute | solution.py:403
  28.6 0.0 copy-done.3
  28.6 2.1 %shard_map.71.refs_9_ = f32[256,512]{1,0:T(8,128)S(1)} custom-call(s32[2]{0:T(128)S(1)} %copy-done.3, bf16[2,384,256]{2,1,0:T(8,128)(2,1)S(1)} %get-tuple-element.21.refs_0_, bf16[2,384,256]{2,1,0:T(8,128)(2,1)S(1)} %collective-permute-done.4.refs_1_.refs_3_, bf16[2,416,256]{2,1,0:T(8,128)(2,1)S(1)} %collective-permute-done.2.across.refs_2_.refs_6_), custom_call_target="tpu_custom_call" | custom-call | flops 1024 | bytes 1024 | tf_op jit(solution)/shard_map/pallas_call | solution.py:476
  30.7 1.1 %collective-permute-done.3.first.refs_8_ = bf16[2,416,256]{2,1,0:T(8,128)(2,1)S(1)} collective-permute-done((bf16[2,416,256]{2,1,0:T(8,128)(2,1)S(1)}, bf16[2,416,256]{2,1,0:T(8,128)(2,1)S(1)}, u32[]{:S(2)}, u32[]{:S(2)}) %collective-permute-start.3) | collective-permute-done | bytes 426016 | tf_op jit(solution)/shard_map/ppermute | solution.py:439
  31.8 3.1 %shard_map.72 = (bf16[2,384,256]{2,1,0:T(8,128)(2,1)S(1)}, bf16[2,384,256]{2,1,0:T(8,128)(2,1)S(1)}) custom-call(bf16[2,416,256]{2,1,0:T(8,128)(2,1)S(1)} %collective-permute-done.2.across.refs_2_.refs_6_, bf16[2,416,256]{2,1,0:T(8,128)(2,1)S(1)} %get-tuple-element.19.own.refs_7_, bf16[2,416,256]{2,1,0:T(8,128)(2,1)S(1)} %collective-permute-done.3.first.refs_8_, ...), custom_call_target="tpu_custom_call" | custom-call | flops 1024 | bytes 1024 | tf_op jit(solution)/shard_map/pallas_call | solution.py:447
  34.9 0.1 collective-permute-start.6
  34.9 2.1 %collective-permute-done.5.last = bf16[416,256]{1,0:T(8,128)(2,1)S(1)} collective-permute-done((bf16[416,256]{1,0:T(8,128)(2,1)S(1)}, bf16[416,256]{1,0:T(8,128)(2,1)S(1)}, u32[]{:S(2)}, u32[]{:S(2)}) %collective-permute-start.5) | collective-permute-done | bytes 213024 | tf_op jit(solution)/shard_map/ppermute | solution.py:440
  37.1 2.7 %shard_map.73.refs_2_ = bf16[1,384,256]{2,1,0:T(8,128)(2,1)S(1)} custom-call(bf16[2,416,256]{2,1,0:T(8,128)(2,1)S(1)} %get-tuple-element.19.own.refs_7_, bf16[2,416,256]{2,1,0:T(8,128)(2,1)S(1)} %collective-permute-done.3.first.refs_8_, bf16[416,256]{1,0:T(8,128)(2,1)S(1)} %collective-permute-done.5.last, bf16[2,384,256]{2,1,0:T(8,128)(2,1)S(1)} %get-tuple-element.26.u_in), custom_call_target="tpu_custom_call" | custom-call | flops 1024 | bytes 1024 | tf_op jit(solution)/shard_map/pallas_call | solution.py:447
  39.8 0.1 collective-permute-start.7
  39.8 1.4 %collective-permute-done.7.refs_5_ = bf16[1,384,256]{2,1,0:T(8,128)(2,1)S(1)} collective-permute-done((bf16[1,384,256]{2,1,0:T(8,128)(2,1)S(1)}, bf16[1,384,256]{2,1,0:T(8,128)(2,1)S(1)}, u32[]{:S(2)}, u32[]{:S(2)}) %collective-permute-start.7) | collective-permute-done | bytes 196640 | tf_op jit(solution)/shard_map/ppermute | solution.py:403
  41.3 0.0 collective-permute-done.6.refs_4_
  41.3 4.1 %shard_map.74 = (f32[256,256]{1,0:T(8,128)S(1)}, bf16[256,256]{1,0:T(8,128)(2,1)S(1)}) custom-call(s32[2]{0:T(128)S(1)} %copy-done.3, bf16[2,384,256]{2,1,0:T(8,128)(2,1)S(1)} %get-tuple-element.21.refs_0_, bf16[2,384,256]{2,1,0:T(8,128)(2,1)S(1)} %get-tuple-element.24.refs_1_, bf16[1,384,256]{2,1,0:T(8,128)(2,1)S(1)} %shard_map.73.refs_2_, ...), custom_call_target="tpu_custom_call" | custom-call | flops 1024 | bytes 1024 | tf_op jit(solution)/shard_map/pallas_call | solution.py:476
  45.3 0.0 copy-start
  45.3 2.7 %collective-permute-start.8 = (bf16[256,256]{1,0:T(8,128)(2,1)S(1)}, bf16[256,256]{1,0:T(8,128)(2,1)S(1)}, u32[]{:S(2)}, u32[]{:S(2)}) collective-permute-start(bf16[256,256]{1,0:T(8,128)(2,1)S(1)} %get-tuple-element.29), channel_id=1, source_target_pairs={{0,12},{1,13},{2,14},{3,15},{4,8},{5,9},{6,10},{7,11},{8,4},{9,5},... | collective-permute-start | bytes 393224 | tf_op jit(solution)/shard_map/ppermute | solution.py:403
  48.0 4.8 %collective-permute-done.8 = bf16[256,256]{1,0:T(8,128)(2,1)S(1)} collective-permute-done((bf16[256,256]{1,0:T(8,128)(2,1)S(1)}, bf16[256,256]{1,0:T(8,128)(2,1)S(1)}, u32[]{:S(2)}, u32[]{:S(2)}) %collective-permute-start.8) | collective-permute-done | bytes 131104 | tf_op jit(solution)/shard_map/ppermute | solution.py:403
  52.9 1.6 %collective-permute-start.9 = (bf16[256,256]{1,0:T(8,128)(2,1)S(1)}, bf16[256,256]{1,0:T(8,128)(2,1)S(1)}, u32[]{:S(2)}, u32[]{:S(2)}) collective-permute-start(bf16[256,256]{1,0:T(8,128)(2,1)S(1)} %fusion), channel_id=1, source_target_pairs={{0,4},{1,5},{2,6},{3,7},{4,0},{5,1},{6,2},{7,3},{8,12},{9,13},{10,... | collective-permute-start | bytes 393224 | tf_op jit(solution)/shard_map/ppermute | solution.py:403
  54.5 3.5 %collective-permute-done.9 = bf16[256,256]{1,0:T(8,128)(2,1)S(1)} collective-permute-done((bf16[256,256]{1,0:T(8,128)(2,1)S(1)}, bf16[256,256]{1,0:T(8,128)(2,1)S(1)}, u32[]{:S(2)}, u32[]{:S(2)}) %collective-permute-start.9) | collective-permute-done | bytes 131104 | tf_op jit(solution)/shard_map/ppermute | solution.py:403
  58.0 0.0 copy-start.4
  58.0 0.6 collective-permute-start.10
  58.6 0.0 collective-permute-start.11
  58.6 4.4 %collective-permute-done.10.s10 = bf16[256,256]{1,0:T(8,128)(2,1)S(1)} collective-permute-done((bf16[256,256]{1,0:T(8,128)(2,1)S(1)}, bf16[256,256]{1,0:T(8,128)(2,1)S(1)}, u32[]{:S(2)}, u32[]{:S(2)}) %collective-permute-start.10) | collective-permute-done | bytes 131104 | tf_op jit(solution)/shard_map/ppermute | solution.py:403
  63.0 0.0 collective-permute-start.12
  63.0 0.0 collective-permute-done.11.s01
  63.0 1.3 %collective-permute-done.12.s11 = bf16[256,256]{1,0:T(8,128)(2,1)S(1)} collective-permute-done((bf16[256,256]{1,0:T(8,128)(2,1)S(1)}, bf16[256,256]{1,0:T(8,128)(2,1)S(1)}, u32[]{:S(2)}, u32[]{:S(2)}) %collective-permute-start.12) | collective-permute-done | bytes 131104 | tf_op jit(solution)/shard_map/ppermute | solution.py:403
  64.4 0.0 copy-done
  64.4 0.0 copy-done.4
  64.4 4.2 %shard_map.75 = (f32[2,2,2,16,256]{4,3,2,1,0:T(8,128)}, bf16[4,2,256,256]{3,2,1,0:T(8,128)(2,1)}) custom-call(s32[2,4]{1,0:T(2,128)S(1)} %bitcast.3, bf16[256,256]{1,0:T(8,128)(2,1)S(1)} %add_convert_fusion.s00, bf16[256,256]{1,0:T(8,128)(2,1)S(1)} %collective-permute-done.10.s10, bf16[256,256]{1,0:T(8,128)(2,1)S(1)} %collective-permute-done.11.s01, ...), custom_call_target="tpu_custom_call" | custom-call | tf_op jit(solution)/shard_map/pallas_call | solution.py:526
  (2 shorter events, 0.1 us)
Async XLA Ops:
  0.6 1.1 %copy-start.1 = (bf16[2,2,3,1,128,256]{5,4,3,2,1,0:T(8,128)(2,1)S(1)}, bf16[2,2,3,1,128,256]{5,4,3,2,1,0:T(8,128)(2,1)}, u32[]{:S(2)}) copy-start(bf16[2,2,3,1,128,256]{5,4,3,2,1,0:T(8,128)(2,1)} %vectors.1) | copy-start | bytes 2359300
  1.8 0.7 %copy-start.2 = (bf16[2,3,2,3,3,1,128]{6,2,5,4,3,1,0:T(2,128)(2,1)S(1)}, bf16[2,3,2,3,3,1,128]{6,2,5,4,3,1,0:T(2,128)(2,1)}, u32[]{:S(2)}) copy-start(bf16[2,3,2,3,3,1,128]{6,2,5,4,3,1,0:T(2,128)(2,1)} %param.6) | copy-start | bytes 82948
  3.1 1.9 %collective-permute-start = (bf16[2,416,256]{2,1,0:T(8,128)(2,1)S(1)}, bf16[2,416,256]{2,1,0:T(8,128)(2,1)S(1)}, u32[]{:S(2)}, u32[]{:S(2)}) collective-permute-start(bf16[2,416,256]{2,1,0:T(8,128)(2,1)S(1)} %get-tuple-element.16), channel_id=1, source_target_pairs={{0,1},{1,0},{2,3},{3,2},{4,5},{5,4},{6,7},{7,6},{8,9},{9,8},{10,11... | collective-permute-start | bytes 1277960 | tf_op jit(solution)/shard_map/ppermute | solution.py:403
  5.9 13.1 %collective-permute-start.2 = (bf16[2,416,256]{2,1,0:T(8,128)(2,1)S(1)}, bf16[2,416,256]{2,1,0:T(8,128)(2,1)S(1)}, u32[]{:S(2)}, u32[]{:S(2)}) collective-permute-start(bf16[2,416,256]{2,1,0:T(8,128)(2,1)S(1)} %get-tuple-element.20), channel_id=1, source_target_pairs={{0,2},{1,3},{2,0},{3,1},{4,6},{5,7},{6,4},{7,5},{8,10},{9,11},{10,... | collective-permute-start | bytes 1277960 | tf_op jit(solution)/shard_map/ppermute | solution.py:403
  8.8 13.8 %collective-permute-start.1 = (bf16[2,416,256]{2,1,0:T(8,128)(2,1)S(1)}, bf16[2,416,256]{2,1,0:T(8,128)(2,1)S(1)}, u32[]{:S(2)}, u32[]{:S(2)}) collective-permute-start(bf16[2,416,256]{2,1,0:T(8,128)(2,1)S(1)} %get-tuple-element.19.own.refs_7_), channel_id=1, source_target_pairs={{2,6},{0,12},{3,7},{1,13},{6,10},{4,0},{7,11},{5,1},{10,14},{8,4},... | collective-permute-start | bytes 1277960 | tf_op jit(solution)/shard_map/ppermute | solution.py:438
  12.4 19.4 %collective-permute-start.3 = (bf16[2,416,256]{2,1,0:T(8,128)(2,1)S(1)}, bf16[2,416,256]{2,1,0:T(8,128)(2,1)S(1)}, u32[]{:S(2)}, u32[]{:S(2)}) collective-permute-start(bf16[2,416,256]{2,1,0:T(8,128)(2,1)S(1)} %get-tuple-element.20), channel_id=1, source_target_pairs={{2,4},{0,14},{3,5},{1,15},{6,8},{4,2},{7,9},{5,3},{10,12},{8,6},{1... | collective-permute-start | bytes 1277960 | tf_op jit(solution)/shard_map/ppermute | solution.py:439
  26.8 1.8 %copy-start.3 = (s32[2]{0:T(128)S(1)}, s32[2]{0:T(128)}, u32[]{:S(2)}) copy-start(s32[2]{0:T(128)} %directions.3) | copy-start | bytes 28
  26.8 1.8 %collective-permute-start.4 = (bf16[2,384,256]{2,1,0:T(8,128)(2,1)S(1)}, bf16[2,384,256]{2,1,0:T(8,128)(2,1)S(1)}, u32[]{:S(2)}, u32[]{:S(2)}) collective-permute-start(bf16[2,384,256]{2,1,0:T(8,128)(2,1)S(1)} %get-tuple-element.21.refs_0_), channel_id=1, source_target_pairs={{0,1},{1,0},{2,3},{3,2},{4,5},{5,4},{6,7},{7,6},{8,9},{9,8},{10,11... | collective-permute-start | bytes 1179656 | tf_op jit(solution)/shard_map/ppermute | solution.py:403
  26.9 10.2 %collective-permute-start.5 = (bf16[416,256]{1,0:T(8,128)(2,1)S(1)}, bf16[416,256]{1,0:T(8,128)(2,1)S(1)}, u32[]{:S(2)}, u32[]{:S(2)}) collective-permute-start(bf16[416,256]{1,0:T(8,128)(2,1)S(1)} %get-tuple-element.25), channel_id=1, source_target_pairs={{0,4},{2,14},{1,5},{3,15},{4,8},{6,2},{5,9},{7,3},{8,12},{10,6},{9... | collective-permute-start | bytes 638984 | tf_op jit(solution)/shard_map/ppermute | solution.py:440
  34.9 6.4 %collective-permute-start.6 = (bf16[2,384,256]{2,1,0:T(8,128)(2,1)S(1)}, bf16[2,384,256]{2,1,0:T(8,128)(2,1)S(1)}, u32[]{:S(2)}, u32[]{:S(2)}) collective-permute-start(bf16[2,384,256]{2,1,0:T(8,128)(2,1)S(1)} %get-tuple-element.24.refs_1_), channel_id=1, source_target_pairs={{0,1},{1,0},{2,3},{3,2},{4,5},{5,4},{6,7},{7,6},{8,9},{9,8},{10,11... | collective-permute-start | bytes 1179656 | tf_op jit(solution)/shard_map/ppermute | solution.py:403
  39.8 1.5 %collective-permute-start.7 = (bf16[1,384,256]{2,1,0:T(8,128)(2,1)S(1)}, bf16[1,384,256]{2,1,0:T(8,128)(2,1)S(1)}, u32[]{:S(2)}, u32[]{:S(2)}) collective-permute-start(bf16[1,384,256]{2,1,0:T(8,128)(2,1)S(1)} %shard_map.73.refs_2_), channel_id=1, source_target_pairs={{0,1},{1,0},{2,3},{3,2},{4,5},{5,4},{6,7},{7,6},{8,9},{9,8},{10,11... | collective-permute-start | bytes 589832 | tf_op jit(solution)/shard_map/ppermute | solution.py:403
  45.3 19.0 %copy-start = (bf16[4,2,256,256]{3,2,1,0:T(8,128)(2,1)S(1)}, bf16[4,2,256,256]{3,2,1,0:T(8,128)(2,1)}, u32[]{:S(2)}) copy-start(bf16[4,2,256,256]{3,2,1,0:T(8,128)(2,1)} %perambulators.1) | copy-start | bytes 3145732
  45.3 7.5 %collective-permute-start.8 = (bf16[256,256]{1,0:T(8,128)(2,1)S(1)}, bf16[256,256]{1,0:T(8,128)(2,1)S(1)}, u32[]{:S(2)}, u32[]{:S(2)}) collective-permute-start(bf16[256,256]{1,0:T(8,128)(2,1)S(1)} %get-tuple-element.29), channel_id=1, source_target_pairs={{0,12},{1,13},{2,14},{3,15},{4,8},{5,9},{6,10},{7,11},{8,4},{9,5},... | collective-permute-start | bytes 393224 | tf_op jit(solution)/shard_map/ppermute | solution.py:403
  52.9 5.0 %collective-permute-start.9 = (bf16[256,256]{1,0:T(8,128)(2,1)S(1)}, bf16[256,256]{1,0:T(8,128)(2,1)S(1)}, u32[]{:S(2)}, u32[]{:S(2)}) collective-permute-start(bf16[256,256]{1,0:T(8,128)(2,1)S(1)} %fusion), channel_id=1, source_target_pairs={{0,4},{1,5},{2,6},{3,7},{4,0},{5,1},{6,2},{7,3},{8,12},{9,13},{10,... | collective-permute-start | bytes 393224 | tf_op jit(solution)/shard_map/ppermute | solution.py:403
  58.0 6.4 %copy-start.4 = (s32[4,2]{0,1:T(2,128)S(1)}, s32[4,2]{0,1:T(2,128)}, u32[]{:S(2)}) copy-start(s32[4,2]{0,1:T(2,128)} %param.8) | copy-start | bytes 100
  58.0 5.0 %collective-permute-start.10 = (bf16[256,256]{1,0:T(8,128)(2,1)S(1)}, bf16[256,256]{1,0:T(8,128)(2,1)S(1)}, u32[]{:S(2)}, u32[]{:S(2)}) collective-permute-start(bf16[256,256]{1,0:T(8,128)(2,1)S(1)} %add_convert_fusion.s00), channel_id=1, source_target_pairs={{0,2},{1,3},{2,0},{3,1},{4,6},{5,7},{6,4},{7,5},{8,10},{9,11},{10,... | collective-permute-start | bytes 393224 | tf_op jit(solution)/shard_map/ppermute | solution.py:403
  58.6 4.4 %collective-permute-start.11 = (bf16[256,256]{1,0:T(8,128)(2,1)S(1)}, bf16[256,256]{1,0:T(8,128)(2,1)S(1)}, u32[]{:S(2)}, u32[]{:S(2)}) collective-permute-start(bf16[256,256]{1,0:T(8,128)(2,1)S(1)} %add_convert_fusion.s00), channel_id=1, source_target_pairs={{0,1},{1,0},{2,3},{3,2},{4,5},{5,4},{6,7},{7,6},{8,9},{9,8},{10,11... | collective-permute-start | bytes 393224 | tf_op jit(solution)/shard_map/ppermute | solution.py:403
  63.0 1.3 %collective-permute-start.12 = (bf16[256,256]{1,0:T(8,128)(2,1)S(1)}, bf16[256,256]{1,0:T(8,128)(2,1)S(1)}, u32[]{:S(2)}, u32[]{:S(2)}) collective-permute-start(bf16[256,256]{1,0:T(8,128)(2,1)S(1)} %collective-permute-done.10.s10), channel_id=1, source_target_pairs={{0,1},{1,0},{2,3},{3,2},{4,5},{5,4},{6,7},{7,6},{8,9},{9,8},{10,11... | collective-permute-start | bytes 393224 | tf_op jit(solution)/shard_map/ppermute | solution.py:403

commit v5 on v4

--- a/solution.py
+++ b/solution.py
@@ -142,12 +142,20 @@
     return package.at[:, pl.ds(FIELD, PACKED_LINKS)]
 
 
-def build(operator, rims, at):
+BEFORE, WITHIN, AFTER = range(3)
+
+
+def build(operator, rims, at, pieces=(BEFORE, WITHIN, AFTER)):
     _, chip = position()
     ascending = chip == 1
     ahead_x, ahead_y, behind_x, behind_y, same = site_masks()
     table = link_planes(rims[at])
-    below = link_planes(jnp.where(ascending, rims[at - 1], rims[at + 1]))
+    if AFTER not in pieces:
+        below = link_planes(rims[at - 1])
+    elif BEFORE not in pieces:
+        below = link_planes(rims[at + 1])
+    else:
+        below = link_planes(jnp.where(ascending, rims[at - 1], rims[at + 1]))
     lane = lax.broadcasted_iota(jnp.int32, table.shape, 1)
     from_x = pltpu.roll(table, LY, 1)
     from_y = shift_y(table, lane)
@@ -162,22 +170,25 @@
             rows = pl.ds((part * COLORS + i) * SITES, SITES)
             for j in range(COLORS):
                 zero = jnp.zeros((SITES, SITES), f32)
-                plane = jnp.where(ahead_x, row_of(from_x, 0, part, i, j), zero)
-                plane = jnp.where(ahead_y, row_of(from_y, 1, part, i, j), plane)
-                plane = jnp.where(behind_x, sign * row_of(table, 0, part, j, i), plane)
-                plane = jnp.where(behind_y, sign * row_of(table, 1, part, j, i), plane)
                 lower = sign * row_of(below, 2, part, j, i)
                 upper = row_of(table, 2, part, i, j)
-                before = jnp.where(same, jnp.where(ascending, lower, upper), zero)
-                after = jnp.where(same, jnp.where(ascending, upper, lower), zero)
-                for k, block in enumerate((before, plane, after)):
+                for k, piece in enumerate(pieces):
+                    if piece == BEFORE:
+                        block = jnp.where(same, jnp.where(ascending, lower, upper), zero)
+                    elif piece == AFTER:
+                        block = jnp.where(same, jnp.where(ascending, upper, lower), zero)
+                    else:
+                        block = jnp.where(ahead_x, row_of(from_x, 0, part, i, j), zero)
+                        block = jnp.where(ahead_y, row_of(from_y, 1, part, i, j), block)
+                        block = jnp.where(behind_x, sign * row_of(table, 0, part, j, i), block)
+                        block = jnp.where(behind_y, sign * row_of(table, 1, part, j, i), block)
                     operator[rows, pl.ds((k * COLORS + j) * SITES, SITES)] = block.astype(bf16)
 
 
-def smeared(operator, source, at):
+def weighted_hops(operator, planes):
     half = SITES
-    window = source[pl.ds(at - 1, 3)].reshape(3 * FIELD, 2 * half)
-    product = jnp.dot(operator[...], window, preferred_element_type=f32)
+    window = planes.reshape(-1, 2 * half)
+    product = jnp.dot(operator, window, preferred_element_type=f32)
     hops = jnp.concatenate(
         [
             product[:FIELD, :half] - product[FIELD:, half:],
@@ -185,8 +196,18 @@
         ],
         axis=1,
     )
-    center = source[at].astype(f32)
-    return ((1.0 - 6.0 * SMEAR) * center + SMEAR * hops).astype(bf16)
+    return SMEAR * hops
+
+
+def smeared(operator, source, at):
+    center = (1.0 - 6.0 * SMEAR) * source[at].astype(f32)
+    return (center + weighted_hops(operator[...], source[pl.ds(at - 1, 3)])).astype(bf16)
+
+
+def smeared_short(operator, source, at):
+    center = (1.0 - 6.0 * SMEAR) * source[at].astype(f32)
+    columns = operator[:, pl.ds(0, 2 * FIELD)]
+    return center + weighted_hops(columns, source[pl.ds(at - 1, 2)])
 
 
 def smear_inner(second, across, own, w_out, u_out, fields, rims, grown, operators, sems):
@@ -203,7 +224,9 @@
     u_out[...] = grown[2:4]
 
 
-def smear_middle(across, own, first, u_in, w_out, u_out, fields, rims, grown, operators, sems):
+def smear_middle(
+    across, own, first, u_in, w_out, first_short, second_short, after_out, fields, rims, grown, operators, sems
+):
     fetch(
         [
             (field_of(own), fields.at[pl.ds(0, 2)]),
@@ -219,27 +242,21 @@
         build(operators.at[r - 4], rims, r - 3)
         if r > 4:
             grown[r - 3] = smeared(operators.at[r - 4], fields, r - 4)
+    build(operators.at[3], rims, 4, (BEFORE, WITHIN))
     for r in (4, 5):
         w_out[r - 4] = smeared(operators.at[r - 4], grown, r - 3)
-    u_out[...] = grown[2:4]
-
-
-def smear_outer(own, first, last, u_in, w_out, fields, rims, grown, operators, sems):
-    fetch(
-        [
-            (field_of(first), fields.at[pl.ds(0, 2)]),
-            (last.at[pl.ds(0, FIELD)], fields.at[2]),
-            (own.at[1, pl.ds(FIELD, PACKED_LINKS)], rims.at[0]),
-            (links_of(first), rims.at[pl.ds(1, 2)]),
-            (last.at[pl.ds(FIELD, PACKED_LINKS)], rims.at[3]),
-            (u_in, grown.at[pl.ds(0, 2)]),
-        ],
-        sems,
-    )
-    build(operators.at[1], rims, 2)
-    grown[2] = smeared(operators.at[1], fields, 1)
-    build(operators.at[0], rims, 1)
-    w_out[0] = smeared(operators.at[0], grown, 1)
+    first_short[...] = smeared_short(operators.at[3], fields, 3)
+    second_short[...] = smeared_short(operators.at[2], grown, 3)
+    after_out[...] = operators[2, :, pl.ds(2 * FIELD, FIELD)]
+
+
+def smear_outer(first, last, first_short, second_short, after, w_out, rims, operator):
+    rims[0] = first[1, pl.ds(FIELD, PACKED_LINKS)]
+    rims[1] = last[pl.ds(FIELD, PACKED_LINKS)]
+    build(operator, rims, 0, (AFTER,))
+    outer = last[pl.ds(0, FIELD)]
+    grown = (first_short[...] + weighted_hops(operator[...], outer)).astype(bf16)
+    w_out[0] = (second_short[...] + weighted_hops(after[...], grown)).astype(bf16)
 
 
 def elemental_kernel(scale, vector_pieces, link_pieces, directions, *refs):
@@ -247,27 +264,22 @@
     packages = max(piece[0] for piece in link_pieces) + 1
     mine, theirs, refs = refs[:groups], refs[groups : 2 * groups], refs[2 * groups :]
     packages, refs = refs[:packages], refs[packages:]
-    *sums, w, rims, right, sems = refs
+    *sums, w, rims, right = refs
     core, chip = position()
     half = SITES
-    copies = []
     at = 0
     for k, first, count in link_pieces:
-        copies.append((links_of(packages[k].at[pl.ds(first, count)]), rims.at[pl.ds(at, count)]))
+        rims[pl.ds(at, count)] = packages[k][pl.ds(first, count), pl.ds(FIELD, PACKED_LINKS)]
         at += count
     for group, side in ((mine, core), (theirs, 1 - core)):
         lanes = pl.ds(pl.multiple_of(side * half, half), half)
         at = 0
         for k, first, count in vector_pieces:
             for part in range(2):
-                copies.append(
-                    (
-                        group[k].at[pl.ds(first, count), :, pl.ds(part * half, half)],
-                        w.at[pl.ds(at, count), part, :, lanes],
-                    )
-                )
+                w[pl.ds(at, count), part, :, lanes] = group[k][
+                    pl.ds(first, count), :, pl.ds(part * half, half)
+                ]
             at += count
-    fetch(copies, sems)
     direction = directions[core]
     ahead_x, ahead_y, _, _, same = site_masks()
     one = jnp.ones((SITES, SITES), f32)
@@ -439,16 +451,17 @@
     first = lax.ppermute(other, "space", crossing)
     last = lax.ppermute(edge, "space", outer)
 
-    def smear(kernel, operands, ranks, link_planes_held, grown_held, operators_held, outputs):
+    small = pl.CostEstimate(flops=1024, bytes_accessed=1024, transcendentals=0)
+
+    def smear(kernel, operands, ranks, link_planes_held, grown_held, operators_held, outputs, more=()):
         def shape(count):
             return jax.ShapeDtypeStruct((count, FIELD, vector_count), bf16)
 
-        products = 2 * FIELD * 3 * FIELD * vector_count * (operators_held + outputs[0])
         return pl.pallas_call(
             kernel,
-            out_shape=tuple(shape(count) for count in outputs),
+            out_shape=tuple(shape(count) for count in outputs) + more,
             in_specs=[anywhere] * len(operands),
-            out_specs=(vmem,) * len(outputs),
+            out_specs=(vmem,) * (len(outputs) + len(more)),
             scratch_shapes=[
                 pltpu.VMEM((ranks, FIELD, vector_count), bf16),
                 pltpu.VMEM((link_planes_held, PACKED_LINKS, 2 * SITES), bf16),
@@ -457,9 +470,7 @@
                 pltpu.SemaphoreType.DMA((6,)),
             ],
             compiler_params=params(20),
-            cost_estimate=pl.CostEstimate(
-                flops=1024, bytes_accessed=1024, transcendentals=0
-            ),
+            cost_estimate=small,
         )(*operands)
 
     site_scale = (6.0 * n * SITES) ** (-0.5)
@@ -472,22 +483,18 @@
         if scale is not None:
             outputs = (jax.ShapeDtypeStruct(square, f32), jax.ShapeDtypeStruct(square, bf16))
         operands = [part[0] for part in groups] + [part[1] for part in groups] + list(packages)
-        products = (ranks - 1) * 4 * FIELD * vector_count * (FIELD + 2 * vector_count)
         return pl.pallas_call(
             functools.partial(elemental_kernel, scale, vector_pieces, link_pieces),
             out_shape=outputs,
-            in_specs=[smem] + [anywhere] * len(operands) + [vmem] * len(sums),
+            in_specs=[smem] + [vmem] * (len(operands) + len(sums)),
             out_specs=(vmem,) * len(outputs),
             scratch_shapes=[
                 pltpu.VMEM((ranks, 2, FIELD, vector_count), bf16),
                 pltpu.VMEM((ranks, PACKED_LINKS, 2 * SITES), bf16),
                 pltpu.VMEM((ranks - 1, 2, FIELD, 2 * vector_count), bf16),
-                pltpu.SemaphoreType.DMA((4 * len(vector_pieces) + len(link_pieces),)),
             ],
             compiler_params=params(16),
-            cost_estimate=pl.CostEstimate(
-                flops=1024, bytes_accessed=1024, transcendentals=0
-            ),
+            cost_estimate=small,
         )(directions, *operands, *sums)
 
     def with_partner(part):
@@ -497,17 +504,30 @@
     inner = with_partner(w_inner)
     (sum_inner,) = elemental(None, (inner,), ((0, 0, 2),), (across,), ((0, 0, 2),), ())
     u_inner, sum_inner = lax.optimization_barrier((u_inner, sum_inner))
-    w_middle, u_middle = smear(smear_middle, (across, own, first, u_inner), 4, 5, 4, 3, (2, 2))
+    short = jax.ShapeDtypeStruct((FIELD, vector_count), f32)
+    after_shape = jax.ShapeDtypeStruct((2 * FIELD, FIELD), bf16)
+    w_middle, first_short, second_short, after = smear(
+        smear_middle, (across, own, first, u_inner), 4, 5, 4, 4, (2,), (short, short, after_shape)
+    )
     middle = with_partner(w_middle)
-    (w_outer,) = smear(smear_outer, (own, first, last, u_middle), 3, 4, 3, 2, (1,))
+    w_outer = pl.pallas_call(
+        smear_outer,
+        out_shape=jax.ShapeDtypeStruct((1, FIELD, vector_count), bf16),
+        in_specs=[vmem] * 5,
+        out_specs=vmem,
+        scratch_shapes=[
+            pltpu.VMEM((2, PACKED_LINKS, 2 * SITES), bf16),
+            pltpu.VMEM((2 * FIELD, FIELD), bf16),
+        ],
+        compiler_params=params(8),
+        cost_estimate=small,
+    )(first, last, first_short, second_short, after)
     outer_part = with_partner(w_outer)
+    (sum_middle,) = elemental(
+        None, (inner, middle), ((0, 1, 1), (1, 0, 2)), (across, own), ((0, 1, 1), (1, 0, 2)), (sum_inner,)
+    )
     partial, partial_low = elemental(
-        site_scale,
-        (inner, middle, outer_part),
-        ((0, 1, 1), (1, 0, 2), (2, 0, 1)),
-        (across, own, first),
-        ((0, 1, 1), (1, 0, 2), (2, 0, 1)),
-        (sum_inner,),
+        site_scale, (middle, outer_part), ((0, 1, 1), (1, 0, 1)), (own, first), ((0, 1, 1), (1, 0, 1)), (sum_middle,)
     )
 
     bit = n // 2

time: 68.7 us -> 66.5 us (0.968)
  waiting for transfers between devices: 31.3 us -> 29.3 us
  Pallas kernels: 21.6 us -> 20.9 us
    pallas_call x3 -> x2, Pallas kernels: 9.91 us -> 8.02 us  [smear(): pl.pallas_call(kernel, out_shape=tuple((shape(count) for count in outputs...]
    ppermute x10, waiting for transfers between devices: 24.4 us -> 23 us  [swap(): return lax.ppermute(value, 'space', [(i, i ^ bit) for i in range(n)])]
    pallas_call x0 -> x1, Pallas kernels: none -> 1.05 us  [body(): pl.pallas_call(smear_outer, out_shape=jax.ShapeDtypeStruct((1, FIELD, vec...]
    ppermute x1, waiting for transfers between devices: 2.14 us -> 1.35 us  [body(): last = lax.ppermute(edge, 'space', outer)]
    pallas_call x2 -> x3, Pallas kernels: 6.14 us -> 6.31 us  [elemental(): pl.pallas_call(functools.partial(elemental_kernel, scale, vector_pieces,...]
  transfers between devices with their start and end apart: 13 -> 13, of which waited for: 11 -> 10; matrix products, arithmetic and copies ran while one was open for 0% -> 0% of each run, Pallas kernels for 17% -> 20%
where the time goes in v5:
time: 66.5 us; the launch traced here: 66.2 us
  waiting for transfers between devices  29.3 us (44%)
  Pallas kernels  20.9 us (31%)
  starting transfers between devices  13.3 us (20%)
  local copies, waits for them, and re-layouts  1.89 us (3%)
  between operations  0.78 us (1%)
    ppermute x10, waiting for transfers between devices, swap(): return lax.ppermute(value, 'space', [(i, i ^ bit) for i in range(n)])  23 us
    ppermute x10, starting transfers between devices, swap(): return lax.ppermute(value, 'space', [(i, i ^ bit) for i in range(n)])  8.97 us
    pallas_call x2, Pallas kernels, smear(): pl.pallas_call(kernel, out_shape=tuple((shape(count) for count in outputs...  8.02 us
    pallas_call x3, Pallas kernels, elemental(): pl.pallas_call(functools.partial(elemental_kernel, scale, vector_pieces,...  6.31 us
    pallas_call x1, Pallas kernels, body(): pl.pallas_call(functools.partial(pair_kernel, pair_scale), out_shape=(jax...  4.16 us
    ppermute x1, waiting for transfers between devices, body(): second = lax.ppermute(own, 'space', straight)  3.71 us
    ppermute x1, starting transfers between devices, body(): second = lax.ppermute(own, 'space', straight)  3.6 us
    unnamed x10, local copies, waits for them, and re-layouts  1.89 us
  transfers between devices with their start and end apart: 13, of which 10 were waited for; matrix products, arithmetic and copies ran while one was open for 0% of the time, Pallas kernels for 20%

profile of v5, /device:TPU:0, one launch (start us, length us, event | category | flops | bytes accessed | tf_op | source)
XLA Modules:
  0.0 66.2 jit_solution(11449605700530380151)
XLA Ops:
  0.6 0.0 copy-start.1
  0.6 1.1 %copy-done.1 = bf16[2,2,3,1,128,256]{5,4,3,2,1,0:T(8,128)(2,1)S(1)} copy-done((bf16[2,2,3,1,128,256]{5,4,3,2,1,0:T(8,128)(2,1)S(1)}, bf16[2,2,3,1,128,256]{5,4,3,2,1,0:T(8,128)(2,1)}, u32[]{:S(2)}) %copy-start.1) | copy-done | bytes 786456
  1.8 0.0 copy-start.2
  1.8 0.7 %copy-done.2 = bf16[2,3,2,3,3,1,128]{6,2,5,4,3,1,0:T(2,128)(2,1)S(1)} copy-done((bf16[2,3,2,3,3,1,128]{6,2,5,4,3,1,0:T(2,128)(2,1)S(1)}, bf16[2,3,2,3,3,1,128]{6,2,5,4,3,1,0:T(2,128)(2,1)}, u32[]{:S(2)}) %copy-start.2) | copy-done | bytes 27672
  2.5 0.6 shard_map.68
  3.1 0.5 collective-permute-start
  3.6 1.4 %collective-permute-done.received = bf16[2,416,256]{2,1,0:T(8,128)(2,1)S(1)} collective-permute-done((bf16[2,416,256]{2,1,0:T(8,128)(2,1)S(1)}, bf16[2,416,256]{2,1,0:T(8,128)(2,1)S(1)}, u32[]{:S(2)}, u32[]{:S(2)}) %collective-permute-start) | collective-permute-done | bytes 426016 | tf_op jit(solution)/shard_map/ppermute | solution.py:415
  5.0 0.8 %shard_map.69 = (bf16[2,416,256]{2,1,0:T(8,128)(2,1)S(1)}, bf16[2,416,256]{2,1,0:T(8,128)(2,1)S(1)}, bf16[416,256]{1,0:T(8,128)(2,1)S(1)}) custom-call(bf16[2,416,256]{2,1,0:T(8,128)(2,1)S(1)} %collective-permute-done.received, bf16[2,416,256]{2,1,0:T(8,128)(2,1)S(1)} %get-tuple-element.19.own_in, ...), custom_call_target="tpu_custom_call", output_to_operand_aliasing={{0}: (1, {}), {1}: (2, {})} | custom-call | tf_op jit(solution)/shard_map/pallas_call | solution.py:431
  5.9 3.0 %collective-permute-start.1 = (bf16[2,416,256]{2,1,0:T(8,128)(2,1)S(1)}, bf16[2,416,256]{2,1,0:T(8,128)(2,1)S(1)}, u32[]{:S(2)}, u32[]{:S(2)}) collective-permute-start(bf16[2,416,256]{2,1,0:T(8,128)(2,1)S(1)} %get-tuple-element.21), channel_id=1, source_target_pairs={{0,2},{1,3},{2,0},{3,1},{4,6},{5,7},{6,4},{7,5},{8,10},{9,11},{10,... | collective-permute-start | bytes 1277960 | tf_op jit(solution)/shard_map/ppermute | solution.py:415
  8.8 3.6 %collective-permute-start.3 = (bf16[2,416,256]{2,1,0:T(8,128)(2,1)S(1)}, bf16[2,416,256]{2,1,0:T(8,128)(2,1)S(1)}, u32[]{:S(2)}, u32[]{:S(2)}) collective-permute-start(bf16[2,416,256]{2,1,0:T(8,128)(2,1)S(1)} %get-tuple-element.22.own.refs_5_.refs_4_), channel_id=1, source_target_pairs={{2,6},{0,12},{3,7},{1,13},{6,10},{4,0},{7,11},{5,1},{10,14},{8,4},... | collective-permute-start | bytes 1277960 | tf_op jit(solution)/shard_map/ppermute | solution.py:450
  12.4 0.0 collective-permute-start.2
  12.4 6.5 %collective-permute-done.1.across.refs_2_.refs_4_ = bf16[2,416,256]{2,1,0:T(8,128)(2,1)S(1)} collective-permute-done((bf16[2,416,256]{2,1,0:T(8,128)(2,1)S(1)}, bf16[2,416,256]{2,1,0:T(8,128)(2,1)S(1)}, u32[]{:S(2)}, u32[]{:S(2)}) %collective-permute-start.1) | collective-permute-done | bytes 426016 | tf_op jit(solution)/shard_map/ppermute | solution.py:415
  18.9 3.7 %collective-permute-done.3.second = bf16[2,416,256]{2,1,0:T(8,128)(2,1)S(1)} collective-permute-done((bf16[2,416,256]{2,1,0:T(8,128)(2,1)S(1)}, bf16[2,416,256]{2,1,0:T(8,128)(2,1)S(1)}, u32[]{:S(2)}, u32[]{:S(2)}) %collective-permute-start.3) | collective-permute-done | bytes 426016 | tf_op jit(solution)/shard_map/ppermute | solution.py:450
  22.6 4.1 %shard_map.70 = (bf16[2,384,256]{2,1,0:T(8,128)(2,1)S(1)}, bf16[2,384,256]{2,1,0:T(8,128)(2,1)S(1)}) custom-call(bf16[2,416,256]{2,1,0:T(8,128)(2,1)S(1)} %collective-permute-done.3.second, bf16[2,416,256]{2,1,0:T(8,128)(2,1)S(1)} %collective-permute-done.1.across.refs_2_.refs_4_, bf16[2,416,256]{2,1,0:T(8,128)(2,1)S(1)} %get-tuple-element.22.own.refs_5_.refs_4_), custom_call_target="tpu_custom_call" | custom-call | flops 1024 | bytes 1024 | tf_op jit(solution)/shard_map/pallas_call | solution.py:460
  26.8 0.0 copy-start.3
  26.8 0.1 collective-permute-start.4
  26.9 0.7 %collective-permute-start.5 = (bf16[416,256]{1,0:T(8,128)(2,1)S(1)}, bf16[416,256]{1,0:T(8,128)(2,1)S(1)}, u32[]{:S(2)}, u32[]{:S(2)}) collective-permute-start(bf16[416,256]{1,0:T(8,128)(2,1)S(1)} %get-tuple-element.27), channel_id=1, source_target_pairs={{0,4},{2,14},{1,5},{3,15},{4,8},{6,2},{5,9},{7,3},{8,12},{10,6},{9... | collective-permute-start | bytes 638984 | tf_op jit(solution)/shard_map/ppermute | solution.py:452
  27.6 1.0 %collective-permute-done.4.refs_1_.refs_2_ = bf16[2,384,256]{2,1,0:T(8,128)(2,1)S(1)} collective-permute-done((bf16[2,384,256]{2,1,0:T(8,128)(2,1)S(1)}, bf16[2,384,256]{2,1,0:T(8,128)(2,1)S(1)}, u32[]{:S(2)}, u32[]{:S(2)}) %collective-permute-start.4) | collective-permute-done | bytes 393248 | tf_op jit(solution)/shard_map/ppermute | solution.py:415
  28.6 0.0 copy-done.3
  28.6 1.9 %shard_map.71.refs_6_ = f32[256,512]{1,0:T(8,128)S(1)} custom-call(s32[2]{0:T(128)S(1)} %copy-done.3, bf16[2,384,256]{2,1,0:T(8,128)(2,1)S(1)} %get-tuple-element.24.refs_0_, bf16[2,384,256]{2,1,0:T(8,128)(2,1)S(1)} %collective-permute-done.4.refs_1_.refs_2_, bf16[2,416,256]{2,1,0:T(8,128)(2,1)S(1)} %collective-permute-done.1.across.refs_2_.refs_4_), custom_call_target="tpu_custom_call" | custom-call | flops 1024 | bytes 1024 | tf_op jit(solution)/shard_map/pallas_call | solution.py:486
  30.5 1.2 %collective-permute-done.2.first.refs_5_ = bf16[2,416,256]{2,1,0:T(8,128)(2,1)S(1)} collective-permute-done((bf16[2,416,256]{2,1,0:T(8,128)(2,1)S(1)}, bf16[2,416,256]{2,1,0:T(8,128)(2,1)S(1)}, u32[]{:S(2)}, u32[]{:S(2)}) %collective-permute-start.2) | collective-permute-done | bytes 426016 | tf_op jit(solution)/shard_map/ppermute | solution.py:451
  31.8 3.9 %shard_map.72 = (bf16[2,384,256]{2,1,0:T(8,128)(2,1)S(1)}, f32[384,256]{1,0:T(8,128)S(1)}, f32[384,256]{1,0:T(8,128)S(1)}, bf16[768,384]{1,0:T(8,128)(2,1)S(1)}) custom-call(bf16[2,416,256]{2,1,0:T(8,128)(2,1)S(1)} %collective-permute-done.1.across.refs_2_.refs_4_, bf16[2,416,256]{2,1,0:T(8,128)(2,1)S(1)} %get-tuple-element.22.own.refs_5_.refs_4_, ...), custom_call_target="tpu_custom_call" | custom-call | flops 1024 | bytes 1024 | tf_op jit(solution)/shard_map/pallas_call | solution.py:460
  35.6 0.1 collective-permute-start.6
  35.7 1.4 %collective-permute-done.5.last = bf16[416,256]{1,0:T(8,128)(2,1)S(1)} collective-permute-done((bf16[416,256]{1,0:T(8,128)(2,1)S(1)}, bf16[416,256]{1,0:T(8,128)(2,1)S(1)}, u32[]{:S(2)}, u32[]{:S(2)}) %collective-permute-start.5) | collective-permute-done | bytes 213024 | tf_op jit(solution)/shard_map/ppermute | solution.py:452
  37.1 1.1 %shard_map.73.refs_1_ = bf16[1,384,256]{2,1,0:T(8,128)(2,1)S(1)} custom-call(bf16[2,416,256]{2,1,0:T(8,128)(2,1)S(1)} %collective-permute-done.2.first.refs_5_, bf16[416,256]{1,0:T(8,128)(2,1)S(1)} %collective-permute-done.5.last, f32[384,256]{1,0:T(8,128)S(1)} %get-tuple-element.28.first_short, f32[384,256]{1,0:T(8,128)S(1)} %get-tuple-element.29.second_short, ...), custom_call_target="tpu_custom_call" | custom-call | flops 1024 | bytes 1024 | tf_op jit(solution)/shard_map/pallas_call | solution.py:513
  38.1 0.1 collective-permute-start.7
  38.2 0.0 collective-permute-done.6.refs_3_.refs_2_
  38.2 2.3 %shard_map.74.refs_6_ = f32[256,512]{1,0:T(8,128)S(1)} custom-call(s32[2]{0:T(128)S(1)} %copy-done.3, bf16[2,384,256]{2,1,0:T(8,128)(2,1)S(1)} %get-tuple-element.24.refs_0_, bf16[2,384,256]{2,1,0:T(8,128)(2,1)S(1)} %get-tuple-element.26.refs_1_.refs_0_, bf16[2,384,256]{2,1,0:T(8,128)(2,1)S(1)} %collective-permute-done.4.refs_1_.refs_2_, ...), custom_call_target="tpu_custom_call" | custom-call | flops 1024 | bytes 1024 | tf_op jit(solution)/shard_map/pallas_call | solution.py:486
  40.5 0.0 collective-permute-done.7.refs_3_
  40.5 2.1 %shard_map.75 = (f32[256,256]{1,0:T(8,128)S(1)}, bf16[256,256]{1,0:T(8,128)(2,1)S(1)}) custom-call(s32[2]{0:T(128)S(1)} %copy-done.3, bf16[2,384,256]{2,1,0:T(8,128)(2,1)S(1)} %get-tuple-element.26.refs_1_.refs_0_, bf16[1,384,256]{2,1,0:T(8,128)(2,1)S(1)} %shard_map.73.refs_1_, bf16[2,384,256]{2,1,0:T(8,128)(2,1)S(1)} %collective-permute-done.6.refs_3_.refs_2_, ...), custom_call_target="tpu_custom_call" | custom-call | flops 1024 | bytes 1024 | tf_op jit(solution)/shard_map/pallas_call | solution.py:486
  42.6 0.0 copy-start
  42.6 2.7 %collective-permute-start.8 = (bf16[256,256]{1,0:T(8,128)(2,1)S(1)}, bf16[256,256]{1,0:T(8,128)(2,1)S(1)}, u32[]{:S(2)}, u32[]{:S(2)}) collective-permute-start(bf16[256,256]{1,0:T(8,128)(2,1)S(1)} %get-tuple-element.33), channel_id=1, source_target_pairs={{0,12},{1,13},{2,14},{3,15},{4,8},{5,9},{6,10},{7,11},{8,4},{9,5},... | collective-permute-start | bytes 393224 | tf_op jit(solution)/shard_map/ppermute | solution.py:415
  45.3 5.2 %collective-permute-done.8 = bf16[256,256]{1,0:T(8,128)(2,1)S(1)} collective-permute-done((bf16[256,256]{1,0:T(8,128)(2,1)S(1)}, bf16[256,256]{1,0:T(8,128)(2,1)S(1)}, u32[]{:S(2)}, u32[]{:S(2)}) %collective-permute-start.8) | collective-permute-done | bytes 131104 | tf_op jit(solution)/shard_map/ppermute | solution.py:415
  50.5 1.6 %collective-permute-start.9 = (bf16[256,256]{1,0:T(8,128)(2,1)S(1)}, bf16[256,256]{1,0:T(8,128)(2,1)S(1)}, u32[]{:S(2)}, u32[]{:S(2)}) collective-permute-start(bf16[256,256]{1,0:T(8,128)(2,1)S(1)} %fusion), channel_id=1, source_target_pairs={{0,4},{1,5},{2,6},{3,7},{4,0},{5,1},{6,2},{7,3},{8,12},{9,13},{10,... | collective-permute-start | bytes 393224 | tf_op jit(solution)/shard_map/ppermute | solution.py:415
  52.1 3.5 %collective-permute-done.9 = bf16[256,256]{1,0:T(8,128)(2,1)S(1)} collective-permute-done((bf16[256,256]{1,0:T(8,128)(2,1)S(1)}, bf16[256,256]{1,0:T(8,128)(2,1)S(1)}, u32[]{:S(2)}, u32[]{:S(2)}) %collective-permute-start.9) | collective-permute-done | bytes 131104 | tf_op jit(solution)/shard_map/ppermute | solution.py:415
  55.7 0.0 copy-start.4
  55.7 1.0 %collective-permute-start.10 = (bf16[256,256]{1,0:T(8,128)(2,1)S(1)}, bf16[256,256]{1,0:T(8,128)(2,1)S(1)}, u32[]{:S(2)}, u32[]{:S(2)}) collective-permute-start(bf16[256,256]{1,0:T(8,128)(2,1)S(1)} %add_convert_fusion.s00), channel_id=1, source_target_pairs={{0,2},{1,3},{2,0},{3,1},{4,6},{5,7},{6,4},{7,5},{8,10},{9,11},{10,... | collective-permute-start | bytes 393224 | tf_op jit(solution)/shard_map/ppermute | solution.py:415
  56.7 0.0 collective-permute-start.11
  56.7 4.0 %collective-permute-done.10.s10 = bf16[256,256]{1,0:T(8,128)(2,1)S(1)} collective-permute-done((bf16[256,256]{1,0:T(8,128)(2,1)S(1)}, bf16[256,256]{1,0:T(8,128)(2,1)S(1)}, u32[]{:S(2)}, u32[]{:S(2)}) %collective-permute-start.10) | collective-permute-done | bytes 131104 | tf_op jit(solution)/shard_map/ppermute | solution.py:415
  60.7 0.0 collective-permute-start.12
  60.7 0.0 collective-permute-done.11.s01
  60.7 1.3 %collective-permute-done.12.s11 = bf16[256,256]{1,0:T(8,128)(2,1)S(1)} collective-permute-done((bf16[256,256]{1,0:T(8,128)(2,1)S(1)}, bf16[256,256]{1,0:T(8,128)(2,1)S(1)}, u32[]{:S(2)}, u32[]{:S(2)}) %collective-permute-start.12) | collective-permute-done | bytes 131104 | tf_op jit(solution)/shard_map/ppermute | solution.py:415
  62.1 0.0 copy-done
  62.1 0.0 copy-done.4
  62.1 4.2 %shard_map.76 = (f32[2,2,2,16,256]{4,3,2,1,0:T(8,128)}, bf16[4,2,256,256]{3,2,1,0:T(8,128)(2,1)}) custom-call(s32[2,4]{1,0:T(2,128)S(1)} %bitcast.3, bf16[256,256]{1,0:T(8,128)(2,1)S(1)} %add_convert_fusion.s00, bf16[256,256]{1,0:T(8,128)(2,1)S(1)} %collective-permute-done.10.s10, bf16[256,256]{1,0:T(8,128)(2,1)S(1)} %collective-permute-done.11.s01, ...), custom_call_target="tpu_custom_call" | custom-call | tf_op jit(solution)/shard_map/pallas_call | solution.py:546
  (2 shorter events, 0.1 us)
Async XLA Ops:
  0.6 1.1 %copy-start.1 = (bf16[2,2,3,1,128,256]{5,4,3,2,1,0:T(8,128)(2,1)S(1)}, bf16[2,2,3,1,128,256]{5,4,3,2,1,0:T(8,128)(2,1)}, u32[]{:S(2)}) copy-start(bf16[2,2,3,1,128,256]{5,4,3,2,1,0:T(8,128)(2,1)} %vectors.1) | copy-start | bytes 2359300
  1.8 0.7 %copy-start.2 = (bf16[2,3,2,3,3,1,128]{6,2,5,4,3,1,0:T(2,128)(2,1)S(1)}, bf16[2,3,2,3,3,1,128]{6,2,5,4,3,1,0:T(2,128)(2,1)}, u32[]{:S(2)}) copy-start(bf16[2,3,2,3,3,1,128]{6,2,5,4,3,1,0:T(2,128)(2,1)} %param.6) | copy-start | bytes 82948
  3.1 1.9 %collective-permute-start = (bf16[2,416,256]{2,1,0:T(8,128)(2,1)S(1)}, bf16[2,416,256]{2,1,0:T(8,128)(2,1)S(1)}, u32[]{:S(2)}, u32[]{:S(2)}) collective-permute-start(bf16[2,416,256]{2,1,0:T(8,128)(2,1)S(1)} %get-tuple-element.18), channel_id=1, source_target_pairs={{0,1},{1,0},{2,3},{3,2},{4,5},{5,4},{6,7},{7,6},{8,9},{9,8},{10,11... | collective-permute-start | bytes 1277960 | tf_op jit(solution)/shard_map/ppermute | solution.py:415
  5.9 13.1 %collective-permute-start.1 = (bf16[2,416,256]{2,1,0:T(8,128)(2,1)S(1)}, bf16[2,416,256]{2,1,0:T(8,128)(2,1)S(1)}, u32[]{:S(2)}, u32[]{:S(2)}) collective-permute-start(bf16[2,416,256]{2,1,0:T(8,128)(2,1)S(1)} %get-tuple-element.21), channel_id=1, source_target_pairs={{0,2},{1,3},{2,0},{3,1},{4,6},{5,7},{6,4},{7,5},{8,10},{9,11},{10,... | collective-permute-start | bytes 1277960 | tf_op jit(solution)/shard_map/ppermute | solution.py:415
  8.8 13.8 %collective-permute-start.3 = (bf16[2,416,256]{2,1,0:T(8,128)(2,1)S(1)}, bf16[2,416,256]{2,1,0:T(8,128)(2,1)S(1)}, u32[]{:S(2)}, u32[]{:S(2)}) collective-permute-start(bf16[2,416,256]{2,1,0:T(8,128)(2,1)S(1)} %get-tuple-element.22.own.refs_5_.refs_4_), channel_id=1, source_target_pairs={{2,6},{0,12},{3,7},{1,13},{6,10},{4,0},{7,11},{5,1},{10,14},{8,4},... | collective-permute-start | bytes 1277960 | tf_op jit(solution)/shard_map/ppermute | solution.py:450
  12.4 19.4 %collective-permute-start.2 = (bf16[2,416,256]{2,1,0:T(8,128)(2,1)S(1)}, bf16[2,416,256]{2,1,0:T(8,128)(2,1)S(1)}, u32[]{:S(2)}, u32[]{:S(2)}) collective-permute-start(bf16[2,416,256]{2,1,0:T(8,128)(2,1)S(1)} %get-tuple-element.21), channel_id=1, source_target_pairs={{2,4},{0,14},{3,5},{1,15},{6,8},{4,2},{7,9},{5,3},{10,12},{8,6},{1... | collective-permute-start | bytes 1277960 | tf_op jit(solution)/shard_map/ppermute | solution.py:451
  26.8 1.8 %copy-start.3 = (s32[2]{0:T(128)S(1)}, s32[2]{0:T(128)}, u32[]{:S(2)}) copy-start(s32[2]{0:T(128)} %directions.5) | copy-start | bytes 28
  26.8 1.8 %collective-permute-start.4 = (bf16[2,384,256]{2,1,0:T(8,128)(2,1)S(1)}, bf16[2,384,256]{2,1,0:T(8,128)(2,1)S(1)}, u32[]{:S(2)}, u32[]{:S(2)}) collective-permute-start(bf16[2,384,256]{2,1,0:T(8,128)(2,1)S(1)} %get-tuple-element.24.refs_0_), channel_id=1, source_target_pairs={{0,1},{1,0},{2,3},{3,2},{4,5},{5,4},{6,7},{7,6},{8,9},{9,8},{10,11... | collective-permute-start | bytes 1179656 | tf_op jit(solution)/shard_map/ppermute | solution.py:415
  26.9 10.2 %collective-permute-start.5 = (bf16[416,256]{1,0:T(8,128)(2,1)S(1)}, bf16[416,256]{1,0:T(8,128)(2,1)S(1)}, u32[]{:S(2)}, u32[]{:S(2)}) collective-permute-start(bf16[416,256]{1,0:T(8,128)(2,1)S(1)} %get-tuple-element.27), channel_id=1, source_target_pairs={{0,4},{2,14},{1,5},{3,15},{4,8},{6,2},{5,9},{7,3},{8,12},{10,6},{9... | collective-permute-start | bytes 638984 | tf_op jit(solution)/shard_map/ppermute | solution.py:452
  35.6 2.6 %collective-permute-start.6 = (bf16[2,384,256]{2,1,0:T(8,128)(2,1)S(1)}, bf16[2,384,256]{2,1,0:T(8,128)(2,1)S(1)}, u32[]{:S(2)}, u32[]{:S(2)}) collective-permute-start(bf16[2,384,256]{2,1,0:T(8,128)(2,1)S(1)} %get-tuple-element.26.refs_1_.refs_0_), channel_id=1, source_target_pairs={{0,1},{1,0},{2,3},{3,2},{4,5},{5,4},{6,7},{7,6},{8,9},{9,8},{10,11... | collective-permute-start | bytes 1179656 | tf_op jit(solution)/shard_map/ppermute | solution.py:415
  38.1 2.4 %collective-permute-start.7 = (bf16[1,384,256]{2,1,0:T(8,128)(2,1)S(1)}, bf16[1,384,256]{2,1,0:T(8,128)(2,1)S(1)}, u32[]{:S(2)}, u32[]{:S(2)}) collective-permute-start(bf16[1,384,256]{2,1,0:T(8,128)(2,1)S(1)} %shard_map.73.refs_1_), channel_id=1, source_target_pairs={{0,1},{1,0},{2,3},{3,2},{4,5},{5,4},{6,7},{7,6},{8,9},{9,8},{10,11... | collective-permute-start | bytes 589832 | tf_op jit(solution)/shard_map/ppermute | solution.py:415
  42.6 19.5 %copy-start = (bf16[4,2,256,256]{3,2,1,0:T(8,128)(2,1)S(1)}, bf16[4,2,256,256]{3,2,1,0:T(8,128)(2,1)}, u32[]{:S(2)}) copy-start(bf16[4,2,256,256]{3,2,1,0:T(8,128)(2,1)} %perambulators.1) | copy-start | bytes 3145732
  42.6 7.9 %collective-permute-start.8 = (bf16[256,256]{1,0:T(8,128)(2,1)S(1)}, bf16[256,256]{1,0:T(8,128)(2,1)S(1)}, u32[]{:S(2)}, u32[]{:S(2)}) collective-permute-start(bf16[256,256]{1,0:T(8,128)(2,1)S(1)} %get-tuple-element.33), channel_id=1, source_target_pairs={{0,12},{1,13},{2,14},{3,15},{4,8},{5,9},{6,10},{7,11},{8,4},{9,5},... | collective-permute-start | bytes 393224 | tf_op jit(solution)/shard_map/ppermute | solution.py:415
  50.5 5.1 %collective-permute-start.9 = (bf16[256,256]{1,0:T(8,128)(2,1)S(1)}, bf16[256,256]{1,0:T(8,128)(2,1)S(1)}, u32[]{:S(2)}, u32[]{:S(2)}) collective-permute-start(bf16[256,256]{1,0:T(8,128)(2,1)S(1)} %fusion), channel_id=1, source_target_pairs={{0,4},{1,5},{2,6},{3,7},{4,0},{5,1},{6,2},{7,3},{8,12},{9,13},{10,... | collective-permute-start | bytes 393224 | tf_op jit(solution)/shard_map/ppermute | solution.py:415
  55.7 6.4 %copy-start.4 = (s32[4,2]{0,1:T(2,128)S(1)}, s32[4,2]{0,1:T(2,128)}, u32[]{:S(2)}) copy-start(s32[4,2]{0,1:T(2,128)} %param.8) | copy-start | bytes 100
  55.7 5.0 %collective-permute-start.10 = (bf16[256,256]{1,0:T(8,128)(2,1)S(1)}, bf16[256,256]{1,0:T(8,128)(2,1)S(1)}, u32[]{:S(2)}, u32[]{:S(2)}) collective-permute-start(bf16[256,256]{1,0:T(8,128)(2,1)S(1)} %add_convert_fusion.s00), channel_id=1, source_target_pairs={{0,2},{1,3},{2,0},{3,1},{4,6},{5,7},{6,4},{7,5},{8,10},{9,11},{10,... | collective-permute-start | bytes 393224 | tf_op jit(solution)/shard_map/ppermute | solution.py:415
  56.7 4.0 %collective-permute-start.11 = (bf16[256,256]{1,0:T(8,128)(2,1)S(1)}, bf16[256,256]{1,0:T(8,128)(2,1)S(1)}, u32[]{:S(2)}, u32[]{:S(2)}) collective-permute-start(bf16[256,256]{1,0:T(8,128)(2,1)S(1)} %add_convert_fusion.s00), channel_id=1, source_target_pairs={{0,1},{1,0},{2,3},{3,2},{4,5},{5,4},{6,7},{7,6},{8,9},{9,8},{10,11... | collective-permute-start | bytes 393224 | tf_op jit(solution)/shard_map/ppermute | solution.py:415
  60.7 1.3 %collective-permute-start.12 = (bf16[256,256]{1,0:T(8,128)(2,1)S(1)}, bf16[256,256]{1,0:T(8,128)(2,1)S(1)}, u32[]{:S(2)}, u32[]{:S(2)}) collective-permute-start(bf16[256,256]{1,0:T(8,128)(2,1)S(1)} %collective-permute-done.10.s10), channel_id=1, source_target_pairs={{0,1},{1,0},{2,3},{3,2},{4,5},{5,4},{6,7},{7,6},{8,9},{9,8},{10,11... | collective-permute-start | bytes 393224 | tf_op jit(solution)/shard_map/ppermute | solution.py:415

commit v6 on v5

--- a/solution.py
+++ b/solution.py
@@ -204,50 +204,54 @@
     return (center + weighted_hops(operator[...], source[pl.ds(at - 1, 3)])).astype(bf16)
 
 
-def smeared_short(operator, source, at):
-    center = (1.0 - 6.0 * SMEAR) * source[at].astype(f32)
-    columns = operator[:, pl.ds(0, 2 * FIELD)]
-    return center + weighted_hops(columns, source[pl.ds(at - 1, 2)])
-
-
-def smear_inner(second, across, own, w_out, u_out, fields, rims, grown, operators, sems):
+def smeared_short(operator, planes):
+    center = (1.0 - 6.0 * SMEAR) * planes[1].astype(f32)
+    return center + weighted_hops(operator, planes)
+
+
+def smear_inner(second, across, own, w_out, u_out, operator_out, fields, rims, grown, operators, sems):
     copies = []
     for k, package in enumerate((second, across, own)):
         copies.append((field_of(package), fields.at[pl.ds(2 * k, 2)]))
         copies.append((links_of(package), rims.at[pl.ds(2 * k, 2)]))
     fetch(copies, sems)
     for r in range(1, 5):
-        build(operators.at[r - 1], rims, r)
-        grown[r - 1] = smeared(operators.at[r - 1], fields, r)
+        operator = operators.at[r - 1] if r < 4 else operator_out
+        build(operator, rims, r)
+        grown[r - 1] = smeared(operator, fields, r)
     for r in range(2, 4):
         w_out[r - 2] = smeared(operators.at[r - 1], grown, r - 1)
     u_out[...] = grown[2:4]
 
 
+def smear_prepare(own, u_in, operator, first_short, second_short, within_out, rims):
+    for k in range(2):
+        rims[k] = own[k, pl.ds(FIELD, PACKED_LINKS)]
+    build(within_out, rims, 1, (BEFORE, WITHIN))
+    first_short[...] = smeared_short(within_out[...], own[:, pl.ds(0, FIELD)])
+    second_short[...] = smeared_short(operator[:, pl.ds(0, 2 * FIELD)], u_in[...])
+
+
 def smear_middle(
-    across, own, first, u_in, w_out, first_short, second_short, after_out, fields, rims, grown, operators, sems
+    own, first, u_in, operator_in, short_in, second_in, within_in, w_out, first_short, second_short, after_out, fields, rims, grown, operator, within, after
 ):
-    fetch(
-        [
-            (field_of(own), fields.at[pl.ds(0, 2)]),
-            (field_of(first), fields.at[pl.ds(2, 2)]),
-            (across.at[1, pl.ds(FIELD, PACKED_LINKS)], rims.at[0]),
-            (links_of(own), rims.at[pl.ds(1, 2)]),
-            (links_of(first), rims.at[pl.ds(3, 2)]),
-            (u_in, grown.at[pl.ds(0, 2)]),
-        ],
-        sems,
-    )
-    for r in (5, 6, 4):
-        build(operators.at[r - 4], rims, r - 3)
-        if r > 4:
-            grown[r - 3] = smeared(operators.at[r - 4], fields, r - 4)
-    build(operators.at[3], rims, 4, (BEFORE, WITHIN))
-    for r in (4, 5):
-        w_out[r - 4] = smeared(operators.at[r - 4], grown, r - 3)
-    first_short[...] = smeared_short(operators.at[3], fields, 3)
-    second_short[...] = smeared_short(operators.at[2], grown, 3)
-    after_out[...] = operators[2, :, pl.ds(2 * FIELD, FIELD)]
+    fields[0] = own[1, pl.ds(0, FIELD)]
+    rims[0] = own[1, pl.ds(FIELD, PACKED_LINKS)]
+    for k in range(2):
+        fields[1 + k] = first[k, pl.ds(0, FIELD)]
+        rims[1 + k] = first[k, pl.ds(FIELD, PACKED_LINKS)]
+    grown[0] = u_in[1]
+    build(after, rims, 0, (AFTER,))
+    grown[1] = (short_in[...] + weighted_hops(after[...], fields[1])).astype(bf16)
+    build(operator, rims, 1)
+    grown[2] = smeared(operator, fields, 1)
+    w_out[0] = (second_in[...] + weighted_hops(operator_in[:, pl.ds(2 * FIELD, FIELD)], grown[1])).astype(bf16)
+    short = smeared_short(within_in[...], grown[pl.ds(0, 2)])
+    w_out[1] = (short + weighted_hops(after[...], grown[2])).astype(bf16)
+    build(within, rims, 2, (BEFORE, WITHIN))
+    first_short[...] = smeared_short(within[...], fields[pl.ds(1, 2)])
+    second_short[...] = smeared_short(operator[:, pl.ds(0, 2 * FIELD)], grown[pl.ds(1, 2)])
+    after_out[...] = operator[:, pl.ds(2 * FIELD, FIELD)]
 
 
 def smear_outer(first, last, first_short, second_short, after, w_out, rims, operator):
@@ -453,26 +457,13 @@
 
     small = pl.CostEstimate(flops=1024, bytes_accessed=1024, transcendentals=0)
 
-    def smear(kernel, operands, ranks, link_planes_held, grown_held, operators_held, outputs, more=()):
-        def shape(count):
-            return jax.ShapeDtypeStruct((count, FIELD, vector_count), bf16)
-
-        return pl.pallas_call(
-            kernel,
-            out_shape=tuple(shape(count) for count in outputs) + more,
-            in_specs=[anywhere] * len(operands),
-            out_specs=(vmem,) * (len(outputs) + len(more)),
-            scratch_shapes=[
-                pltpu.VMEM((ranks, FIELD, vector_count), bf16),
-                pltpu.VMEM((link_planes_held, PACKED_LINKS, 2 * SITES), bf16),
-                pltpu.VMEM((grown_held, FIELD, vector_count), bf16),
-                pltpu.VMEM((operators_held, 2 * FIELD, 3 * FIELD), bf16),
-                pltpu.SemaphoreType.DMA((6,)),
-            ],
-            compiler_params=params(20),
-            cost_estimate=small,
-        )(*operands)
-
+    def field(count):
+        return jax.ShapeDtypeStruct((count, FIELD, vector_count), bf16)
+
+    def scratch(*shape):
+        return pltpu.VMEM(shape, bf16)
+
+    small = pl.CostEstimate(flops=1024, bytes_accessed=1024, transcendentals=0)
     site_scale = (6.0 * n * SITES) ** (-0.5)
     square = (vector_count, vector_count)
     running = jax.ShapeDtypeStruct((vector_count, 2 * vector_count), f32)
@@ -500,15 +491,52 @@
     def with_partner(part):
         return part, swap(part, 1)
 
-    w_inner, u_inner = smear(smear_inner, (second, across, own), 6, 6, 4, 4, (2, 2))
-    inner = with_partner(w_inner)
-    (sum_inner,) = elemental(None, (inner,), ((0, 0, 2),), (across,), ((0, 0, 2),), ())
-    u_inner, sum_inner = lax.optimization_barrier((u_inner, sum_inner))
     short = jax.ShapeDtypeStruct((FIELD, vector_count), f32)
     after_shape = jax.ShapeDtypeStruct((2 * FIELD, FIELD), bf16)
-    w_middle, first_short, second_short, after = smear(
-        smear_middle, (across, own, first, u_inner), 4, 5, 4, 4, (2,), (short, short, after_shape)
-    )
+    within_shape = jax.ShapeDtypeStruct((2 * FIELD, 2 * FIELD), bf16)
+    w_inner, u_inner, operator = pl.pallas_call(
+        smear_inner,
+        out_shape=(field(2), field(2), jax.ShapeDtypeStruct((2 * FIELD, 3 * FIELD), bf16)),
+        in_specs=[anywhere] * 3,
+        out_specs=(vmem,) * 3,
+        scratch_shapes=[
+            scratch(6, FIELD, vector_count),
+            scratch(6, PACKED_LINKS, 2 * SITES),
+            scratch(4, FIELD, vector_count),
+            scratch(3, 2 * FIELD, 3 * FIELD),
+            pltpu.SemaphoreType.DMA((6,)),
+        ],
+        compiler_params=params(24),
+        cost_estimate=small,
+    )(second, across, own)
+    inner = with_partner(w_inner)
+    prepared = pl.pallas_call(
+        smear_prepare,
+        out_shape=(short, short, within_shape),
+        in_specs=[vmem] * 3,
+        out_specs=(vmem,) * 3,
+        scratch_shapes=[scratch(2, PACKED_LINKS, 2 * SITES)],
+        compiler_params=params(12),
+        cost_estimate=small,
+    )(own, u_inner, operator)
+    (sum_inner,) = elemental(None, (inner,), ((0, 0, 2),), (across,), ((0, 0, 2),), ())
+    prepared, sum_inner = lax.optimization_barrier((prepared, sum_inner))
+    w_middle, first_short, second_short, after = pl.pallas_call(
+        smear_middle,
+        out_shape=(field(2), short, short, after_shape),
+        in_specs=[vmem] * 7,
+        out_specs=(vmem,) * 4,
+        scratch_shapes=[
+            scratch(3, FIELD, vector_count),
+            scratch(3, PACKED_LINKS, 2 * SITES),
+            scratch(3, FIELD, vector_count),
+            scratch(2 * FIELD, 3 * FIELD),
+            scratch(2 * FIELD, 2 * FIELD),
+            scratch(2 * FIELD, FIELD),
+        ],
+        compiler_params=params(20),
+        cost_estimate=small,
+    )(own, first, u_inner, operator, *prepared)
     middle = with_partner(w_middle)
     w_outer = pl.pallas_call(
         smear_outer,

time: 66.5 us -> 66.5 us (level)
  waiting for transfers between devices: 29.3 us -> 30.4 us
  starting transfers between devices: 13.3 us -> 12.4 us
    ppermute x1, waiting for transfers between devices: 1.35 us -> 2.59 us  [body(): last = lax.ppermute(edge, 'space', outer)]
    ppermute x10, starting transfers between devices: 8.97 us -> 8.13 us  [swap(): return lax.ppermute(value, 'space', [(i, i ^ bit) for i in range(n)])]
    pallas_call x2 -> x3, Pallas kernels: 8.02 us -> 7.69 us  [the longest x1 4.15 us: body(): pl.pallas_call(smear_inner, out_shape=(field(2), field(2), jax.ShapeDtype...]
where the time goes in v6:
time: 66.5 us; the launch traced here: 66.2 us
  waiting for transfers between devices  30.4 us (46%)
  Pallas kernels  20.6 us (31%)
  starting transfers between devices  12.4 us (19%)
  local copies, waits for them, and re-layouts  1.89 us (3%)
  between operations  0.8 us (1%)
    ppermute x10, waiting for transfers between devices, swap(): return lax.ppermute(value, 'space', [(i, i ^ bit) for i in range(n)])  22.9 us
    ppermute x10, starting transfers between devices, swap(): return lax.ppermute(value, 'space', [(i, i ^ bit) for i in range(n)])  8.13 us
    pallas_call x3, Pallas kernels, elemental(): pl.pallas_call(functools.partial(elemental_kernel, scale, vector_pieces,...  6.31 us
    pallas_call x1, Pallas kernels, body(): pl.pallas_call(smear_inner, out_shape=(field(2), field(2), jax.ShapeDtype...  4.15 us
    pallas_call x1, Pallas kernels, body(): pl.pallas_call(functools.partial(pair_kernel, pair_scale), out_shape=(jax...  4.15 us
    ppermute x1, waiting for transfers between devices, body(): second = lax.ppermute(own, 'space', straight)  3.71 us
    ppermute x1, starting transfers between devices, body(): second = lax.ppermute(own, 'space', straight)  3.6 us
    pallas_call x1, Pallas kernels, body(): pl.pallas_call(smear_middle, out_shape=(field(2), short, short, after_sha...  2.63 us
  transfers between devices with their start and end apart: 13, of which 10 were waited for; matrix products, arithmetic and copies ran while one was open for 0% of the time, Pallas kernels for 20%

profile of v6, /device:TPU:0, one launch (start us, length us, event | category | flops | bytes accessed | tf_op | source)
XLA Modules:
  0.0 66.2 jit_solution(14280984493271077849)
XLA Ops:
  0.6 0.0 copy-start.1
  0.6 1.1 %copy-done.1 = bf16[2,2,3,1,128,256]{5,4,3,2,1,0:T(8,128)(2,1)S(1)} copy-done((bf16[2,2,3,1,128,256]{5,4,3,2,1,0:T(8,128)(2,1)S(1)}, bf16[2,2,3,1,128,256]{5,4,3,2,1,0:T(8,128)(2,1)}, u32[]{:S(2)}) %copy-start.1) | copy-done | bytes 786456
  1.8 0.0 copy-start.2
  1.8 0.7 %copy-done.2 = bf16[2,3,2,3,3,1,128]{6,2,5,4,3,1,0:T(2,128)(2,1)S(1)} copy-done((bf16[2,3,2,3,3,1,128]{6,2,5,4,3,1,0:T(2,128)(2,1)S(1)}, bf16[2,3,2,3,3,1,128]{6,2,5,4,3,1,0:T(2,128)(2,1)}, u32[]{:S(2)}) %copy-start.2) | copy-done | bytes 27672
  2.5 0.6 shard_map.68
  3.1 0.5 collective-permute-start
  3.6 1.4 %collective-permute-done.received = bf16[2,416,256]{2,1,0:T(8,128)(2,1)S(1)} collective-permute-done((bf16[2,416,256]{2,1,0:T(8,128)(2,1)S(1)}, bf16[2,416,256]{2,1,0:T(8,128)(2,1)S(1)}, u32[]{:S(2)}, u32[]{:S(2)}) %collective-permute-start) | collective-permute-done | bytes 426016 | tf_op jit(solution)/shard_map/ppermute | solution.py:419
  5.0 0.8 %shard_map.69 = (bf16[2,416,256]{2,1,0:T(8,128)(2,1)S(1)}, bf16[2,416,256]{2,1,0:T(8,128)(2,1)S(1)}, bf16[416,256]{1,0:T(8,128)(2,1)S(1)}) custom-call(bf16[2,416,256]{2,1,0:T(8,128)(2,1)S(1)} %collective-permute-done.received, bf16[2,416,256]{2,1,0:T(8,128)(2,1)S(1)} %get-tuple-element.25.own_in, ...), custom_call_target="tpu_custom_call", output_to_operand_aliasing={{0}: (1, {}), {1}: (2, {})} | custom-call | tf_op jit(solution)/shard_map/pallas_call | solution.py:435
  5.9 3.0 %collective-permute-start.3 = (bf16[2,416,256]{2,1,0:T(8,128)(2,1)S(1)}, bf16[2,416,256]{2,1,0:T(8,128)(2,1)S(1)}, u32[]{:S(2)}, u32[]{:S(2)}) collective-permute-start(bf16[2,416,256]{2,1,0:T(8,128)(2,1)S(1)} %get-tuple-element.28), channel_id=1, source_target_pairs={{0,2},{1,3},{2,0},{3,1},{4,6},{5,7},{6,4},{7,5},{8,10},{9,11},{10,... | collective-permute-start | bytes 1277960 | tf_op jit(solution)/shard_map/ppermute | solution.py:419
  8.8 0.0 copy-start.3
  8.8 3.6 %collective-permute-start.2 = (bf16[2,416,256]{2,1,0:T(8,128)(2,1)S(1)}, bf16[2,416,256]{2,1,0:T(8,128)(2,1)S(1)}, u32[]{:S(2)}, u32[]{:S(2)}) collective-permute-start(bf16[2,416,256]{2,1,0:T(8,128)(2,1)S(1)} %get-tuple-element.27.own.refs_5_.refs_4_), channel_id=1, source_target_pairs={{2,6},{0,12},{3,7},{1,13},{6,10},{4,0},{7,11},{5,1},{10,14},{8,4},... | collective-permute-start | bytes 1277960 | tf_op jit(solution)/shard_map/ppermute | solution.py:454
  12.4 0.0 collective-permute-start.1
  12.4 6.5 %collective-permute-done.3.across.refs_2_.refs_4_ = bf16[2,416,256]{2,1,0:T(8,128)(2,1)S(1)} collective-permute-done((bf16[2,416,256]{2,1,0:T(8,128)(2,1)S(1)}, bf16[2,416,256]{2,1,0:T(8,128)(2,1)S(1)}, u32[]{:S(2)}, u32[]{:S(2)}) %collective-permute-start.3) | collective-permute-done | bytes 426016 | tf_op jit(solution)/shard_map/ppermute | solution.py:419
  18.9 3.7 %collective-permute-done.2.second = bf16[2,416,256]{2,1,0:T(8,128)(2,1)S(1)} collective-permute-done((bf16[2,416,256]{2,1,0:T(8,128)(2,1)S(1)}, bf16[2,416,256]{2,1,0:T(8,128)(2,1)S(1)}, u32[]{:S(2)}, u32[]{:S(2)}) %collective-permute-start.2) | collective-permute-done | bytes 426016 | tf_op jit(solution)/shard_map/ppermute | solution.py:454
  22.6 4.2 %shard_map.70 = (bf16[2,384,256]{2,1,0:T(8,128)(2,1)S(1)}, bf16[2,384,256]{2,1,0:T(8,128)(2,1)S(1)}, bf16[768,1152]{1,0:T(8,128)(2,1)S(1)}) custom-call(bf16[2,416,256]{2,1,0:T(8,128)(2,1)S(1)} %collective-permute-done.2.second, bf16[2,416,256]{2,1,0:T(8,128)(2,1)S(1)} %collective-permute-done.3.across.refs_2_.refs_4_, ...), custom_call_target="tpu_custom_call" | custom-call | flops 1024 | bytes 1024 | tf_op jit(solution)/shard_map/pallas_call | solution.py:497
  26.8 0.1 collective-permute-start.4
  26.9 0.7 %collective-permute-start.5 = (bf16[416,256]{1,0:T(8,128)(2,1)S(1)}, bf16[416,256]{1,0:T(8,128)(2,1)S(1)}, u32[]{:S(2)}, u32[]{:S(2)}) collective-permute-start(bf16[416,256]{1,0:T(8,128)(2,1)S(1)} %get-tuple-element.39), channel_id=1, source_target_pairs={{0,4},{2,14},{1,5},{3,15},{4,8},{6,2},{5,9},{7,3},{8,12},{10,6},{9... | collective-permute-start | bytes 638984 | tf_op jit(solution)/shard_map/ppermute | solution.py:456
  27.6 0.9 %shard_map.71 = (f32[384,256]{1,0:T(8,128)S(1)}, f32[384,256]{1,0:T(8,128)S(1)}, bf16[768,768]{1,0:T(8,128)(2,1)S(1)}) custom-call(bf16[2,416,256]{2,1,0:T(8,128)(2,1)S(1)} %get-tuple-element.27.own.refs_5_.refs_4_, bf16[2,384,256]{2,1,0:T(8,128)(2,1)S(1)} %get-tuple-element.29.u_in, bf16[768,1152]{1,0:T(8,128)(2,1)S(1)} %get-tuple-element.30.operator.operator_in), custom_call_target="tpu_custom_call" | custom-call | flops 1024 | bytes 1024 | tf_op jit(solution)/shard_map/pallas_call | solution.py:513
  28.5 0.1 collective-permute-done.4.refs_1_.refs_2_
  28.6 0.0 copy-done.3
  28.6 1.9 %shard_map.72.refs_6_ = f32[256,512]{1,0:T(8,128)S(1)} custom-call(s32[2]{0:T(128)S(1)} %copy-done.3, bf16[2,384,256]{2,1,0:T(8,128)(2,1)S(1)} %get-tuple-element.34.refs_0_, bf16[2,384,256]{2,1,0:T(8,128)(2,1)S(1)} %collective-permute-done.4.refs_1_.refs_2_, bf16[2,416,256]{2,1,0:T(8,128)(2,1)S(1)} %collective-permute-done.3.across.refs_2_.refs_4_), custom_call_target="tpu_custom_call" | custom-call | flops 1024 | bytes 1024 | tf_op jit(solution)/shard_map/pallas_call | solution.py:477
  30.5 1.2 %collective-permute-done.1.first.refs_5_ = bf16[2,416,256]{2,1,0:T(8,128)(2,1)S(1)} collective-permute-done((bf16[2,416,256]{2,1,0:T(8,128)(2,1)S(1)}, bf16[2,416,256]{2,1,0:T(8,128)(2,1)S(1)}, u32[]{:S(2)}, u32[]{:S(2)}) %collective-permute-start.1) | collective-permute-done | bytes 426016 | tf_op jit(solution)/shard_map/ppermute | solution.py:455
  31.8 2.6 %shard_map.73 = (bf16[2,384,256]{2,1,0:T(8,128)(2,1)S(1)}, f32[384,256]{1,0:T(8,128)S(1)}, f32[384,256]{1,0:T(8,128)S(1)}, bf16[768,384]{1,0:T(8,128)(2,1)S(1)}) custom-call(bf16[2,416,256]{2,1,0:T(8,128)(2,1)S(1)} %get-tuple-element.27.own.refs_5_.refs_4_, bf16[2,416,256]{2,1,0:T(8,128)(2,1)S(1)} %collective-permute-done.1.first.refs_5_, ...), custom_call_target="tpu_custom_call" | custom-call | flops 1024 | bytes 1024 | tf_op jit(solution)/shard_map/pallas_call | solution.py:524
  34.4 0.1 collective-permute-start.6
  34.5 2.6 %collective-permute-done.5.last = bf16[416,256]{1,0:T(8,128)(2,1)S(1)} collective-permute-done((bf16[416,256]{1,0:T(8,128)(2,1)S(1)}, bf16[416,256]{1,0:T(8,128)(2,1)S(1)}, u32[]{:S(2)}, u32[]{:S(2)}) %collective-permute-start.5) | collective-permute-done | bytes 213024 | tf_op jit(solution)/shard_map/ppermute | solution.py:456
  37.1 1.1 %shard_map.74.refs_1_ = bf16[1,384,256]{2,1,0:T(8,128)(2,1)S(1)} custom-call(bf16[2,416,256]{2,1,0:T(8,128)(2,1)S(1)} %collective-permute-done.1.first.refs_5_, bf16[416,256]{1,0:T(8,128)(2,1)S(1)} %collective-permute-done.5.last, f32[384,256]{1,0:T(8,128)S(1)} %get-tuple-element.40.first_short, f32[384,256]{1,0:T(8,128)S(1)} %get-tuple-element.41.second_short, ...), custom_call_target="tpu_custom_call" | custom-call | flops 1024 | bytes 1024 | tf_op jit(solution)/shard_map/pallas_call | solution.py:541
  38.1 0.1 collective-permute-start.7
  38.2 0.0 collective-permute-done.6.refs_3_.refs_2_
  38.2 2.3 %shard_map.75.refs_6_ = f32[256,512]{1,0:T(8,128)S(1)} custom-call(s32[2]{0:T(128)S(1)} %copy-done.3, bf16[2,384,256]{2,1,0:T(8,128)(2,1)S(1)} %get-tuple-element.34.refs_0_, bf16[2,384,256]{2,1,0:T(8,128)(2,1)S(1)} %get-tuple-element.38.refs_1_.refs_0_, bf16[2,384,256]{2,1,0:T(8,128)(2,1)S(1)} %collective-permute-done.4.refs_1_.refs_2_, ...), custom_call_target="tpu_custom_call" | custom-call | flops 1024 | bytes 1024 | tf_op jit(solution)/shard_map/pallas_call | solution.py:477
  40.5 0.0 copy-start
  40.5 0.0 copy-start.4
  40.5 0.0 collective-permute-done.7.refs_3_
  40.5 2.1 %shard_map.76 = (f32[256,256]{1,0:T(8,128)S(1)}, bf16[256,256]{1,0:T(8,128)(2,1)S(1)}) custom-call(s32[2]{0:T(128)S(1)} %copy-done.3, bf16[2,384,256]{2,1,0:T(8,128)(2,1)S(1)} %get-tuple-element.38.refs_1_.refs_0_, bf16[1,384,256]{2,1,0:T(8,128)(2,1)S(1)} %shard_map.74.refs_1_, bf16[2,384,256]{2,1,0:T(8,128)(2,1)S(1)} %collective-permute-done.6.refs_3_.refs_2_, ...), custom_call_target="tpu_custom_call" | custom-call | flops 1024 | bytes 1024 | tf_op jit(solution)/shard_map/pallas_call | solution.py:477
  42.6 2.7 %collective-permute-start.8 = (bf16[256,256]{1,0:T(8,128)(2,1)S(1)}, bf16[256,256]{1,0:T(8,128)(2,1)S(1)}, u32[]{:S(2)}, u32[]{:S(2)}) collective-permute-start(bf16[256,256]{1,0:T(8,128)(2,1)S(1)} %get-tuple-element.45), channel_id=1, source_target_pairs={{0,12},{1,13},{2,14},{3,15},{4,8},{5,9},{6,10},{7,11},{8,4},{9,5},... | collective-permute-start | bytes 393224 | tf_op jit(solution)/shard_map/ppermute | solution.py:419
  45.4 5.1 %collective-permute-done.8 = bf16[256,256]{1,0:T(8,128)(2,1)S(1)} collective-permute-done((bf16[256,256]{1,0:T(8,128)(2,1)S(1)}, bf16[256,256]{1,0:T(8,128)(2,1)S(1)}, u32[]{:S(2)}, u32[]{:S(2)}) %collective-permute-start.8) | collective-permute-done | bytes 131104 | tf_op jit(solution)/shard_map/ppermute | solution.py:419
  50.5 1.6 %collective-permute-start.9 = (bf16[256,256]{1,0:T(8,128)(2,1)S(1)}, bf16[256,256]{1,0:T(8,128)(2,1)S(1)}, u32[]{:S(2)}, u32[]{:S(2)}) collective-permute-start(bf16[256,256]{1,0:T(8,128)(2,1)S(1)} %fusion), channel_id=1, source_target_pairs={{0,4},{1,5},{2,6},{3,7},{4,0},{5,1},{6,2},{7,3},{8,12},{9,13},{10,... | collective-permute-start | bytes 393224 | tf_op jit(solution)/shard_map/ppermute | solution.py:419
  52.1 3.5 %collective-permute-done.9 = bf16[256,256]{1,0:T(8,128)(2,1)S(1)} collective-permute-done((bf16[256,256]{1,0:T(8,128)(2,1)S(1)}, bf16[256,256]{1,0:T(8,128)(2,1)S(1)}, u32[]{:S(2)}, u32[]{:S(2)}) %collective-permute-start.9) | collective-permute-done | bytes 131104 | tf_op jit(solution)/shard_map/ppermute | solution.py:419
  55.6 0.1 add_convert_fusion.s00
  55.7 0.1 collective-permute-start.10
  55.8 0.1 collective-permute-start.11
  55.9 4.9 %collective-permute-done.10.s10 = bf16[256,256]{1,0:T(8,128)(2,1)S(1)} collective-permute-done((bf16[256,256]{1,0:T(8,128)(2,1)S(1)}, bf16[256,256]{1,0:T(8,128)(2,1)S(1)}, u32[]{:S(2)}, u32[]{:S(2)}) %collective-permute-start.10) | collective-permute-done | bytes 131104 | tf_op jit(solution)/shard_map/ppermute | solution.py:419
  60.7 0.0 collective-permute-start.12
  60.7 0.0 collective-permute-done.11.s01
  60.7 1.3 %collective-permute-done.12.s11 = bf16[256,256]{1,0:T(8,128)(2,1)S(1)} collective-permute-done((bf16[256,256]{1,0:T(8,128)(2,1)S(1)}, bf16[256,256]{1,0:T(8,128)(2,1)S(1)}, u32[]{:S(2)}, u32[]{:S(2)}) %collective-permute-start.12) | collective-permute-done | bytes 131104 | tf_op jit(solution)/shard_map/ppermute | solution.py:419
  62.1 0.0 copy-done
  62.1 0.0 copy-done.4
  62.1 4.1 %shard_map.77 = (f32[2,2,2,16,256]{4,3,2,1,0:T(8,128)}, bf16[4,2,256,256]{3,2,1,0:T(8,128)(2,1)}) custom-call(s32[2,4]{1,0:T(2,128)S(1)} %bitcast.3, bf16[256,256]{1,0:T(8,128)(2,1)S(1)} %add_convert_fusion.s00, bf16[256,256]{1,0:T(8,128)(2,1)S(1)} %collective-permute-done.10.s10, bf16[256,256]{1,0:T(8,128)(2,1)S(1)} %collective-permute-done.11.s01, ...), custom_call_target="tpu_custom_call" | custom-call | tf_op jit(solution)/shard_map/pallas_call | solution.py:574
  (1 shorter events, 0.0 us)
Async XLA Ops:
  0.6 1.1 %copy-start.1 = (bf16[2,2,3,1,128,256]{5,4,3,2,1,0:T(8,128)(2,1)S(1)}, bf16[2,2,3,1,128,256]{5,4,3,2,1,0:T(8,128)(2,1)}, u32[]{:S(2)}) copy-start(bf16[2,2,3,1,128,256]{5,4,3,2,1,0:T(8,128)(2,1)} %vectors.1) | copy-start | bytes 2359300
  1.8 0.7 %copy-start.2 = (bf16[2,3,2,3,3,1,128]{6,2,5,4,3,1,0:T(2,128)(2,1)S(1)}, bf16[2,3,2,3,3,1,128]{6,2,5,4,3,1,0:T(2,128)(2,1)}, u32[]{:S(2)}) copy-start(bf16[2,3,2,3,3,1,128]{6,2,5,4,3,1,0:T(2,128)(2,1)} %param.6) | copy-start | bytes 82948
  3.1 1.9 %collective-permute-start = (bf16[2,416,256]{2,1,0:T(8,128)(2,1)S(1)}, bf16[2,416,256]{2,1,0:T(8,128)(2,1)S(1)}, u32[]{:S(2)}, u32[]{:S(2)}) collective-permute-start(bf16[2,416,256]{2,1,0:T(8,128)(2,1)S(1)} %get-tuple-element.24), channel_id=1, source_target_pairs={{0,1},{1,0},{2,3},{3,2},{4,5},{5,4},{6,7},{7,6},{8,9},{9,8},{10,11... | collective-permute-start | bytes 1277960 | tf_op jit(solution)/shard_map/ppermute | solution.py:419
  5.9 13.1 %collective-permute-start.3 = (bf16[2,416,256]{2,1,0:T(8,128)(2,1)S(1)}, bf16[2,416,256]{2,1,0:T(8,128)(2,1)S(1)}, u32[]{:S(2)}, u32[]{:S(2)}) collective-permute-start(bf16[2,416,256]{2,1,0:T(8,128)(2,1)S(1)} %get-tuple-element.28), channel_id=1, source_target_pairs={{0,2},{1,3},{2,0},{3,1},{4,6},{5,7},{6,4},{7,5},{8,10},{9,11},{10,... | collective-permute-start | bytes 1277960 | tf_op jit(solution)/shard_map/ppermute | solution.py:419
  8.8 19.8 %copy-start.3 = (s32[2]{0:T(128)S(1)}, s32[2]{0:T(128)}, u32[]{:S(2)}) copy-start(s32[2]{0:T(128)} %directions.5) | copy-start | bytes 28
  8.8 13.8 %collective-permute-start.2 = (bf16[2,416,256]{2,1,0:T(8,128)(2,1)S(1)}, bf16[2,416,256]{2,1,0:T(8,128)(2,1)S(1)}, u32[]{:S(2)}, u32[]{:S(2)}) collective-permute-start(bf16[2,416,256]{2,1,0:T(8,128)(2,1)S(1)} %get-tuple-element.27.own.refs_5_.refs_4_), channel_id=1, source_target_pairs={{2,6},{0,12},{3,7},{1,13},{6,10},{4,0},{7,11},{5,1},{10,14},{8,4},... | collective-permute-start | bytes 1277960 | tf_op jit(solution)/shard_map/ppermute | solution.py:454
  12.4 19.4 %collective-permute-start.1 = (bf16[2,416,256]{2,1,0:T(8,128)(2,1)S(1)}, bf16[2,416,256]{2,1,0:T(8,128)(2,1)S(1)}, u32[]{:S(2)}, u32[]{:S(2)}) collective-permute-start(bf16[2,416,256]{2,1,0:T(8,128)(2,1)S(1)} %get-tuple-element.28), channel_id=1, source_target_pairs={{2,4},{0,14},{3,5},{1,15},{6,8},{4,2},{7,9},{5,3},{10,12},{8,6},{1... | collective-permute-start | bytes 1277960 | tf_op jit(solution)/shard_map/ppermute | solution.py:455
  26.8 1.8 %collective-permute-start.4 = (bf16[2,384,256]{2,1,0:T(8,128)(2,1)S(1)}, bf16[2,384,256]{2,1,0:T(8,128)(2,1)S(1)}, u32[]{:S(2)}, u32[]{:S(2)}) collective-permute-start(bf16[2,384,256]{2,1,0:T(8,128)(2,1)S(1)} %get-tuple-element.34.refs_0_), channel_id=1, source_target_pairs={{0,1},{1,0},{2,3},{3,2},{4,5},{5,4},{6,7},{7,6},{8,9},{9,8},{10,11... | collective-permute-start | bytes 1179656 | tf_op jit(solution)/shard_map/ppermute | solution.py:419
  26.9 10.2 %collective-permute-start.5 = (bf16[416,256]{1,0:T(8,128)(2,1)S(1)}, bf16[416,256]{1,0:T(8,128)(2,1)S(1)}, u32[]{:S(2)}, u32[]{:S(2)}) collective-permute-start(bf16[416,256]{1,0:T(8,128)(2,1)S(1)} %get-tuple-element.39), channel_id=1, source_target_pairs={{0,4},{2,14},{1,5},{3,15},{4,8},{6,2},{5,9},{7,3},{8,12},{10,6},{9... | collective-permute-start | bytes 638984 | tf_op jit(solution)/shard_map/ppermute | solution.py:456
  34.4 3.8 %collective-permute-start.6 = (bf16[2,384,256]{2,1,0:T(8,128)(2,1)S(1)}, bf16[2,384,256]{2,1,0:T(8,128)(2,1)S(1)}, u32[]{:S(2)}, u32[]{:S(2)}) collective-permute-start(bf16[2,384,256]{2,1,0:T(8,128)(2,1)S(1)} %get-tuple-element.38.refs_1_.refs_0_), channel_id=1, source_target_pairs={{0,1},{1,0},{2,3},{3,2},{4,5},{5,4},{6,7},{7,6},{8,9},{9,8},{10,11... | collective-permute-start | bytes 1179656 | tf_op jit(solution)/shard_map/ppermute | solution.py:419
  38.1 2.4 %collective-permute-start.7 = (bf16[1,384,256]{2,1,0:T(8,128)(2,1)S(1)}, bf16[1,384,256]{2,1,0:T(8,128)(2,1)S(1)}, u32[]{:S(2)}, u32[]{:S(2)}) collective-permute-start(bf16[1,384,256]{2,1,0:T(8,128)(2,1)S(1)} %shard_map.74.refs_1_), channel_id=1, source_target_pairs={{0,1},{1,0},{2,3},{3,2},{4,5},{5,4},{6,7},{7,6},{8,9},{9,8},{10,11... | collective-permute-start | bytes 589832 | tf_op jit(solution)/shard_map/ppermute | solution.py:419
  40.5 21.6 %copy-start = (bf16[4,2,256,256]{3,2,1,0:T(8,128)(2,1)S(1)}, bf16[4,2,256,256]{3,2,1,0:T(8,128)(2,1)}, u32[]{:S(2)}) copy-start(bf16[4,2,256,256]{3,2,1,0:T(8,128)(2,1)} %perambulators.1) | copy-start | bytes 3145732
  40.5 21.6 %copy-start.4 = (s32[4,2]{0,1:T(2,128)S(1)}, s32[4,2]{0,1:T(2,128)}, u32[]{:S(2)}) copy-start(s32[4,2]{0,1:T(2,128)} %param.8) | copy-start | bytes 100
  42.6 7.9 %collective-permute-start.8 = (bf16[256,256]{1,0:T(8,128)(2,1)S(1)}, bf16[256,256]{1,0:T(8,128)(2,1)S(1)}, u32[]{:S(2)}, u32[]{:S(2)}) collective-permute-start(bf16[256,256]{1,0:T(8,128)(2,1)S(1)} %get-tuple-element.45), channel_id=1, source_target_pairs={{0,12},{1,13},{2,14},{3,15},{4,8},{5,9},{6,10},{7,11},{8,4},{9,5},... | collective-permute-start | bytes 393224 | tf_op jit(solution)/shard_map/ppermute | solution.py:419
  50.5 5.1 %collective-permute-start.9 = (bf16[256,256]{1,0:T(8,128)(2,1)S(1)}, bf16[256,256]{1,0:T(8,128)(2,1)S(1)}, u32[]{:S(2)}, u32[]{:S(2)}) collective-permute-start(bf16[256,256]{1,0:T(8,128)(2,1)S(1)} %fusion), channel_id=1, source_target_pairs={{0,4},{1,5},{2,6},{3,7},{4,0},{5,1},{6,2},{7,3},{8,12},{9,13},{10,... | collective-permute-start | bytes 393224 | tf_op jit(solution)/shard_map/ppermute | solution.py:419
  55.7 5.0 %collective-permute-start.10 = (bf16[256,256]{1,0:T(8,128)(2,1)S(1)}, bf16[256,256]{1,0:T(8,128)(2,1)S(1)}, u32[]{:S(2)}, u32[]{:S(2)}) collective-permute-start(bf16[256,256]{1,0:T(8,128)(2,1)S(1)} %add_convert_fusion.s00), channel_id=1, source_target_pairs={{0,2},{1,3},{2,0},{3,1},{4,6},{5,7},{6,4},{7,5},{8,10},{9,11},{10,... | collective-permute-start | bytes 393224 | tf_op jit(solution)/shard_map/ppermute | solution.py:419
  55.8 5.0 %collective-permute-start.11 = (bf16[256,256]{1,0:T(8,128)(2,1)S(1)}, bf16[256,256]{1,0:T(8,128)(2,1)S(1)}, u32[]{:S(2)}, u32[]{:S(2)}) collective-permute-start(bf16[256,256]{1,0:T(8,128)(2,1)S(1)} %add_convert_fusion.s00), channel_id=1, source_target_pairs={{0,1},{1,0},{2,3},{3,2},{4,5},{5,4},{6,7},{7,6},{8,9},{9,8},{10,11... | collective-permute-start | bytes 393224 | tf_op jit(solution)/shard_map/ppermute | solution.py:419
  60.7 1.3 %collective-permute-start.12 = (bf16[256,256]{1,0:T(8,128)(2,1)S(1)}, bf16[256,256]{1,0:T(8,128)(2,1)S(1)}, u32[]{:S(2)}, u32[]{:S(2)}) collective-permute-start(bf16[256,256]{1,0:T(8,128)(2,1)S(1)} %collective-permute-done.10.s10), channel_id=1, source_target_pairs={{0,1},{1,0},{2,3},{3,2},{4,5},{5,4},{6,7},{7,6},{8,9},{9,8},{10,11... | collective-permute-start | bytes 393224 | tf_op jit(solution)/shard_map/ppermute | solution.py:419

commit v7 on v6

--- a/solution.py
+++ b/solution.py
@@ -380,21 +380,22 @@
         right[t, size:, :size] = -imag
         right[t, size:, size:] = real
 
-    for p in range(perambulators.shape[0]):
-        source, sink = pairs[0, p], pairs[1, p]
+    count = perambulators.shape[0]
+    wide = []
+    for p in range(count):
         propagator = perambulators[p].reshape(2 * size, size)
-        first = jnp.dot(left[sink], propagator, preferred_element_type=f32).astype(bf16)
-        wide = jnp.concatenate([first[:size], first[size:]], axis=1)
-        second = (
-            jnp.dot(wide, right[source], preferred_element_type=f32) * pair_scale
-        ).astype(bf16)
+        first = jnp.dot(left[pairs[1, p]], propagator, preferred_element_type=f32).astype(bf16)
+        wide.append(jnp.concatenate([first[:size], first[size:]], axis=1))
+    both = []
+    for p in range(count):
+        second = jnp.dot(wide[p], right[pairs[0, p]], preferred_element_type=f32) * pair_scale
+        second = second.astype(bf16)
         real, imag = second[:, :size], second[:, size:]
-        both = jnp.concatenate(
-            [second, jnp.concatenate([imag, -real], axis=1)], axis=0
-        )
-        turned = jnp.concatenate([propagator[:size], propagator[size:]], axis=1)
+        both.append(jnp.concatenate([second, jnp.concatenate([imag, -real], axis=1)], axis=0))
+    for p in range(count):
+        turned = jnp.concatenate([perambulators[p, 0], perambulators[p, 1]], axis=1)
         third = lax.dot_general(
-            both, turned, (((1,), (1,)), ((), ())), preferred_element_type=f32
+            both[p], turned, (((1,), (1,)), ((), ())), preferred_element_type=f32
         ).astype(bf16)
         out[p] = third.reshape(2, size, size)
 

time: 66.5 us -> 66 us (level)
  no operation moved by 1% of the time
where the time goes in v7:
time: 66 us; the launch traced here: 65.8 us
  waiting for transfers between devices  30.4 us (46%)
  Pallas kernels  20.1 us (30%)
  starting transfers between devices  12.4 us (19%)
  local copies, waits for them, and re-layouts  1.89 us (3%)
  between operations  0.8 us (1%)
    ppermute x10, waiting for transfers between devices, swap(): return lax.ppermute(value, 'space', [(i, i ^ bit) for i in range(n)])  22.9 us
    ppermute x10, starting transfers between devices, swap(): return lax.ppermute(value, 'space', [(i, i ^ bit) for i in range(n)])  8.13 us
    pallas_call x3, Pallas kernels, elemental(): pl.pallas_call(functools.partial(elemental_kernel, scale, vector_pieces,...  6.31 us
    pallas_call x1, Pallas kernels, body(): pl.pallas_call(smear_inner, out_shape=(field(2), field(2), jax.ShapeDtype...  4.15 us
    ppermute x1, waiting for transfers between devices, body(): second = lax.ppermute(own, 'space', straight)  3.71 us
    pallas_call x1, Pallas kernels, body(): pl.pallas_call(functools.partial(pair_kernel, pair_scale), out_shape=(jax...  3.69 us
    ppermute x1, starting transfers between devices, body(): second = lax.ppermute(own, 'space', straight)  3.6 us
    pallas_call x1, Pallas kernels, body(): pl.pallas_call(smear_middle, out_shape=(field(2), short, short, after_sha...  2.63 us
  transfers between devices with their start and end apart: 13, of which 10 were waited for; matrix products, arithmetic and copies ran while one was open for 0% of the time, Pallas kernels for 20%

profile of v7, /device:TPU:0, one launch (start us, length us, event | category | flops | bytes accessed | tf_op | source)
XLA Modules:
  0.0 65.8 jit_solution(10416205404328275804)
XLA Ops:
  0.6 0.0 copy-start.1
  0.6 1.1 %copy-done.1 = bf16[2,2,3,1,128,256]{5,4,3,2,1,0:T(8,128)(2,1)S(1)} copy-done((bf16[2,2,3,1,128,256]{5,4,3,2,1,0:T(8,128)(2,1)S(1)}, bf16[2,2,3,1,128,256]{5,4,3,2,1,0:T(8,128)(2,1)}, u32[]{:S(2)}) %copy-start.1) | copy-done | bytes 786456
  1.8 0.0 copy-start.2
  1.8 0.7 %copy-done.2 = bf16[2,3,2,3,3,1,128]{6,2,5,4,3,1,0:T(2,128)(2,1)S(1)} copy-done((bf16[2,3,2,3,3,1,128]{6,2,5,4,3,1,0:T(2,128)(2,1)S(1)}, bf16[2,3,2,3,3,1,128]{6,2,5,4,3,1,0:T(2,128)(2,1)}, u32[]{:S(2)}) %copy-start.2) | copy-done | bytes 27672
  2.5 0.6 shard_map.68
  3.1 0.5 collective-permute-start
  3.6 1.4 %collective-permute-done.received = bf16[2,416,256]{2,1,0:T(8,128)(2,1)S(1)} collective-permute-done((bf16[2,416,256]{2,1,0:T(8,128)(2,1)S(1)}, bf16[2,416,256]{2,1,0:T(8,128)(2,1)S(1)}, u32[]{:S(2)}, u32[]{:S(2)}) %collective-permute-start) | collective-permute-done | bytes 426016 | tf_op jit(solution)/shard_map/ppermute | solution.py:420
  5.0 0.8 %shard_map.69 = (bf16[2,416,256]{2,1,0:T(8,128)(2,1)S(1)}, bf16[2,416,256]{2,1,0:T(8,128)(2,1)S(1)}, bf16[416,256]{1,0:T(8,128)(2,1)S(1)}) custom-call(bf16[2,416,256]{2,1,0:T(8,128)(2,1)S(1)} %collective-permute-done.received, bf16[2,416,256]{2,1,0:T(8,128)(2,1)S(1)} %get-tuple-element.25.own_in, ...), custom_call_target="tpu_custom_call", output_to_operand_aliasing={{0}: (1, {}), {1}: (2, {})} | custom-call | tf_op jit(solution)/shard_map/pallas_call | solution.py:436
  5.9 3.0 %collective-permute-start.3 = (bf16[2,416,256]{2,1,0:T(8,128)(2,1)S(1)}, bf16[2,416,256]{2,1,0:T(8,128)(2,1)S(1)}, u32[]{:S(2)}, u32[]{:S(2)}) collective-permute-start(bf16[2,416,256]{2,1,0:T(8,128)(2,1)S(1)} %get-tuple-element.28), channel_id=1, source_target_pairs={{0,2},{1,3},{2,0},{3,1},{4,6},{5,7},{6,4},{7,5},{8,10},{9,11},{10,... | collective-permute-start | bytes 1277960 | tf_op jit(solution)/shard_map/ppermute | solution.py:420
  8.8 0.0 copy-start.3
  8.8 3.6 %collective-permute-start.2 = (bf16[2,416,256]{2,1,0:T(8,128)(2,1)S(1)}, bf16[2,416,256]{2,1,0:T(8,128)(2,1)S(1)}, u32[]{:S(2)}, u32[]{:S(2)}) collective-permute-start(bf16[2,416,256]{2,1,0:T(8,128)(2,1)S(1)} %get-tuple-element.27.own.refs_5_.refs_4_), channel_id=1, source_target_pairs={{2,6},{0,12},{3,7},{1,13},{6,10},{4,0},{7,11},{5,1},{10,14},{8,4},... | collective-permute-start | bytes 1277960 | tf_op jit(solution)/shard_map/ppermute | solution.py:455
  12.4 0.0 collective-permute-start.1
  12.4 6.5 %collective-permute-done.3.across.refs_2_.refs_4_ = bf16[2,416,256]{2,1,0:T(8,128)(2,1)S(1)} collective-permute-done((bf16[2,416,256]{2,1,0:T(8,128)(2,1)S(1)}, bf16[2,416,256]{2,1,0:T(8,128)(2,1)S(1)}, u32[]{:S(2)}, u32[]{:S(2)}) %collective-permute-start.3) | collective-permute-done | bytes 426016 | tf_op jit(solution)/shard_map/ppermute | solution.py:420
  18.9 3.7 %collective-permute-done.2.second = bf16[2,416,256]{2,1,0:T(8,128)(2,1)S(1)} collective-permute-done((bf16[2,416,256]{2,1,0:T(8,128)(2,1)S(1)}, bf16[2,416,256]{2,1,0:T(8,128)(2,1)S(1)}, u32[]{:S(2)}, u32[]{:S(2)}) %collective-permute-start.2) | collective-permute-done | bytes 426016 | tf_op jit(solution)/shard_map/ppermute | solution.py:455
  22.6 4.2 %shard_map.70 = (bf16[2,384,256]{2,1,0:T(8,128)(2,1)S(1)}, bf16[2,384,256]{2,1,0:T(8,128)(2,1)S(1)}, bf16[768,1152]{1,0:T(8,128)(2,1)S(1)}) custom-call(bf16[2,416,256]{2,1,0:T(8,128)(2,1)S(1)} %collective-permute-done.2.second, bf16[2,416,256]{2,1,0:T(8,128)(2,1)S(1)} %collective-permute-done.3.across.refs_2_.refs_4_, ...), custom_call_target="tpu_custom_call" | custom-call | flops 1024 | bytes 1024 | tf_op jit(solution)/shard_map/pallas_call | solution.py:498
  26.8 0.1 collective-permute-start.4
  26.9 0.7 %collective-permute-start.5 = (bf16[416,256]{1,0:T(8,128)(2,1)S(1)}, bf16[416,256]{1,0:T(8,128)(2,1)S(1)}, u32[]{:S(2)}, u32[]{:S(2)}) collective-permute-start(bf16[416,256]{1,0:T(8,128)(2,1)S(1)} %get-tuple-element.39), channel_id=1, source_target_pairs={{0,4},{2,14},{1,5},{3,15},{4,8},{6,2},{5,9},{7,3},{8,12},{10,6},{9... | collective-permute-start | bytes 638984 | tf_op jit(solution)/shard_map/ppermute | solution.py:457
  27.6 0.9 %shard_map.71 = (f32[384,256]{1,0:T(8,128)S(1)}, f32[384,256]{1,0:T(8,128)S(1)}, bf16[768,768]{1,0:T(8,128)(2,1)S(1)}) custom-call(bf16[2,416,256]{2,1,0:T(8,128)(2,1)S(1)} %get-tuple-element.27.own.refs_5_.refs_4_, bf16[2,384,256]{2,1,0:T(8,128)(2,1)S(1)} %get-tuple-element.29.u_in, bf16[768,1152]{1,0:T(8,128)(2,1)S(1)} %get-tuple-element.30.operator.operator_in), custom_call_target="tpu_custom_call" | custom-call | flops 1024 | bytes 1024 | tf_op jit(solution)/shard_map/pallas_call | solution.py:514
  28.5 0.1 collective-permute-done.4.refs_1_.refs_2_
  28.6 0.0 copy-done.3
  28.6 1.9 %shard_map.72.refs_6_ = f32[256,512]{1,0:T(8,128)S(1)} custom-call(s32[2]{0:T(128)S(1)} %copy-done.3, bf16[2,384,256]{2,1,0:T(8,128)(2,1)S(1)} %get-tuple-element.34.refs_0_, bf16[2,384,256]{2,1,0:T(8,128)(2,1)S(1)} %collective-permute-done.4.refs_1_.refs_2_, bf16[2,416,256]{2,1,0:T(8,128)(2,1)S(1)} %collective-permute-done.3.across.refs_2_.refs_4_), custom_call_target="tpu_custom_call" | custom-call | flops 1024 | bytes 1024 | tf_op jit(solution)/shard_map/pallas_call | solution.py:478
  30.5 1.2 %collective-permute-done.1.first.refs_5_ = bf16[2,416,256]{2,1,0:T(8,128)(2,1)S(1)} collective-permute-done((bf16[2,416,256]{2,1,0:T(8,128)(2,1)S(1)}, bf16[2,416,256]{2,1,0:T(8,128)(2,1)S(1)}, u32[]{:S(2)}, u32[]{:S(2)}) %collective-permute-start.1) | collective-permute-done | bytes 426016 | tf_op jit(solution)/shard_map/ppermute | solution.py:456
  31.8 2.6 %shard_map.73 = (bf16[2,384,256]{2,1,0:T(8,128)(2,1)S(1)}, f32[384,256]{1,0:T(8,128)S(1)}, f32[384,256]{1,0:T(8,128)S(1)}, bf16[768,384]{1,0:T(8,128)(2,1)S(1)}) custom-call(bf16[2,416,256]{2,1,0:T(8,128)(2,1)S(1)} %get-tuple-element.27.own.refs_5_.refs_4_, bf16[2,416,256]{2,1,0:T(8,128)(2,1)S(1)} %collective-permute-done.1.first.refs_5_, ...), custom_call_target="tpu_custom_call" | custom-call | flops 1024 | bytes 1024 | tf_op jit(solution)/shard_map/pallas_call | solution.py:525
  34.4 0.1 collective-permute-start.6
  34.5 2.6 %collective-permute-done.5.last = bf16[416,256]{1,0:T(8,128)(2,1)S(1)} collective-permute-done((bf16[416,256]{1,0:T(8,128)(2,1)S(1)}, bf16[416,256]{1,0:T(8,128)(2,1)S(1)}, u32[]{:S(2)}, u32[]{:S(2)}) %collective-permute-start.5) | collective-permute-done | bytes 213024 | tf_op jit(solution)/shard_map/ppermute | solution.py:457
  37.1 1.1 %shard_map.74.refs_1_ = bf16[1,384,256]{2,1,0:T(8,128)(2,1)S(1)} custom-call(bf16[2,416,256]{2,1,0:T(8,128)(2,1)S(1)} %collective-permute-done.1.first.refs_5_, bf16[416,256]{1,0:T(8,128)(2,1)S(1)} %collective-permute-done.5.last, f32[384,256]{1,0:T(8,128)S(1)} %get-tuple-element.40.first_short, f32[384,256]{1,0:T(8,128)S(1)} %get-tuple-element.41.second_short, ...), custom_call_target="tpu_custom_call" | custom-call | flops 1024 | bytes 1024 | tf_op jit(solution)/shard_map/pallas_call | solution.py:542
  38.1 0.1 collective-permute-start.7
  38.2 0.0 collective-permute-done.6.refs_3_.refs_2_
  38.2 2.3 %shard_map.75.refs_6_ = f32[256,512]{1,0:T(8,128)S(1)} custom-call(s32[2]{0:T(128)S(1)} %copy-done.3, bf16[2,384,256]{2,1,0:T(8,128)(2,1)S(1)} %get-tuple-element.34.refs_0_, bf16[2,384,256]{2,1,0:T(8,128)(2,1)S(1)} %get-tuple-element.38.refs_1_.refs_0_, bf16[2,384,256]{2,1,0:T(8,128)(2,1)S(1)} %collective-permute-done.4.refs_1_.refs_2_, ...), custom_call_target="tpu_custom_call" | custom-call | flops 1024 | bytes 1024 | tf_op jit(solution)/shard_map/pallas_call | solution.py:478
  40.5 0.0 copy-start
  40.5 0.0 copy-start.4
  40.5 0.0 collective-permute-done.7.refs_3_
  40.5 2.1 %shard_map.76 = (f32[256,256]{1,0:T(8,128)S(1)}, bf16[256,256]{1,0:T(8,128)(2,1)S(1)}) custom-call(s32[2]{0:T(128)S(1)} %copy-done.3, bf16[2,384,256]{2,1,0:T(8,128)(2,1)S(1)} %get-tuple-element.38.refs_1_.refs_0_, bf16[1,384,256]{2,1,0:T(8,128)(2,1)S(1)} %shard_map.74.refs_1_, bf16[2,384,256]{2,1,0:T(8,128)(2,1)S(1)} %collective-permute-done.6.refs_3_.refs_2_, ...), custom_call_target="tpu_custom_call" | custom-call | flops 1024 | bytes 1024 | tf_op jit(solution)/shard_map/pallas_call | solution.py:478
  42.6 2.7 %collective-permute-start.8 = (bf16[256,256]{1,0:T(8,128)(2,1)S(1)}, bf16[256,256]{1,0:T(8,128)(2,1)S(1)}, u32[]{:S(2)}, u32[]{:S(2)}) collective-permute-start(bf16[256,256]{1,0:T(8,128)(2,1)S(1)} %get-tuple-element.45), channel_id=1, source_target_pairs={{0,12},{1,13},{2,14},{3,15},{4,8},{5,9},{6,10},{7,11},{8,4},{9,5},... | collective-permute-start | bytes 393224 | tf_op jit(solution)/shard_map/ppermute | solution.py:420
  45.4 5.1 %collective-permute-done.8 = bf16[256,256]{1,0:T(8,128)(2,1)S(1)} collective-permute-done((bf16[256,256]{1,0:T(8,128)(2,1)S(1)}, bf16[256,256]{1,0:T(8,128)(2,1)S(1)}, u32[]{:S(2)}, u32[]{:S(2)}) %collective-permute-start.8) | collective-permute-done | bytes 131104 | tf_op jit(solution)/shard_map/ppermute | solution.py:420
  50.5 1.6 %collective-permute-start.9 = (bf16[256,256]{1,0:T(8,128)(2,1)S(1)}, bf16[256,256]{1,0:T(8,128)(2,1)S(1)}, u32[]{:S(2)}, u32[]{:S(2)}) collective-permute-start(bf16[256,256]{1,0:T(8,128)(2,1)S(1)} %fusion), channel_id=1, source_target_pairs={{0,4},{1,5},{2,6},{3,7},{4,0},{5,1},{6,2},{7,3},{8,12},{9,13},{10,... | collective-permute-start | bytes 393224 | tf_op jit(solution)/shard_map/ppermute | solution.py:420
  52.1 3.5 %collective-permute-done.9 = bf16[256,256]{1,0:T(8,128)(2,1)S(1)} collective-permute-done((bf16[256,256]{1,0:T(8,128)(2,1)S(1)}, bf16[256,256]{1,0:T(8,128)(2,1)S(1)}, u32[]{:S(2)}, u32[]{:S(2)}) %collective-permute-start.9) | collective-permute-done | bytes 131104 | tf_op jit(solution)/shard_map/ppermute | solution.py:420
  55.6 0.1 add_convert_fusion.s00
  55.7 0.1 collective-permute-start.10
  55.8 0.1 collective-permute-start.11
  55.9 4.9 %collective-permute-done.10.s10 = bf16[256,256]{1,0:T(8,128)(2,1)S(1)} collective-permute-done((bf16[256,256]{1,0:T(8,128)(2,1)S(1)}, bf16[256,256]{1,0:T(8,128)(2,1)S(1)}, u32[]{:S(2)}, u32[]{:S(2)}) %collective-permute-start.10) | collective-permute-done | bytes 131104 | tf_op jit(solution)/shard_map/ppermute | solution.py:420
  60.7 0.0 collective-permute-start.12
  60.7 0.0 collective-permute-done.11.s01
  60.7 1.3 %collective-permute-done.12.s11 = bf16[256,256]{1,0:T(8,128)(2,1)S(1)} collective-permute-done((bf16[256,256]{1,0:T(8,128)(2,1)S(1)}, bf16[256,256]{1,0:T(8,128)(2,1)S(1)}, u32[]{:S(2)}, u32[]{:S(2)}) %collective-permute-start.12) | collective-permute-done | bytes 131104 | tf_op jit(solution)/shard_map/ppermute | solution.py:420
  62.1 0.0 copy-done
  62.1 0.0 copy-done.4
  62.1 3.7 %shard_map.77 = (f32[2,2,2,16,256]{4,3,2,1,0:T(8,128)}, bf16[4,2,256,256]{3,2,1,0:T(8,128)(2,1)}) custom-call(s32[2,4]{1,0:T(2,128)S(1)} %bitcast.3, bf16[256,256]{1,0:T(8,128)(2,1)S(1)} %add_convert_fusion.s00, bf16[256,256]{1,0:T(8,128)(2,1)S(1)} %collective-permute-done.10.s10, bf16[256,256]{1,0:T(8,128)(2,1)S(1)} %collective-permute-done.11.s01, ...), custom_call_target="tpu_custom_call" | custom-call | tf_op jit(solution)/shard_map/pallas_call | solution.py:575
  (1 shorter events, 0.0 us)
Async XLA Ops:
  0.6 1.1 %copy-start.1 = (bf16[2,2,3,1,128,256]{5,4,3,2,1,0:T(8,128)(2,1)S(1)}, bf16[2,2,3,1,128,256]{5,4,3,2,1,0:T(8,128)(2,1)}, u32[]{:S(2)}) copy-start(bf16[2,2,3,1,128,256]{5,4,3,2,1,0:T(8,128)(2,1)} %vectors.1) | copy-start | bytes 2359300
  1.8 0.7 %copy-start.2 = (bf16[2,3,2,3,3,1,128]{6,2,5,4,3,1,0:T(2,128)(2,1)S(1)}, bf16[2,3,2,3,3,1,128]{6,2,5,4,3,1,0:T(2,128)(2,1)}, u32[]{:S(2)}) copy-start(bf16[2,3,2,3,3,1,128]{6,2,5,4,3,1,0:T(2,128)(2,1)} %param.6) | copy-start | bytes 82948
  3.1 1.9 %collective-permute-start = (bf16[2,416,256]{2,1,0:T(8,128)(2,1)S(1)}, bf16[2,416,256]{2,1,0:T(8,128)(2,1)S(1)}, u32[]{:S(2)}, u32[]{:S(2)}) collective-permute-start(bf16[2,416,256]{2,1,0:T(8,128)(2,1)S(1)} %get-tuple-element.24), channel_id=1, source_target_pairs={{0,1},{1,0},{2,3},{3,2},{4,5},{5,4},{6,7},{7,6},{8,9},{9,8},{10,11... | collective-permute-start | bytes 1277960 | tf_op jit(solution)/shard_map/ppermute | solution.py:420
  5.9 13.1 %collective-permute-start.3 = (bf16[2,416,256]{2,1,0:T(8,128)(2,1)S(1)}, bf16[2,416,256]{2,1,0:T(8,128)(2,1)S(1)}, u32[]{:S(2)}, u32[]{:S(2)}) collective-permute-start(bf16[2,416,256]{2,1,0:T(8,128)(2,1)S(1)} %get-tuple-element.28), channel_id=1, source_target_pairs={{0,2},{1,3},{2,0},{3,1},{4,6},{5,7},{6,4},{7,5},{8,10},{9,11},{10,... | collective-permute-start | bytes 1277960 | tf_op jit(solution)/shard_map/ppermute | solution.py:420
  8.8 19.8 %copy-start.3 = (s32[2]{0:T(128)S(1)}, s32[2]{0:T(128)}, u32[]{:S(2)}) copy-start(s32[2]{0:T(128)} %directions.5) | copy-start | bytes 28
  8.8 13.8 %collective-permute-start.2 = (bf16[2,416,256]{2,1,0:T(8,128)(2,1)S(1)}, bf16[2,416,256]{2,1,0:T(8,128)(2,1)S(1)}, u32[]{:S(2)}, u32[]{:S(2)}) collective-permute-start(bf16[2,416,256]{2,1,0:T(8,128)(2,1)S(1)} %get-tuple-element.27.own.refs_5_.refs_4_), channel_id=1, source_target_pairs={{2,6},{0,12},{3,7},{1,13},{6,10},{4,0},{7,11},{5,1},{10,14},{8,4},... | collective-permute-start | bytes 1277960 | tf_op jit(solution)/shard_map/ppermute | solution.py:455
  12.4 19.4 %collective-permute-start.1 = (bf16[2,416,256]{2,1,0:T(8,128)(2,1)S(1)}, bf16[2,416,256]{2,1,0:T(8,128)(2,1)S(1)}, u32[]{:S(2)}, u32[]{:S(2)}) collective-permute-start(bf16[2,416,256]{2,1,0:T(8,128)(2,1)S(1)} %get-tuple-element.28), channel_id=1, source_target_pairs={{2,4},{0,14},{3,5},{1,15},{6,8},{4,2},{7,9},{5,3},{10,12},{8,6},{1... | collective-permute-start | bytes 1277960 | tf_op jit(solution)/shard_map/ppermute | solution.py:456
  26.8 1.8 %collective-permute-start.4 = (bf16[2,384,256]{2,1,0:T(8,128)(2,1)S(1)}, bf16[2,384,256]{2,1,0:T(8,128)(2,1)S(1)}, u32[]{:S(2)}, u32[]{:S(2)}) collective-permute-start(bf16[2,384,256]{2,1,0:T(8,128)(2,1)S(1)} %get-tuple-element.34.refs_0_), channel_id=1, source_target_pairs={{0,1},{1,0},{2,3},{3,2},{4,5},{5,4},{6,7},{7,6},{8,9},{9,8},{10,11... | collective-permute-start | bytes 1179656 | tf_op jit(solution)/shard_map/ppermute | solution.py:420
  26.9 10.2 %collective-permute-start.5 = (bf16[416,256]{1,0:T(8,128)(2,1)S(1)}, bf16[416,256]{1,0:T(8,128)(2,1)S(1)}, u32[]{:S(2)}, u32[]{:S(2)}) collective-permute-start(bf16[416,256]{1,0:T(8,128)(2,1)S(1)} %get-tuple-element.39), channel_id=1, source_target_pairs={{0,4},{2,14},{1,5},{3,15},{4,8},{6,2},{5,9},{7,3},{8,12},{10,6},{9... | collective-permute-start | bytes 638984 | tf_op jit(solution)/shard_map/ppermute | solution.py:457
  34.4 3.8 %collective-permute-start.6 = (bf16[2,384,256]{2,1,0:T(8,128)(2,1)S(1)}, bf16[2,384,256]{2,1,0:T(8,128)(2,1)S(1)}, u32[]{:S(2)}, u32[]{:S(2)}) collective-permute-start(bf16[2,384,256]{2,1,0:T(8,128)(2,1)S(1)} %get-tuple-element.38.refs_1_.refs_0_), channel_id=1, source_target_pairs={{0,1},{1,0},{2,3},{3,2},{4,5},{5,4},{6,7},{7,6},{8,9},{9,8},{10,11... | collective-permute-start | bytes 1179656 | tf_op jit(solution)/shard_map/ppermute | solution.py:420
  38.1 2.4 %collective-permute-start.7 = (bf16[1,384,256]{2,1,0:T(8,128)(2,1)S(1)}, bf16[1,384,256]{2,1,0:T(8,128)(2,1)S(1)}, u32[]{:S(2)}, u32[]{:S(2)}) collective-permute-start(bf16[1,384,256]{2,1,0:T(8,128)(2,1)S(1)} %shard_map.74.refs_1_), channel_id=1, source_target_pairs={{0,1},{1,0},{2,3},{3,2},{4,5},{5,4},{6,7},{7,6},{8,9},{9,8},{10,11... | collective-permute-start | bytes 589832 | tf_op jit(solution)/shard_map/ppermute | solution.py:420
  40.5 21.6 %copy-start = (bf16[4,2,256,256]{3,2,1,0:T(8,128)(2,1)S(1)}, bf16[4,2,256,256]{3,2,1,0:T(8,128)(2,1)}, u32[]{:S(2)}) copy-start(bf16[4,2,256,256]{3,2,1,0:T(8,128)(2,1)} %perambulators.1) | copy-start | bytes 3145732
  40.5 21.6 %copy-start.4 = (s32[4,2]{0,1:T(2,128)S(1)}, s32[4,2]{0,1:T(2,128)}, u32[]{:S(2)}) copy-start(s32[4,2]{0,1:T(2,128)} %param.8) | copy-start | bytes 100
  42.6 7.9 %collective-permute-start.8 = (bf16[256,256]{1,0:T(8,128)(2,1)S(1)}, bf16[256,256]{1,0:T(8,128)(2,1)S(1)}, u32[]{:S(2)}, u32[]{:S(2)}) collective-permute-start(bf16[256,256]{1,0:T(8,128)(2,1)S(1)} %get-tuple-element.45), channel_id=1, source_target_pairs={{0,12},{1,13},{2,14},{3,15},{4,8},{5,9},{6,10},{7,11},{8,4},{9,5},... | collective-permute-start | bytes 393224 | tf_op jit(solution)/shard_map/ppermute | solution.py:420
  50.5 5.1 %collective-permute-start.9 = (bf16[256,256]{1,0:T(8,128)(2,1)S(1)}, bf16[256,256]{1,0:T(8,128)(2,1)S(1)}, u32[]{:S(2)}, u32[]{:S(2)}) collective-permute-start(bf16[256,256]{1,0:T(8,128)(2,1)S(1)} %fusion), channel_id=1, source_target_pairs={{0,4},{1,5},{2,6},{3,7},{4,0},{5,1},{6,2},{7,3},{8,12},{9,13},{10,... | collective-permute-start | bytes 393224 | tf_op jit(solution)/shard_map/ppermute | solution.py:420
  55.7 5.0 %collective-permute-start.10 = (bf16[256,256]{1,0:T(8,128)(2,1)S(1)}, bf16[256,256]{1,0:T(8,128)(2,1)S(1)}, u32[]{:S(2)}, u32[]{:S(2)}) collective-permute-start(bf16[256,256]{1,0:T(8,128)(2,1)S(1)} %add_convert_fusion.s00), channel_id=1, source_target_pairs={{0,2},{1,3},{2,0},{3,1},{4,6},{5,7},{6,4},{7,5},{8,10},{9,11},{10,... | collective-permute-start | bytes 393224 | tf_op jit(solution)/shard_map/ppermute | solution.py:420
  55.8 5.0 %collective-permute-start.11 = (bf16[256,256]{1,0:T(8,128)(2,1)S(1)}, bf16[256,256]{1,0:T(8,128)(2,1)S(1)}, u32[]{:S(2)}, u32[]{:S(2)}) collective-permute-start(bf16[256,256]{1,0:T(8,128)(2,1)S(1)} %add_convert_fusion.s00), channel_id=1, source_target_pairs={{0,1},{1,0},{2,3},{3,2},{4,5},{5,4},{6,7},{7,6},{8,9},{9,8},{10,11... | collective-permute-start | bytes 393224 | tf_op jit(solution)/shard_map/ppermute | solution.py:420
  60.7 1.3 %collective-permute-start.12 = (bf16[256,256]{1,0:T(8,128)(2,1)S(1)}, bf16[256,256]{1,0:T(8,128)(2,1)S(1)}, u32[]{:S(2)}, u32[]{:S(2)}) collective-permute-start(bf16[256,256]{1,0:T(8,128)(2,1)S(1)} %collective-permute-done.10.s10), channel_id=1, source_target_pairs={{0,1},{1,0},{2,3},{3,2},{4,5},{5,4},{6,7},{7,6},{8,9},{9,8},{10,11... | collective-permute-start | bytes 393224 | tf_op jit(solution)/shard_map/ppermute | solution.py:420

commit v8 on v7

--- a/solution.py
+++ b/solution.py
@@ -37,67 +37,44 @@
     return core + (1 - 2 * core) * ((1 - chip) if t == 0 else chip)
 
 
-def split_kernel(vectors, links_in, own, other, send, links, packed, sems):
+def split_kernel(vectors, links, own, other, send):
     core, chip = position()
     half = vectors.shape[5] // 2
-    arriving = pltpu.make_async_copy(links_in, links, sems.at[28])
-    arriving.start()
-    copies = []
-    for t in range(2):
+    for t, kept in enumerate((own, other)):
+        time = chip + t * (1 - 2 * chip)
+        slot = slot_of(core, chip, t)
         for part in range(2):
             for color in range(COLORS):
                 rows = pl.ds(color * SITES, SITES)
                 lanes = pl.ds(part * half, half)
-                near = pl.ds(pl.multiple_of(core * half, half), half)
-                far = pl.ds(pl.multiple_of((1 - core) * half, half), half)
-                block = vectors.at[chip + t * (1 - 2 * chip), part, color, 0]
-                kept = (own, other)[t]
-                for source, target in (
-                    (block.at[:, near], kept.at[slot_of(core, chip, t), rows, lanes]),
-                    (block.at[:, far], send.at[t, rows, lanes]),
-                ):
-                    copies.append(pltpu.make_async_copy(source, target, sems.at[len(copies)]))
-                    copies[-1].start()
-    arriving.wait()
-    for t in range(2):
-        table = links.at[chip + t * (1 - 2 * chip)]
+                block = vectors[time, part, color, 0]
+                low, high = block[:, :half], block[:, half:]
+                kept[slot, rows, lanes] = jnp.where(core == 0, low, high)
+                send[t, rows, lanes] = jnp.where(core == 0, high, low)
         gathered = [
-            table[d, row, column, 0].astype(f32)
+            links[time, d, row, column, 0].astype(f32)
             for d in range(3)
             for row in range(COLORS)
             for column in range(COLORS)
         ]
         gathered.append(jnp.zeros((2 * PACKED_LINKS - LINK_ROWS, SITES), f32))
-        rows = jnp.concatenate(gathered, axis=0).astype(bf16)
-        packed[t, :, pl.ds(0, SITES)] = rows[:PACKED_LINKS]
-        packed[t, :, pl.ds(SITES, SITES)] = rows[PACKED_LINKS:]
-        for target in ((own, other)[t].at[slot_of(core, chip, t)], send.at[t]):
-            copies.append(
-                pltpu.make_async_copy(
-                    packed.at[t], target.at[pl.ds(FIELD, PACKED_LINKS)], sems.at[len(copies)]
-                )
-            )
-            copies[-1].start()
-    for copy in copies:
-        copy.wait()
-
-
-def join_kernel(received, own_in, other_in, own, other, edge, sems):
+        packed = jnp.concatenate(gathered, axis=0).astype(bf16)
+        rows = pl.ds(FIELD, PACKED_LINKS)
+        for k in range(2):
+            piece = packed[k * PACKED_LINKS : (k + 1) * PACKED_LINKS]
+            kept[slot, rows, pl.ds(k * SITES, SITES)] = piece
+            send[t, rows, pl.ds(k * SITES, SITES)] = piece
+
+
+def join_kernel(received, own_in, other_in, own, other, edge):
     core, chip = position()
-    copies = [
-        pltpu.make_async_copy(received.at[t], kept.at[1 - slot_of(core, chip, t)], sems.at[t])
-        for t, kept in enumerate((own, other))
-    ]
-    for copy in copies:
-        copy.start()
-    here = slot_of(core, chip, 0) == 0
-    kept_edge = pltpu.make_async_copy(own_in.at[0], edge, sems.at[2])
-    received_edge = pltpu.make_async_copy(received.at[0], edge, sems.at[2])
-    pl.when(here)(kept_edge.start)
-    pl.when(jnp.logical_not(here))(received_edge.start)
-    for copy in copies:
-        copy.wait()
-    kept_edge.wait()
+    slot = slot_of(core, chip, 0)
+    own[slot] = own_in[slot]
+    own[1 - slot] = received[0]
+    edge[...] = jnp.where(slot == 0, own_in[0], received[0])
+    slot = slot_of(core, chip, 1)
+    other[slot] = other_in[slot]
+    other[1 - slot] = received[1]
 
 
 def shift_y(row, lane):
@@ -411,7 +388,6 @@
     blocks = n // 4
     vmem = whole_in_vmem()
     anywhere = pl.BlockSpec(memory_space=pl.ANY)
-    hbm = pl.BlockSpec(memory_space=pltpu.HBM)
     smem = pl.BlockSpec(memory_space=pltpu.SMEM)
     table = jnp.transpose(links, (0, 1, 3, 4, 5, 2, 6))
     rows = FIELD + PACKED_LINKS
@@ -423,23 +399,16 @@
     own, other, send = pl.pallas_call(
         split_kernel,
         out_shape=(package, package, package),
-        in_specs=[hbm, hbm],
-        out_specs=(anywhere, anywhere, anywhere),
-        scratch_shapes=[
-            pltpu.VMEM(table.shape, bf16),
-            pltpu.VMEM((2, PACKED_LINKS, 2 * SITES), bf16),
-            pltpu.SemaphoreType.DMA((29,)),
-        ],
+        in_specs=[vmem] * 2,
+        out_specs=(vmem,) * 3,
         compiler_params=params(8),
     )(eigvecs, table)
     received = swap(send, 1)
     own, other, edge = pl.pallas_call(
         join_kernel,
         out_shape=(package, package, jax.ShapeDtypeStruct((rows, vector_count), bf16)),
-        in_specs=[anywhere] * 3,
-        out_specs=(anywhere, anywhere, anywhere),
-        scratch_shapes=[pltpu.SemaphoreType.DMA((3,))],
-        input_output_aliases={1: 0, 2: 1},
+        in_specs=[vmem] * 3,
+        out_specs=(vmem,) * 3,
         compiler_params=params(8),
     )(received, own, other)
 

time: 66 us -> 64.8 us (0.982)
  Pallas kernels: 20.1 us -> 18.9 us
    pallas_call x1, Pallas kernels: 0.82 us -> 0.08 us  [body(): pl.pallas_call(join_kernel, out_shape=(package, package, jax.ShapeDtypeSt...]
where the time goes in v8:
time: 64.8 us; the launch traced here: 64.6 us
  waiting for transfers between devices  30.4 us (47%)
  Pallas kernels  18.9 us (29%)
  starting transfers between devices  12.4 us (19%)
  local copies, waits for them, and re-layouts  1.89 us (3%)
  between operations  0.79 us (1%)
    ppermute x10, waiting for transfers between devices, swap(): return lax.ppermute(value, 'space', [(i, i ^ bit) for i in range(n)])  22.9 us
    ppermute x10, starting transfers between devices, swap(): return lax.ppermute(value, 'space', [(i, i ^ bit) for i in range(n)])  8.12 us
    pallas_call x3, Pallas kernels, elemental(): pl.pallas_call(functools.partial(elemental_kernel, scale, vector_pieces,...  6.31 us
    pallas_call x1, Pallas kernels, body(): pl.pallas_call(smear_inner, out_shape=(field(2), field(2), jax.ShapeDtype...  4.15 us
    ppermute x1, waiting for transfers between devices, body(): second = lax.ppermute(own, 'space', straight)  3.72 us
    pallas_call x1, Pallas kernels, body(): pl.pallas_call(functools.partial(pair_kernel, pair_scale), out_shape=(jax...  3.69 us
    ppermute x1, starting transfers between devices, body(): second = lax.ppermute(own, 'space', straight)  3.6 us
    pallas_call x1, Pallas kernels, body(): pl.pallas_call(smear_middle, out_shape=(field(2), short, short, after_sha...  2.63 us
  transfers between devices with their start and end apart: 13, of which 10 were waited for; matrix products, arithmetic and copies ran while one was open for 0% of the time, Pallas kernels for 20%

profile of v8, /device:TPU:0, one launch (start us, length us, event | category | flops | bytes accessed | tf_op | source)
XLA Modules:
  0.0 64.6 jit_solution(11081666185482813193)
XLA Ops:
  0.6 0.0 copy-start.1
  0.6 1.1 %copy-done.1 = bf16[2,2,3,1,128,256]{5,4,3,2,1,0:T(8,128)(2,1)S(1)} copy-done((bf16[2,2,3,1,128,256]{5,4,3,2,1,0:T(8,128)(2,1)S(1)}, bf16[2,2,3,1,128,256]{5,4,3,2,1,0:T(8,128)(2,1)}, u32[]{:S(2)}) %copy-start.1) | copy-done | bytes 786456
  1.8 0.0 copy-start.2
  1.8 0.7 %copy-done.2 = bf16[2,3,2,3,3,1,128]{6,2,5,4,3,1,0:T(2,128)(2,1)S(1)} copy-done((bf16[2,3,2,3,3,1,128]{6,2,5,4,3,1,0:T(2,128)(2,1)S(1)}, bf16[2,3,2,3,3,1,128]{6,2,5,4,3,1,0:T(2,128)(2,1)}, u32[]{:S(2)}) %copy-start.2) | copy-done | bytes 27672
  2.5 0.1 shard_map.68
  2.6 0.5 collective-permute-start
  3.2 1.4 %collective-permute-done.received = bf16[2,416,256]{2,1,0:T(8,128)(2,1)S(1)} collective-permute-done((bf16[2,416,256]{2,1,0:T(8,128)(2,1)S(1)}, bf16[2,416,256]{2,1,0:T(8,128)(2,1)S(1)}, u32[]{:S(2)}, u32[]{:S(2)}) %collective-permute-start) | collective-permute-done | bytes 426016 | tf_op jit(solution)/shard_map/ppermute | solution.py:396
  4.6 0.1 shard_map.69
  4.6 3.0 %collective-permute-start.3 = (bf16[2,416,256]{2,1,0:T(8,128)(2,1)S(1)}, bf16[2,416,256]{2,1,0:T(8,128)(2,1)S(1)}, u32[]{:S(2)}, u32[]{:S(2)}) collective-permute-start(bf16[2,416,256]{2,1,0:T(8,128)(2,1)S(1)} %get-tuple-element.28), channel_id=1, source_target_pairs={{0,2},{1,3},{2,0},{3,1},{4,6},{5,7},{6,4},{7,5},{8,10},{9,11},{10,... | collective-permute-start | bytes 1277960 | tf_op jit(solution)/shard_map/ppermute | solution.py:396
  7.6 0.0 copy-start.3
  7.6 3.6 %collective-permute-start.2 = (bf16[2,416,256]{2,1,0:T(8,128)(2,1)S(1)}, bf16[2,416,256]{2,1,0:T(8,128)(2,1)S(1)}, u32[]{:S(2)}, u32[]{:S(2)}) collective-permute-start(bf16[2,416,256]{2,1,0:T(8,128)(2,1)S(1)} %get-tuple-element.27.own.refs_5_.refs_4_), channel_id=1, source_target_pairs={{2,6},{0,12},{3,7},{1,13},{6,10},{4,0},{7,11},{5,1},{10,14},{8,4},... | collective-permute-start | bytes 1277960 | tf_op jit(solution)/shard_map/ppermute | solution.py:424
  11.2 0.0 collective-permute-start.1
  11.2 6.5 %collective-permute-done.3.across.refs_2_.refs_4_ = bf16[2,416,256]{2,1,0:T(8,128)(2,1)S(1)} collective-permute-done((bf16[2,416,256]{2,1,0:T(8,128)(2,1)S(1)}, bf16[2,416,256]{2,1,0:T(8,128)(2,1)S(1)}, u32[]{:S(2)}, u32[]{:S(2)}) %collective-permute-start.3) | collective-permute-done | bytes 426016 | tf_op jit(solution)/shard_map/ppermute | solution.py:396
  17.7 3.7 %collective-permute-done.2.second = bf16[2,416,256]{2,1,0:T(8,128)(2,1)S(1)} collective-permute-done((bf16[2,416,256]{2,1,0:T(8,128)(2,1)S(1)}, bf16[2,416,256]{2,1,0:T(8,128)(2,1)S(1)}, u32[]{:S(2)}, u32[]{:S(2)}) %collective-permute-start.2) | collective-permute-done | bytes 426016 | tf_op jit(solution)/shard_map/ppermute | solution.py:424
  21.4 4.1 %shard_map.70 = (bf16[2,384,256]{2,1,0:T(8,128)(2,1)S(1)}, bf16[2,384,256]{2,1,0:T(8,128)(2,1)S(1)}, bf16[768,1152]{1,0:T(8,128)(2,1)S(1)}) custom-call(bf16[2,416,256]{2,1,0:T(8,128)(2,1)S(1)} %collective-permute-done.2.second, bf16[2,416,256]{2,1,0:T(8,128)(2,1)S(1)} %collective-permute-done.3.across.refs_2_.refs_4_, ...), custom_call_target="tpu_custom_call" | custom-call | flops 1024 | bytes 1024 | tf_op jit(solution)/shard_map/pallas_call | solution.py:467
  25.6 0.1 collective-permute-start.4
  25.7 0.7 %collective-permute-start.5 = (bf16[416,256]{1,0:T(8,128)(2,1)S(1)}, bf16[416,256]{1,0:T(8,128)(2,1)S(1)}, u32[]{:S(2)}, u32[]{:S(2)}) collective-permute-start(bf16[416,256]{1,0:T(8,128)(2,1)S(1)} %get-tuple-element.39), channel_id=1, source_target_pairs={{0,4},{2,14},{1,5},{3,15},{4,8},{6,2},{5,9},{7,3},{8,12},{10,6},{9... | collective-permute-start | bytes 638984 | tf_op jit(solution)/shard_map/ppermute | solution.py:426
  26.4 0.9 %shard_map.71 = (f32[384,256]{1,0:T(8,128)S(1)}, f32[384,256]{1,0:T(8,128)S(1)}, bf16[768,768]{1,0:T(8,128)(2,1)S(1)}) custom-call(bf16[2,416,256]{2,1,0:T(8,128)(2,1)S(1)} %get-tuple-element.27.own.refs_5_.refs_4_, bf16[2,384,256]{2,1,0:T(8,128)(2,1)S(1)} %get-tuple-element.29.u_in, bf16[768,1152]{1,0:T(8,128)(2,1)S(1)} %get-tuple-element.30.operator.operator_in), custom_call_target="tpu_custom_call" | custom-call | flops 1024 | bytes 1024 | tf_op jit(solution)/shard_map/pallas_call | solution.py:483
  27.3 0.1 collective-permute-done.4.refs_1_.refs_2_
  27.4 0.0 copy-done.3
  27.4 1.9 %shard_map.72.refs_6_ = f32[256,512]{1,0:T(8,128)S(1)} custom-call(s32[2]{0:T(128)S(1)} %copy-done.3, bf16[2,384,256]{2,1,0:T(8,128)(2,1)S(1)} %get-tuple-element.34.refs_0_, bf16[2,384,256]{2,1,0:T(8,128)(2,1)S(1)} %collective-permute-done.4.refs_1_.refs_2_, bf16[2,416,256]{2,1,0:T(8,128)(2,1)S(1)} %collective-permute-done.3.across.refs_2_.refs_4_), custom_call_target="tpu_custom_call" | custom-call | flops 1024 | bytes 1024 | tf_op jit(solution)/shard_map/pallas_call | solution.py:447
  29.3 1.2 %collective-permute-done.1.first.refs_5_ = bf16[2,416,256]{2,1,0:T(8,128)(2,1)S(1)} collective-permute-done((bf16[2,416,256]{2,1,0:T(8,128)(2,1)S(1)}, bf16[2,416,256]{2,1,0:T(8,128)(2,1)S(1)}, u32[]{:S(2)}, u32[]{:S(2)}) %collective-permute-start.1) | collective-permute-done | bytes 426016 | tf_op jit(solution)/shard_map/ppermute | solution.py:425
  30.6 2.6 %shard_map.73 = (bf16[2,384,256]{2,1,0:T(8,128)(2,1)S(1)}, f32[384,256]{1,0:T(8,128)S(1)}, f32[384,256]{1,0:T(8,128)S(1)}, bf16[768,384]{1,0:T(8,128)(2,1)S(1)}) custom-call(bf16[2,416,256]{2,1,0:T(8,128)(2,1)S(1)} %get-tuple-element.27.own.refs_5_.refs_4_, bf16[2,416,256]{2,1,0:T(8,128)(2,1)S(1)} %collective-permute-done.1.first.refs_5_, ...), custom_call_target="tpu_custom_call" | custom-call | flops 1024 | bytes 1024 | tf_op jit(solution)/shard_map/pallas_call | solution.py:494
  33.2 0.1 collective-permute-start.6
  33.3 2.6 %collective-permute-done.5.last = bf16[416,256]{1,0:T(8,128)(2,1)S(1)} collective-permute-done((bf16[416,256]{1,0:T(8,128)(2,1)S(1)}, bf16[416,256]{1,0:T(8,128)(2,1)S(1)}, u32[]{:S(2)}, u32[]{:S(2)}) %collective-permute-start.5) | collective-permute-done | bytes 213024 | tf_op jit(solution)/shard_map/ppermute | solution.py:426
  35.9 1.1 %shard_map.74.refs_1_ = bf16[1,384,256]{2,1,0:T(8,128)(2,1)S(1)} custom-call(bf16[2,416,256]{2,1,0:T(8,128)(2,1)S(1)} %collective-permute-done.1.first.refs_5_, bf16[416,256]{1,0:T(8,128)(2,1)S(1)} %collective-permute-done.5.last, f32[384,256]{1,0:T(8,128)S(1)} %get-tuple-element.40.first_short, f32[384,256]{1,0:T(8,128)S(1)} %get-tuple-element.41.second_short, ...), custom_call_target="tpu_custom_call" | custom-call | flops 1024 | bytes 1024 | tf_op jit(solution)/shard_map/pallas_call | solution.py:511
  36.9 0.1 collective-permute-start.7
  37.0 0.0 collective-permute-done.6.refs_3_.refs_2_
  37.0 2.3 %shard_map.75.refs_6_ = f32[256,512]{1,0:T(8,128)S(1)} custom-call(s32[2]{0:T(128)S(1)} %copy-done.3, bf16[2,384,256]{2,1,0:T(8,128)(2,1)S(1)} %get-tuple-element.34.refs_0_, bf16[2,384,256]{2,1,0:T(8,128)(2,1)S(1)} %get-tuple-element.38.refs_1_.refs_0_, bf16[2,384,256]{2,1,0:T(8,128)(2,1)S(1)} %collective-permute-done.4.refs_1_.refs_2_, ...), custom_call_target="tpu_custom_call" | custom-call | flops 1024 | bytes 1024 | tf_op jit(solution)/shard_map/pallas_call | solution.py:447
  39.3 0.0 copy-start
  39.3 0.0 copy-start.4
  39.3 0.0 collective-permute-done.7.refs_3_
  39.3 2.1 %shard_map.76 = (f32[256,256]{1,0:T(8,128)S(1)}, bf16[256,256]{1,0:T(8,128)(2,1)S(1)}) custom-call(s32[2]{0:T(128)S(1)} %copy-done.3, bf16[2,384,256]{2,1,0:T(8,128)(2,1)S(1)} %get-tuple-element.38.refs_1_.refs_0_, bf16[1,384,256]{2,1,0:T(8,128)(2,1)S(1)} %shard_map.74.refs_1_, bf16[2,384,256]{2,1,0:T(8,128)(2,1)S(1)} %collective-permute-done.6.refs_3_.refs_2_, ...), custom_call_target="tpu_custom_call" | custom-call | flops 1024 | bytes 1024 | tf_op jit(solution)/shard_map/pallas_call | solution.py:447
  41.4 2.7 %collective-permute-start.8 = (bf16[256,256]{1,0:T(8,128)(2,1)S(1)}, bf16[256,256]{1,0:T(8,128)(2,1)S(1)}, u32[]{:S(2)}, u32[]{:S(2)}) collective-permute-start(bf16[256,256]{1,0:T(8,128)(2,1)S(1)} %get-tuple-element.45), channel_id=1, source_target_pairs={{0,12},{1,13},{2,14},{3,15},{4,8},{5,9},{6,10},{7,11},{8,4},{9,5},... | collective-permute-start | bytes 393224 | tf_op jit(solution)/shard_map/ppermute | solution.py:396
  44.1 5.1 %collective-permute-done.8 = bf16[256,256]{1,0:T(8,128)(2,1)S(1)} collective-permute-done((bf16[256,256]{1,0:T(8,128)(2,1)S(1)}, bf16[256,256]{1,0:T(8,128)(2,1)S(1)}, u32[]{:S(2)}, u32[]{:S(2)}) %collective-permute-start.8) | collective-permute-done | bytes 131104 | tf_op jit(solution)/shard_map/ppermute | solution.py:396
  49.3 1.6 %collective-permute-start.9 = (bf16[256,256]{1,0:T(8,128)(2,1)S(1)}, bf16[256,256]{1,0:T(8,128)(2,1)S(1)}, u32[]{:S(2)}, u32[]{:S(2)}) collective-permute-start(bf16[256,256]{1,0:T(8,128)(2,1)S(1)} %fusion), channel_id=1, source_target_pairs={{0,4},{1,5},{2,6},{3,7},{4,0},{5,1},{6,2},{7,3},{8,12},{9,13},{10,... | collective-permute-start | bytes 393224 | tf_op jit(solution)/shard_map/ppermute | solution.py:396
  50.9 3.5 %collective-permute-done.9 = bf16[256,256]{1,0:T(8,128)(2,1)S(1)} collective-permute-done((bf16[256,256]{1,0:T(8,128)(2,1)S(1)}, bf16[256,256]{1,0:T(8,128)(2,1)S(1)}, u32[]{:S(2)}, u32[]{:S(2)}) %collective-permute-start.9) | collective-permute-done | bytes 131104 | tf_op jit(solution)/shard_map/ppermute | solution.py:396
  54.4 0.1 add_convert_fusion.s00
  54.5 0.1 collective-permute-start.10
  54.6 0.1 collective-permute-start.11
  54.7 4.9 %collective-permute-done.10.s10 = bf16[256,256]{1,0:T(8,128)(2,1)S(1)} collective-permute-done((bf16[256,256]{1,0:T(8,128)(2,1)S(1)}, bf16[256,256]{1,0:T(8,128)(2,1)S(1)}, u32[]{:S(2)}, u32[]{:S(2)}) %collective-permute-start.10) | collective-permute-done | bytes 131104 | tf_op jit(solution)/shard_map/ppermute | solution.py:396
  59.5 0.0 collective-permute-start.12
  59.5 0.0 collective-permute-done.11.s01
  59.5 1.3 %collective-permute-done.12.s11 = bf16[256,256]{1,0:T(8,128)(2,1)S(1)} collective-permute-done((bf16[256,256]{1,0:T(8,128)(2,1)S(1)}, bf16[256,256]{1,0:T(8,128)(2,1)S(1)}, u32[]{:S(2)}, u32[]{:S(2)}) %collective-permute-start.12) | collective-permute-done | bytes 131104 | tf_op jit(solution)/shard_map/ppermute | solution.py:396
  60.9 0.0 copy-done
  60.9 0.0 copy-done.4
  60.9 3.7 %shard_map.77 = (f32[2,2,2,16,256]{4,3,2,1,0:T(8,128)}, bf16[4,2,256,256]{3,2,1,0:T(8,128)(2,1)}) custom-call(s32[2,4]{1,0:T(2,128)S(1)} %bitcast.3, bf16[256,256]{1,0:T(8,128)(2,1)S(1)} %add_convert_fusion.s00, bf16[256,256]{1,0:T(8,128)(2,1)S(1)} %collective-permute-done.10.s10, bf16[256,256]{1,0:T(8,128)(2,1)S(1)} %collective-permute-done.11.s01, ...), custom_call_target="tpu_custom_call" | custom-call | tf_op jit(solution)/shard_map/pallas_call | solution.py:544
  (1 shorter events, 0.0 us)
Async XLA Ops:
  0.6 1.1 %copy-start.1 = (bf16[2,2,3,1,128,256]{5,4,3,2,1,0:T(8,128)(2,1)S(1)}, bf16[2,2,3,1,128,256]{5,4,3,2,1,0:T(8,128)(2,1)}, u32[]{:S(2)}) copy-start(bf16[2,2,3,1,128,256]{5,4,3,2,1,0:T(8,128)(2,1)} %vectors.1) | copy-start | bytes 2359300
  1.8 0.7 %copy-start.2 = (bf16[2,3,2,3,3,1,128]{6,2,5,4,3,1,0:T(2,128)(2,1)S(1)}, bf16[2,3,2,3,3,1,128]{6,2,5,4,3,1,0:T(2,128)(2,1)}, u32[]{:S(2)}) copy-start(bf16[2,3,2,3,3,1,128]{6,2,5,4,3,1,0:T(2,128)(2,1)} %param.6) | copy-start | bytes 82948
  2.6 1.9 %collective-permute-start = (bf16[2,416,256]{2,1,0:T(8,128)(2,1)S(1)}, bf16[2,416,256]{2,1,0:T(8,128)(2,1)S(1)}, u32[]{:S(2)}, u32[]{:S(2)}) collective-permute-start(bf16[2,416,256]{2,1,0:T(8,128)(2,1)S(1)} %get-tuple-element.24), channel_id=1, source_target_pairs={{0,1},{1,0},{2,3},{3,2},{4,5},{5,4},{6,7},{7,6},{8,9},{9,8},{10,11... | collective-permute-start | bytes 1277960 | tf_op jit(solution)/shard_map/ppermute | solution.py:396
  4.6 13.1 %collective-permute-start.3 = (bf16[2,416,256]{2,1,0:T(8,128)(2,1)S(1)}, bf16[2,416,256]{2,1,0:T(8,128)(2,1)S(1)}, u32[]{:S(2)}, u32[]{:S(2)}) collective-permute-start(bf16[2,416,256]{2,1,0:T(8,128)(2,1)S(1)} %get-tuple-element.28), channel_id=1, source_target_pairs={{0,2},{1,3},{2,0},{3,1},{4,6},{5,7},{6,4},{7,5},{8,10},{9,11},{10,... | collective-permute-start | bytes 1277960 | tf_op jit(solution)/shard_map/ppermute | solution.py:396
  7.6 19.8 %copy-start.3 = (s32[2]{0:T(128)S(1)}, s32[2]{0:T(128)}, u32[]{:S(2)}) copy-start(s32[2]{0:T(128)} %directions.5) | copy-start | bytes 28
  7.6 13.8 %collective-permute-start.2 = (bf16[2,416,256]{2,1,0:T(8,128)(2,1)S(1)}, bf16[2,416,256]{2,1,0:T(8,128)(2,1)S(1)}, u32[]{:S(2)}, u32[]{:S(2)}) collective-permute-start(bf16[2,416,256]{2,1,0:T(8,128)(2,1)S(1)} %get-tuple-element.27.own.refs_5_.refs_4_), channel_id=1, source_target_pairs={{2,6},{0,12},{3,7},{1,13},{6,10},{4,0},{7,11},{5,1},{10,14},{8,4},... | collective-permute-start | bytes 1277960 | tf_op jit(solution)/shard_map/ppermute | solution.py:424
  11.2 19.4 %collective-permute-start.1 = (bf16[2,416,256]{2,1,0:T(8,128)(2,1)S(1)}, bf16[2,416,256]{2,1,0:T(8,128)(2,1)S(1)}, u32[]{:S(2)}, u32[]{:S(2)}) collective-permute-start(bf16[2,416,256]{2,1,0:T(8,128)(2,1)S(1)} %get-tuple-element.28), channel_id=1, source_target_pairs={{2,4},{0,14},{3,5},{1,15},{6,8},{4,2},{7,9},{5,3},{10,12},{8,6},{1... | collective-permute-start | bytes 1277960 | tf_op jit(solution)/shard_map/ppermute | solution.py:425
  25.6 1.8 %collective-permute-start.4 = (bf16[2,384,256]{2,1,0:T(8,128)(2,1)S(1)}, bf16[2,384,256]{2,1,0:T(8,128)(2,1)S(1)}, u32[]{:S(2)}, u32[]{:S(2)}) collective-permute-start(bf16[2,384,256]{2,1,0:T(8,128)(2,1)S(1)} %get-tuple-element.34.refs_0_), channel_id=1, source_target_pairs={{0,1},{1,0},{2,3},{3,2},{4,5},{5,4},{6,7},{7,6},{8,9},{9,8},{10,11... | collective-permute-start | bytes 1179656 | tf_op jit(solution)/shard_map/ppermute | solution.py:396
  25.7 10.2 %collective-permute-start.5 = (bf16[416,256]{1,0:T(8,128)(2,1)S(1)}, bf16[416,256]{1,0:T(8,128)(2,1)S(1)}, u32[]{:S(2)}, u32[]{:S(2)}) collective-permute-start(bf16[416,256]{1,0:T(8,128)(2,1)S(1)} %get-tuple-element.39), channel_id=1, source_target_pairs={{0,4},{2,14},{1,5},{3,15},{4,8},{6,2},{5,9},{7,3},{8,12},{10,6},{9... | collective-permute-start | bytes 638984 | tf_op jit(solution)/shard_map/ppermute | solution.py:426
  33.2 3.8 %collective-permute-start.6 = (bf16[2,384,256]{2,1,0:T(8,128)(2,1)S(1)}, bf16[2,384,256]{2,1,0:T(8,128)(2,1)S(1)}, u32[]{:S(2)}, u32[]{:S(2)}) collective-permute-start(bf16[2,384,256]{2,1,0:T(8,128)(2,1)S(1)} %get-tuple-element.38.refs_1_.refs_0_), channel_id=1, source_target_pairs={{0,1},{1,0},{2,3},{3,2},{4,5},{5,4},{6,7},{7,6},{8,9},{9,8},{10,11... | collective-permute-start | bytes 1179656 | tf_op jit(solution)/shard_map/ppermute | solution.py:396
  36.9 2.4 %collective-permute-start.7 = (bf16[1,384,256]{2,1,0:T(8,128)(2,1)S(1)}, bf16[1,384,256]{2,1,0:T(8,128)(2,1)S(1)}, u32[]{:S(2)}, u32[]{:S(2)}) collective-permute-start(bf16[1,384,256]{2,1,0:T(8,128)(2,1)S(1)} %shard_map.74.refs_1_), channel_id=1, source_target_pairs={{0,1},{1,0},{2,3},{3,2},{4,5},{5,4},{6,7},{7,6},{8,9},{9,8},{10,11... | collective-permute-start | bytes 589832 | tf_op jit(solution)/shard_map/ppermute | solution.py:396
  39.3 21.6 %copy-start = (bf16[4,2,256,256]{3,2,1,0:T(8,128)(2,1)S(1)}, bf16[4,2,256,256]{3,2,1,0:T(8,128)(2,1)}, u32[]{:S(2)}) copy-start(bf16[4,2,256,256]{3,2,1,0:T(8,128)(2,1)} %perambulators.1) | copy-start | bytes 3145732
  39.3 21.6 %copy-start.4 = (s32[4,2]{0,1:T(2,128)S(1)}, s32[4,2]{0,1:T(2,128)}, u32[]{:S(2)}) copy-start(s32[4,2]{0,1:T(2,128)} %param.8) | copy-start | bytes 100
  41.4 7.9 %collective-permute-start.8 = (bf16[256,256]{1,0:T(8,128)(2,1)S(1)}, bf16[256,256]{1,0:T(8,128)(2,1)S(1)}, u32[]{:S(2)}, u32[]{:S(2)}) collective-permute-start(bf16[256,256]{1,0:T(8,128)(2,1)S(1)} %get-tuple-element.45), channel_id=1, source_target_pairs={{0,12},{1,13},{2,14},{3,15},{4,8},{5,9},{6,10},{7,11},{8,4},{9,5},... | collective-permute-start | bytes 393224 | tf_op jit(solution)/shard_map/ppermute | solution.py:396
  49.3 5.1 %collective-permute-start.9 = (bf16[256,256]{1,0:T(8,128)(2,1)S(1)}, bf16[256,256]{1,0:T(8,128)(2,1)S(1)}, u32[]{:S(2)}, u32[]{:S(2)}) collective-permute-start(bf16[256,256]{1,0:T(8,128)(2,1)S(1)} %fusion), channel_id=1, source_target_pairs={{0,4},{1,5},{2,6},{3,7},{4,0},{5,1},{6,2},{7,3},{8,12},{9,13},{10,... | collective-permute-start | bytes 393224 | tf_op jit(solution)/shard_map/ppermute | solution.py:396
  54.5 5.0 %collective-permute-start.10 = (bf16[256,256]{1,0:T(8,128)(2,1)S(1)}, bf16[256,256]{1,0:T(8,128)(2,1)S(1)}, u32[]{:S(2)}, u32[]{:S(2)}) collective-permute-start(bf16[256,256]{1,0:T(8,128)(2,1)S(1)} %add_convert_fusion.s00), channel_id=1, source_target_pairs={{0,2},{1,3},{2,0},{3,1},{4,6},{5,7},{6,4},{7,5},{8,10},{9,11},{10,... | collective-permute-start | bytes 393224 | tf_op jit(solution)/shard_map/ppermute | solution.py:396
  54.6 5.0 %collective-permute-start.11 = (bf16[256,256]{1,0:T(8,128)(2,1)S(1)}, bf16[256,256]{1,0:T(8,128)(2,1)S(1)}, u32[]{:S(2)}, u32[]{:S(2)}) collective-permute-start(bf16[256,256]{1,0:T(8,128)(2,1)S(1)} %add_convert_fusion.s00), channel_id=1, source_target_pairs={{0,1},{1,0},{2,3},{3,2},{4,5},{5,4},{6,7},{7,6},{8,9},{9,8},{10,11... | collective-permute-start | bytes 393224 | tf_op jit(solution)/shard_map/ppermute | solution.py:396
  59.5 1.3 %collective-permute-start.12 = (bf16[256,256]{1,0:T(8,128)(2,1)S(1)}, bf16[256,256]{1,0:T(8,128)(2,1)S(1)}, u32[]{:S(2)}, u32[]{:S(2)}) collective-permute-start(bf16[256,256]{1,0:T(8,128)(2,1)S(1)} %collective-permute-done.10.s10), channel_id=1, source_target_pairs={{0,1},{1,0},{2,3},{3,2},{4,5},{5,4},{6,7},{7,6},{8,9},{9,8},{10,11... | collective-permute-start | bytes 393224 | tf_op jit(solution)/shard_map/ppermute | solution.py:396

commit v9 on v8

--- a/solution.py
+++ b/solution.py
@@ -186,12 +186,10 @@
     return center + weighted_hops(operator, planes)
 
 
-def smear_inner(second, across, own, w_out, u_out, operator_out, fields, rims, grown, operators, sems):
-    copies = []
+def smear_inner(second, across, own, w_out, u_out, operator_out, fields, rims, grown, operators):
     for k, package in enumerate((second, across, own)):
-        copies.append((field_of(package), fields.at[pl.ds(2 * k, 2)]))
-        copies.append((links_of(package), rims.at[pl.ds(2 * k, 2)]))
-    fetch(copies, sems)
+        fields[pl.ds(2 * k, 2)] = package[:, pl.ds(0, FIELD)]
+        rims[pl.ds(2 * k, 2)] = package[:, pl.ds(FIELD, PACKED_LINKS)]
     for r in range(1, 5):
         operator = operators.at[r - 1] if r < 4 else operator_out
         build(operator, rims, r)
@@ -467,14 +465,13 @@
     w_inner, u_inner, operator = pl.pallas_call(
         smear_inner,
         out_shape=(field(2), field(2), jax.ShapeDtypeStruct((2 * FIELD, 3 * FIELD), bf16)),
-        in_specs=[anywhere] * 3,
+        in_specs=[vmem] * 3,
         out_specs=(vmem,) * 3,
         scratch_shapes=[
             scratch(6, FIELD, vector_count),
             scratch(6, PACKED_LINKS, 2 * SITES),
             scratch(4, FIELD, vector_count),
             scratch(3, 2 * FIELD, 3 * FIELD),
-            pltpu.SemaphoreType.DMA((6,)),
         ],
         compiler_params=params(24),
         cost_estimate=small,

time: 64.8 us -> 64.7 us (level)
  starting transfers between devices: 12.4 us -> 13.2 us
    ppermute x1, waiting for transfers between devices: 2.59 us -> 1.8 us  [body(): last = lax.ppermute(edge, 'space', outer)]
    ppermute x1, waiting for transfers between devices: 1.24 us -> 2.02 us  [body(): first = lax.ppermute(other, 'space', crossing)]
    ppermute x10, starting transfers between devices: 8.12 us -> 8.86 us  [swap(): return lax.ppermute(value, 'space', [(i, i ^ bit) for i in range(n)])]
  transfers between devices with their start and end apart: 13 -> 13, of which waited for: 10 -> 10; matrix products, arithmetic and copies ran while one was open for 0% -> 0% of each run, Pallas kernels for 20% -> 19%
where the time goes in v9:
time: 64.7 us; the launch traced here: 64.4 us
  waiting for transfers between devices  30 us (46%)
  Pallas kernels  18.5 us (29%)
  starting transfers between devices  13.2 us (20%)
  local copies, waits for them, and re-layouts  1.89 us (3%)
  between operations  0.79 us (1%)
    ppermute x10, waiting for transfers between devices, swap(): return lax.ppermute(value, 'space', [(i, i ^ bit) for i in range(n)])  22.5 us
    ppermute x10, starting transfers between devices, swap(): return lax.ppermute(value, 'space', [(i, i ^ bit) for i in range(n)])  8.86 us
    pallas_call x3, Pallas kernels, elemental(): pl.pallas_call(functools.partial(elemental_kernel, scale, vector_pieces,...  6.3 us
    pallas_call x1, Pallas kernels, body(): pl.pallas_call(smear_inner, out_shape=(field(2), field(2), jax.ShapeDtype...  3.73 us
    ppermute x1, waiting for transfers between devices, body(): second = lax.ppermute(own, 'space', straight)  3.72 us
    pallas_call x1, Pallas kernels, body(): pl.pallas_call(functools.partial(pair_kernel, pair_scale), out_shape=(jax...  3.69 us
    ppermute x1, starting transfers between devices, body(): second = lax.ppermute(own, 'space', straight)  3.6 us
    pallas_call x1, Pallas kernels, body(): pl.pallas_call(smear_middle, out_shape=(field(2), short, short, after_sha...  2.63 us
  transfers between devices with their start and end apart: 13, of which 10 were waited for; matrix products, arithmetic and copies ran while one was open for 0% of the time, Pallas kernels for 19%

profile of v9, /device:TPU:0, one launch (start us, length us, event | category | flops | bytes accessed | tf_op | source)
XLA Modules:
  0.0 64.4 jit_solution(9957089282673416908)
XLA Ops:
  0.6 0.0 copy-start.1
  0.6 1.1 %copy-done.1 = bf16[2,2,3,1,128,256]{5,4,3,2,1,0:T(8,128)(2,1)S(1)} copy-done((bf16[2,2,3,1,128,256]{5,4,3,2,1,0:T(8,128)(2,1)S(1)}, bf16[2,2,3,1,128,256]{5,4,3,2,1,0:T(8,128)(2,1)}, u32[]{:S(2)}) %copy-start.1) | copy-done | bytes 786456
  1.8 0.0 copy-start.2
  1.8 0.7 %copy-done.2 = bf16[2,3,2,3,3,1,128]{6,2,5,4,3,1,0:T(2,128)(2,1)S(1)} copy-done((bf16[2,3,2,3,3,1,128]{6,2,5,4,3,1,0:T(2,128)(2,1)S(1)}, bf16[2,3,2,3,3,1,128]{6,2,5,4,3,1,0:T(2,128)(2,1)}, u32[]{:S(2)}) %copy-start.2) | copy-done | bytes 27672
  2.5 0.1 shard_map.68
  2.6 0.5 collective-permute-start
  3.2 1.4 %collective-permute-done.received = bf16[2,416,256]{2,1,0:T(8,128)(2,1)S(1)} collective-permute-done((bf16[2,416,256]{2,1,0:T(8,128)(2,1)S(1)}, bf16[2,416,256]{2,1,0:T(8,128)(2,1)S(1)}, u32[]{:S(2)}, u32[]{:S(2)}) %collective-permute-start) | collective-permute-done | bytes 426016 | tf_op jit(solution)/shard_map/ppermute | solution.py:394
  4.6 0.1 shard_map.69
  4.6 3.0 %collective-permute-start.3 = (bf16[2,416,256]{2,1,0:T(8,128)(2,1)S(1)}, bf16[2,416,256]{2,1,0:T(8,128)(2,1)S(1)}, u32[]{:S(2)}, u32[]{:S(2)}) collective-permute-start(bf16[2,416,256]{2,1,0:T(8,128)(2,1)S(1)} %get-tuple-element.28), channel_id=1, source_target_pairs={{0,2},{1,3},{2,0},{3,1},{4,6},{5,7},{6,4},{7,5},{8,10},{9,11},{10,... | collective-permute-start | bytes 1277960 | tf_op jit(solution)/shard_map/ppermute | solution.py:394
  7.6 0.0 copy-start.3
  7.6 3.6 %collective-permute-start.2 = (bf16[2,416,256]{2,1,0:T(8,128)(2,1)S(1)}, bf16[2,416,256]{2,1,0:T(8,128)(2,1)S(1)}, u32[]{:S(2)}, u32[]{:S(2)}) collective-permute-start(bf16[2,416,256]{2,1,0:T(8,128)(2,1)S(1)} %get-tuple-element.27.own.refs_5_.refs_4_), channel_id=1, source_target_pairs={{2,6},{0,12},{3,7},{1,13},{6,10},{4,0},{7,11},{5,1},{10,14},{8,4},... | collective-permute-start | bytes 1277960 | tf_op jit(solution)/shard_map/ppermute | solution.py:422
  11.2 0.0 collective-permute-start.1
  11.2 6.5 %collective-permute-done.3.across.refs_2_.refs_4_ = bf16[2,416,256]{2,1,0:T(8,128)(2,1)S(1)} collective-permute-done((bf16[2,416,256]{2,1,0:T(8,128)(2,1)S(1)}, bf16[2,416,256]{2,1,0:T(8,128)(2,1)S(1)}, u32[]{:S(2)}, u32[]{:S(2)}) %collective-permute-start.3) | collective-permute-done | bytes 426016 | tf_op jit(solution)/shard_map/ppermute | solution.py:394
  17.7 3.7 %collective-permute-done.2.second = bf16[2,416,256]{2,1,0:T(8,128)(2,1)S(1)} collective-permute-done((bf16[2,416,256]{2,1,0:T(8,128)(2,1)S(1)}, bf16[2,416,256]{2,1,0:T(8,128)(2,1)S(1)}, u32[]{:S(2)}, u32[]{:S(2)}) %collective-permute-start.2) | collective-permute-done | bytes 426016 | tf_op jit(solution)/shard_map/ppermute | solution.py:422
  21.4 3.7 %shard_map.70 = (bf16[2,384,256]{2,1,0:T(8,128)(2,1)S(1)}, bf16[2,384,256]{2,1,0:T(8,128)(2,1)S(1)}, bf16[768,1152]{1,0:T(8,128)(2,1)S(1)}) custom-call(bf16[2,416,256]{2,1,0:T(8,128)(2,1)S(1)} %collective-permute-done.2.second, bf16[2,416,256]{2,1,0:T(8,128)(2,1)S(1)} %collective-permute-done.3.across.refs_2_.refs_4_, ...), custom_call_target="tpu_custom_call" | custom-call | flops 1024 | bytes 1024 | tf_op jit(solution)/shard_map/pallas_call | solution.py:465
  25.2 0.1 collective-permute-start.4
  25.3 0.7 %collective-permute-start.5 = (bf16[416,256]{1,0:T(8,128)(2,1)S(1)}, bf16[416,256]{1,0:T(8,128)(2,1)S(1)}, u32[]{:S(2)}, u32[]{:S(2)}) collective-permute-start(bf16[416,256]{1,0:T(8,128)(2,1)S(1)} %get-tuple-element.39), channel_id=1, source_target_pairs={{0,4},{2,14},{1,5},{3,15},{4,8},{6,2},{5,9},{7,3},{8,12},{10,6},{9... | collective-permute-start | bytes 638984 | tf_op jit(solution)/shard_map/ppermute | solution.py:424
  25.9 0.9 %shard_map.71 = (f32[384,256]{1,0:T(8,128)S(1)}, f32[384,256]{1,0:T(8,128)S(1)}, bf16[768,768]{1,0:T(8,128)(2,1)S(1)}) custom-call(bf16[2,416,256]{2,1,0:T(8,128)(2,1)S(1)} %get-tuple-element.27.own.refs_5_.refs_4_, bf16[2,384,256]{2,1,0:T(8,128)(2,1)S(1)} %get-tuple-element.29.u_in, bf16[768,1152]{1,0:T(8,128)(2,1)S(1)} %get-tuple-element.30.operator.operator_in), custom_call_target="tpu_custom_call" | custom-call | flops 1024 | bytes 1024 | tf_op jit(solution)/shard_map/pallas_call | solution.py:480
  26.9 0.1 collective-permute-done.4.refs_1_.refs_2_
  27.0 0.0 copy-done.3
  27.0 1.9 %shard_map.72.refs_6_ = f32[256,512]{1,0:T(8,128)S(1)} custom-call(s32[2]{0:T(128)S(1)} %copy-done.3, bf16[2,384,256]{2,1,0:T(8,128)(2,1)S(1)} %get-tuple-element.34.refs_0_, bf16[2,384,256]{2,1,0:T(8,128)(2,1)S(1)} %collective-permute-done.4.refs_1_.refs_2_, bf16[2,416,256]{2,1,0:T(8,128)(2,1)S(1)} %collective-permute-done.3.across.refs_2_.refs_4_), custom_call_target="tpu_custom_call" | custom-call | flops 1024 | bytes 1024 | tf_op jit(solution)/shard_map/pallas_call | solution.py:445
  28.9 2.0 %collective-permute-done.1.first.refs_5_ = bf16[2,416,256]{2,1,0:T(8,128)(2,1)S(1)} collective-permute-done((bf16[2,416,256]{2,1,0:T(8,128)(2,1)S(1)}, bf16[2,416,256]{2,1,0:T(8,128)(2,1)S(1)}, u32[]{:S(2)}, u32[]{:S(2)}) %collective-permute-start.1) | collective-permute-done | bytes 426016 | tf_op jit(solution)/shard_map/ppermute | solution.py:423
  30.9 2.6 %shard_map.73 = (bf16[2,384,256]{2,1,0:T(8,128)(2,1)S(1)}, f32[384,256]{1,0:T(8,128)S(1)}, f32[384,256]{1,0:T(8,128)S(1)}, bf16[768,384]{1,0:T(8,128)(2,1)S(1)}) custom-call(bf16[2,416,256]{2,1,0:T(8,128)(2,1)S(1)} %get-tuple-element.27.own.refs_5_.refs_4_, bf16[2,416,256]{2,1,0:T(8,128)(2,1)S(1)} %collective-permute-done.1.first.refs_5_, ...), custom_call_target="tpu_custom_call" | custom-call | flops 1024 | bytes 1024 | tf_op jit(solution)/shard_map/pallas_call | solution.py:491
  33.6 0.1 collective-permute-start.6
  33.6 1.8 %collective-permute-done.5.last = bf16[416,256]{1,0:T(8,128)(2,1)S(1)} collective-permute-done((bf16[416,256]{1,0:T(8,128)(2,1)S(1)}, bf16[416,256]{1,0:T(8,128)(2,1)S(1)}, u32[]{:S(2)}, u32[]{:S(2)}) %collective-permute-start.5) | collective-permute-done | bytes 213024 | tf_op jit(solution)/shard_map/ppermute | solution.py:424
  35.4 1.1 %shard_map.74.refs_1_ = bf16[1,384,256]{2,1,0:T(8,128)(2,1)S(1)} custom-call(bf16[2,416,256]{2,1,0:T(8,128)(2,1)S(1)} %collective-permute-done.1.first.refs_5_, bf16[416,256]{1,0:T(8,128)(2,1)S(1)} %collective-permute-done.5.last, f32[384,256]{1,0:T(8,128)S(1)} %get-tuple-element.40.first_short, f32[384,256]{1,0:T(8,128)S(1)} %get-tuple-element.41.second_short, ...), custom_call_target="tpu_custom_call" | custom-call | flops 1024 | bytes 1024 | tf_op jit(solution)/shard_map/pallas_call | solution.py:508
  36.5 0.1 collective-permute-start.7
  36.6 0.0 collective-permute-done.6.refs_3_.refs_2_
  36.6 2.3 %shard_map.75.refs_6_ = f32[256,512]{1,0:T(8,128)S(1)} custom-call(s32[2]{0:T(128)S(1)} %copy-done.3, bf16[2,384,256]{2,1,0:T(8,128)(2,1)S(1)} %get-tuple-element.34.refs_0_, bf16[2,384,256]{2,1,0:T(8,128)(2,1)S(1)} %get-tuple-element.38.refs_1_.refs_0_, bf16[2,384,256]{2,1,0:T(8,128)(2,1)S(1)} %collective-permute-done.4.refs_1_.refs_2_, ...), custom_call_target="tpu_custom_call" | custom-call | flops 1024 | bytes 1024 | tf_op jit(solution)/shard_map/pallas_call | solution.py:445
  38.9 0.0 copy-start
  38.9 0.0 copy-start.4
  38.9 0.0 collective-permute-done.7.refs_3_
  38.9 2.1 %shard_map.76 = (f32[256,256]{1,0:T(8,128)S(1)}, bf16[256,256]{1,0:T(8,128)(2,1)S(1)}) custom-call(s32[2]{0:T(128)S(1)} %copy-done.3, bf16[2,384,256]{2,1,0:T(8,128)(2,1)S(1)} %get-tuple-element.38.refs_1_.refs_0_, bf16[1,384,256]{2,1,0:T(8,128)(2,1)S(1)} %shard_map.74.refs_1_, bf16[2,384,256]{2,1,0:T(8,128)(2,1)S(1)} %collective-permute-done.6.refs_3_.refs_2_, ...), custom_call_target="tpu_custom_call" | custom-call | flops 1024 | bytes 1024 | tf_op jit(solution)/shard_map/pallas_call | solution.py:445
  41.0 3.0 %collective-permute-start.8 = (bf16[256,256]{1,0:T(8,128)(2,1)S(1)}, bf16[256,256]{1,0:T(8,128)(2,1)S(1)}, u32[]{:S(2)}, u32[]{:S(2)}) collective-permute-start(bf16[256,256]{1,0:T(8,128)(2,1)S(1)} %get-tuple-element.45), channel_id=1, source_target_pairs={{0,12},{1,13},{2,14},{3,15},{4,8},{5,9},{6,10},{7,11},{8,4},{9,5},... | collective-permute-start | bytes 393224 | tf_op jit(solution)/shard_map/ppermute | solution.py:394
  44.0 4.9 %collective-permute-done.8 = bf16[256,256]{1,0:T(8,128)(2,1)S(1)} collective-permute-done((bf16[256,256]{1,0:T(8,128)(2,1)S(1)}, bf16[256,256]{1,0:T(8,128)(2,1)S(1)}, u32[]{:S(2)}, u32[]{:S(2)}) %collective-permute-start.8) | collective-permute-done | bytes 131104 | tf_op jit(solution)/shard_map/ppermute | solution.py:394
  48.9 2.0 %collective-permute-start.9 = (bf16[256,256]{1,0:T(8,128)(2,1)S(1)}, bf16[256,256]{1,0:T(8,128)(2,1)S(1)}, u32[]{:S(2)}, u32[]{:S(2)}) collective-permute-start(bf16[256,256]{1,0:T(8,128)(2,1)S(1)} %fusion), channel_id=1, source_target_pairs={{0,4},{1,5},{2,6},{3,7},{4,0},{5,1},{6,2},{7,3},{8,12},{9,13},{10,... | collective-permute-start | bytes 393224 | tf_op jit(solution)/shard_map/ppermute | solution.py:394
  51.0 3.4 %collective-permute-done.9 = bf16[256,256]{1,0:T(8,128)(2,1)S(1)} collective-permute-done((bf16[256,256]{1,0:T(8,128)(2,1)S(1)}, bf16[256,256]{1,0:T(8,128)(2,1)S(1)}, u32[]{:S(2)}, u32[]{:S(2)}) %collective-permute-start.9) | collective-permute-done | bytes 131104 | tf_op jit(solution)/shard_map/ppermute | solution.py:394
  54.3 0.1 add_convert_fusion.s00
  54.4 0.1 collective-permute-start.10
  54.5 0.1 collective-permute-start.11
  54.5 4.9 %collective-permute-done.10.s10 = bf16[256,256]{1,0:T(8,128)(2,1)S(1)} collective-permute-done((bf16[256,256]{1,0:T(8,128)(2,1)S(1)}, bf16[256,256]{1,0:T(8,128)(2,1)S(1)}, u32[]{:S(2)}, u32[]{:S(2)}) %collective-permute-start.10) | collective-permute-done | bytes 131104 | tf_op jit(solution)/shard_map/ppermute | solution.py:394
  59.4 0.0 collective-permute-start.12
  59.4 0.0 collective-permute-done.11.s01
  59.4 1.3 %collective-permute-done.12.s11 = bf16[256,256]{1,0:T(8,128)(2,1)S(1)} collective-permute-done((bf16[256,256]{1,0:T(8,128)(2,1)S(1)}, bf16[256,256]{1,0:T(8,128)(2,1)S(1)}, u32[]{:S(2)}, u32[]{:S(2)}) %collective-permute-start.12) | collective-permute-done | bytes 131104 | tf_op jit(solution)/shard_map/ppermute | solution.py:394
  60.8 0.0 copy-done
  60.8 0.0 copy-done.4
  60.8 3.7 %shard_map.77 = (f32[2,2,2,16,256]{4,3,2,1,0:T(8,128)}, bf16[4,2,256,256]{3,2,1,0:T(8,128)(2,1)}) custom-call(s32[2,4]{1,0:T(2,128)S(1)} %bitcast.3, bf16[256,256]{1,0:T(8,128)(2,1)S(1)} %add_convert_fusion.s00, bf16[256,256]{1,0:T(8,128)(2,1)S(1)} %collective-permute-done.10.s10, bf16[256,256]{1,0:T(8,128)(2,1)S(1)} %collective-permute-done.11.s01, ...), custom_call_target="tpu_custom_call" | custom-call | tf_op jit(solution)/shard_map/pallas_call | solution.py:541
  (1 shorter events, 0.0 us)
Async XLA Ops:
  0.6 1.1 %copy-start.1 = (bf16[2,2,3,1,128,256]{5,4,3,2,1,0:T(8,128)(2,1)S(1)}, bf16[2,2,3,1,128,256]{5,4,3,2,1,0:T(8,128)(2,1)}, u32[]{:S(2)}) copy-start(bf16[2,2,3,1,128,256]{5,4,3,2,1,0:T(8,128)(2,1)} %vectors.1) | copy-start | bytes 2359300
  1.8 0.7 %copy-start.2 = (bf16[2,3,2,3,3,1,128]{6,2,5,4,3,1,0:T(2,128)(2,1)S(1)}, bf16[2,3,2,3,3,1,128]{6,2,5,4,3,1,0:T(2,128)(2,1)}, u32[]{:S(2)}) copy-start(bf16[2,3,2,3,3,1,128]{6,2,5,4,3,1,0:T(2,128)(2,1)} %param.6) | copy-start | bytes 82948
  2.6 1.9 %collective-permute-start = (bf16[2,416,256]{2,1,0:T(8,128)(2,1)S(1)}, bf16[2,416,256]{2,1,0:T(8,128)(2,1)S(1)}, u32[]{:S(2)}, u32[]{:S(2)}) collective-permute-start(bf16[2,416,256]{2,1,0:T(8,128)(2,1)S(1)} %get-tuple-element.24), channel_id=1, source_target_pairs={{0,1},{1,0},{2,3},{3,2},{4,5},{5,4},{6,7},{7,6},{8,9},{9,8},{10,11... | collective-permute-start | bytes 1277960 | tf_op jit(solution)/shard_map/ppermute | solution.py:394
  4.6 13.1 %collective-permute-start.3 = (bf16[2,416,256]{2,1,0:T(8,128)(2,1)S(1)}, bf16[2,416,256]{2,1,0:T(8,128)(2,1)S(1)}, u32[]{:S(2)}, u32[]{:S(2)}) collective-permute-start(bf16[2,416,256]{2,1,0:T(8,128)(2,1)S(1)} %get-tuple-element.28), channel_id=1, source_target_pairs={{0,2},{1,3},{2,0},{3,1},{4,6},{5,7},{6,4},{7,5},{8,10},{9,11},{10,... | collective-permute-start | bytes 1277960 | tf_op jit(solution)/shard_map/ppermute | solution.py:394
  7.6 19.4 %copy-start.3 = (s32[2]{0:T(128)S(1)}, s32[2]{0:T(128)}, u32[]{:S(2)}) copy-start(s32[2]{0:T(128)} %directions.5) | copy-start | bytes 28
  7.6 13.8 %collective-permute-start.2 = (bf16[2,416,256]{2,1,0:T(8,128)(2,1)S(1)}, bf16[2,416,256]{2,1,0:T(8,128)(2,1)S(1)}, u32[]{:S(2)}, u32[]{:S(2)}) collective-permute-start(bf16[2,416,256]{2,1,0:T(8,128)(2,1)S(1)} %get-tuple-element.27.own.refs_5_.refs_4_), channel_id=1, source_target_pairs={{2,6},{0,12},{3,7},{1,13},{6,10},{4,0},{7,11},{5,1},{10,14},{8,4},... | collective-permute-start | bytes 1277960 | tf_op jit(solution)/shard_map/ppermute | solution.py:422
  11.2 19.7 %collective-permute-start.1 = (bf16[2,416,256]{2,1,0:T(8,128)(2,1)S(1)}, bf16[2,416,256]{2,1,0:T(8,128)(2,1)S(1)}, u32[]{:S(2)}, u32[]{:S(2)}) collective-permute-start(bf16[2,416,256]{2,1,0:T(8,128)(2,1)S(1)} %get-tuple-element.28), channel_id=1, source_target_pairs={{2,4},{0,14},{3,5},{1,15},{6,8},{4,2},{7,9},{5,3},{10,12},{8,6},{1... | collective-permute-start | bytes 1277960 | tf_op jit(solution)/shard_map/ppermute | solution.py:423
  25.2 1.8 %collective-permute-start.4 = (bf16[2,384,256]{2,1,0:T(8,128)(2,1)S(1)}, bf16[2,384,256]{2,1,0:T(8,128)(2,1)S(1)}, u32[]{:S(2)}, u32[]{:S(2)}) collective-permute-start(bf16[2,384,256]{2,1,0:T(8,128)(2,1)S(1)} %get-tuple-element.34.refs_0_), channel_id=1, source_target_pairs={{0,1},{1,0},{2,3},{3,2},{4,5},{5,4},{6,7},{7,6},{8,9},{9,8},{10,11... | collective-permute-start | bytes 1179656 | tf_op jit(solution)/shard_map/ppermute | solution.py:394
  25.3 10.2 %collective-permute-start.5 = (bf16[416,256]{1,0:T(8,128)(2,1)S(1)}, bf16[416,256]{1,0:T(8,128)(2,1)S(1)}, u32[]{:S(2)}, u32[]{:S(2)}) collective-permute-start(bf16[416,256]{1,0:T(8,128)(2,1)S(1)} %get-tuple-element.39), channel_id=1, source_target_pairs={{0,4},{2,14},{1,5},{3,15},{4,8},{6,2},{5,9},{7,3},{8,12},{10,6},{9... | collective-permute-start | bytes 638984 | tf_op jit(solution)/shard_map/ppermute | solution.py:424
  33.6 3.0 %collective-permute-start.6 = (bf16[2,384,256]{2,1,0:T(8,128)(2,1)S(1)}, bf16[2,384,256]{2,1,0:T(8,128)(2,1)S(1)}, u32[]{:S(2)}, u32[]{:S(2)}) collective-permute-start(bf16[2,384,256]{2,1,0:T(8,128)(2,1)S(1)} %get-tuple-element.38.refs_1_.refs_0_), channel_id=1, source_target_pairs={{0,1},{1,0},{2,3},{3,2},{4,5},{5,4},{6,7},{7,6},{8,9},{9,8},{10,11... | collective-permute-start | bytes 1179656 | tf_op jit(solution)/shard_map/ppermute | solution.py:394
  36.5 2.4 %collective-permute-start.7 = (bf16[1,384,256]{2,1,0:T(8,128)(2,1)S(1)}, bf16[1,384,256]{2,1,0:T(8,128)(2,1)S(1)}, u32[]{:S(2)}, u32[]{:S(2)}) collective-permute-start(bf16[1,384,256]{2,1,0:T(8,128)(2,1)S(1)} %shard_map.74.refs_1_), channel_id=1, source_target_pairs={{0,1},{1,0},{2,3},{3,2},{4,5},{5,4},{6,7},{7,6},{8,9},{9,8},{10,11... | collective-permute-start | bytes 589832 | tf_op jit(solution)/shard_map/ppermute | solution.py:394
  38.9 21.9 %copy-start = (bf16[4,2,256,256]{3,2,1,0:T(8,128)(2,1)S(1)}, bf16[4,2,256,256]{3,2,1,0:T(8,128)(2,1)}, u32[]{:S(2)}) copy-start(bf16[4,2,256,256]{3,2,1,0:T(8,128)(2,1)} %perambulators.1) | copy-start | bytes 3145732
  38.9 21.9 %copy-start.4 = (s32[4,2]{0,1:T(2,128)S(1)}, s32[4,2]{0,1:T(2,128)}, u32[]{:S(2)}) copy-start(s32[4,2]{0,1:T(2,128)} %param.8) | copy-start | bytes 100
  41.0 7.9 %collective-permute-start.8 = (bf16[256,256]{1,0:T(8,128)(2,1)S(1)}, bf16[256,256]{1,0:T(8,128)(2,1)S(1)}, u32[]{:S(2)}, u32[]{:S(2)}) collective-permute-start(bf16[256,256]{1,0:T(8,128)(2,1)S(1)} %get-tuple-element.45), channel_id=1, source_target_pairs={{0,12},{1,13},{2,14},{3,15},{4,8},{5,9},{6,10},{7,11},{8,4},{9,5},... | collective-permute-start | bytes 393224 | tf_op jit(solution)/shard_map/ppermute | solution.py:394
  48.9 5.4 %collective-permute-start.9 = (bf16[256,256]{1,0:T(8,128)(2,1)S(1)}, bf16[256,256]{1,0:T(8,128)(2,1)S(1)}, u32[]{:S(2)}, u32[]{:S(2)}) collective-permute-start(bf16[256,256]{1,0:T(8,128)(2,1)S(1)} %fusion), channel_id=1, source_target_pairs={{0,4},{1,5},{2,6},{3,7},{4,0},{5,1},{6,2},{7,3},{8,12},{9,13},{10,... | collective-permute-start | bytes 393224 | tf_op jit(solution)/shard_map/ppermute | solution.py:394
  54.4 5.0 %collective-permute-start.10 = (bf16[256,256]{1,0:T(8,128)(2,1)S(1)}, bf16[256,256]{1,0:T(8,128)(2,1)S(1)}, u32[]{:S(2)}, u32[]{:S(2)}) collective-permute-start(bf16[256,256]{1,0:T(8,128)(2,1)S(1)} %add_convert_fusion.s00), channel_id=1, source_target_pairs={{0,2},{1,3},{2,0},{3,1},{4,6},{5,7},{6,4},{7,5},{8,10},{9,11},{10,... | collective-permute-start | bytes 393224 | tf_op jit(solution)/shard_map/ppermute | solution.py:394
  54.5 5.0 %collective-permute-start.11 = (bf16[256,256]{1,0:T(8,128)(2,1)S(1)}, bf16[256,256]{1,0:T(8,128)(2,1)S(1)}, u32[]{:S(2)}, u32[]{:S(2)}) collective-permute-start(bf16[256,256]{1,0:T(8,128)(2,1)S(1)} %add_convert_fusion.s00), channel_id=1, source_target_pairs={{0,1},{1,0},{2,3},{3,2},{4,5},{5,4},{6,7},{7,6},{8,9},{9,8},{10,11... | collective-permute-start | bytes 393224 | tf_op jit(solution)/shard_map/ppermute | solution.py:394
  59.4 1.3 %collective-permute-start.12 = (bf16[256,256]{1,0:T(8,128)(2,1)S(1)}, bf16[256,256]{1,0:T(8,128)(2,1)S(1)}, u32[]{:S(2)}, u32[]{:S(2)}) collective-permute-start(bf16[256,256]{1,0:T(8,128)(2,1)S(1)} %collective-permute-done.10.s10), channel_id=1, source_target_pairs={{0,1},{1,0},{2,3},{3,2},{4,5},{5,4},{6,7},{7,6},{8,9},{9,8},{10,11... | collective-permute-start | bytes 393224 | tf_op jit(solution)/shard_map/ppermute | solution.py:394
